TPU v7x, 128 devices: a whole 4x4x4 slice. The times are simulated.
128 devices in a mesh: gx: 8 (over x, core), gy: 16 (over z, y).
Axes of the slice: x: 4, y: 4, z: 4, core: 2. Of those that a mesh axis runs over, the one named last changes fastest.
Arguments:
- thermal_departure: float32 [40, 512, 4096], P(None, 'gx', 'gy'), may hold values from -6 to 6
- current_speeds: float32 [2, 40, 512, 4096], P(None, None, 'gx', 'gy'), may hold values from -3 to 3
- mixing_coefficient: float32 [40, 512, 4096], P(None, 'gx', 'gy'), may hold values from 0.1 to 10
- seawater_indicator: int32 [512, 4096], P('gx', 'gy'), may hold values 0 or 1
- submerged_layer_tally: int32 [512, 4096], P('gx', 'gy'), may hold values from 1 to 40
- rainfall_runoff_input: float32 [512, 4096], P('gx', 'gy'), may hold values from -6 to 6
Outputs:
- temperature_next: float32 [40, 512, 4096], P(None, 'gx', 'gy')
- velocity_next: float32 [2, 40, 512, 4096], P(None, None, 'gx', 'gy')
- surface_pressure: float32 [512, 4096], P('gx', 'gy')
All inputs are finite; a program needn't handle non-finite values. No bound on the sum of `seawater_indicator` on one device may be relied on, other than what follows from the above.
Results may differ from a plain program's by a relative error of at most 0.0003.
Values sent between devices are 32-bit elements; how exact they have to be, the bound alone decides.
No kernel may reach another device: no remote copies, remote signals or barrier semaphores. Data moves between devices by JAX's collectives and lax.ppermute only.
A program may use at most 128 MiB of HBM per device.

v0:
```python
import jax
import jax.numpy as jnp
from jax import lax
from jax.sharding import PartitionSpec as P

ITERS = 6


damping = 0.05
lower_bound = 0.02
upper_bound = 2.0
cheb_alpha = 2.0 / (upper_bound - lower_bound)
cheb_gamma = (upper_bound + lower_bound) / 2.0
advect_scale = 0.4
force_scale = 4.0
source_scale = 0.5
divergence_scale = 4.0


def padded_2(cells, sides, width):
    for axis, dim in sides:
        count = lax.axis_size(axis)
        head = lax.slice_in_dim(cells, 0, width, axis=dim)
        tail = lax.slice_in_dim(cells, cells.shape[dim] - width, cells.shape[dim], axis=dim)
        cells = jnp.concatenate(
            [
                lax.ppermute(tail, axis, [(i, (i + 1) % count) for i in range(count)]),
                cells,
                lax.ppermute(head, axis, [((i + 1) % count, i) for i in range(count)]),
            ],
            axis=dim,
        )
    return cells


def neighbor_total(padded):
    edges = (
        padded[..., 2:, 1:-1]
        + padded[..., :-2, 1:-1]
        + padded[..., 1:-1, 2:]
        + padded[..., 1:-1, :-2]
    )
    corners = (
        padded[..., 2:, 2:] + padded[..., 2:, :-2] + padded[..., :-2, 2:] + padded[..., :-2, :-2]
    )
    return edges + 0.5 * corners


def vertical_mix(source, coupling):
    count = source.shape[0]
    zeros = jnp.zeros_like(source[0])
    above = [zeros] + [coupling[level] for level in range(1, count)]
    below = above[1:] + [zeros]
    factors = []
    values = []
    for level in range(count):
        denominator = 1.0 + above[level] + below[level]
        numerator = source[level]
        if level > 0:
            denominator = denominator - above[level] * factors[-1]
            numerator = numerator + above[level] * values[-1]
        values.append(numerator / denominator)
        factors.append(below[level] / denominator)
    result = [values[-1]]
    for level in range(count - 2, -1, -1):
        result.append(values[level] + factors[level] * result[-1])
    return jnp.stack(result[::-1])


def tracer_update(extended):
    temp_ext = extended[0]
    east_vel = extended[1]
    north_vel = extended[2]
    wet_ext = (extended[3] > 0).astype(jnp.float32)
    east_open = wet_ext[:, :-1, 1:-1] * wet_ext[:, 1:, 1:-1] * east_vel[:, :-1, 1:-1]
    north_open = wet_ext[:, 1:-1, :-1] * wet_ext[:, 1:-1, 1:] * north_vel[:, 1:-1, :-1]
    flux_east = (
        jnp.maximum(east_open, 0.0) * temp_ext[:, :-1, 1:-1]
        + jnp.minimum(east_open, 0.0) * temp_ext[:, 1:, 1:-1]
    )
    flux_north = (
        jnp.maximum(north_open, 0.0) * temp_ext[:, 1:-1, :-1]
        + jnp.minimum(north_open, 0.0) * temp_ext[:, 1:-1, 1:]
    )
    convergence = (
        flux_east[:, 1:] - flux_east[:, :-1] + flux_north[:, :, 1:] - flux_north[:, :, :-1]
    )
    provisional = temp_ext[:, 1:-1, 1:-1] - advect_scale * wet_ext[:, 1:-1, 1:-1] * convergence
    temp_next = vertical_mix(provisional, extended[3][:, 1:-1, 1:-1])
    buoyancy = -temp_next
    pressure = (jnp.cumsum(buoyancy, axis=0) - 0.5 * buoyancy) / temp_next.shape[0]
    return (temp_next, pressure)


def momentum_update(extended, press_ext, ocean, rainfall_runoff_input):
    east_vel = extended[1]
    north_vel = extended[2]
    wet_ext = (extended[3] > 0).astype(jnp.float32)
    east_full = (
        wet_ext[:, :-1, 1:-1]
        * wet_ext[:, 1:, 1:-1]
        * (
            east_vel[:, :-1, 1:-1]
            + force_scale * (press_ext[:, :-1, 1:-1] - press_ext[:, 1:, 1:-1])
        )
    )
    north_full = (
        wet_ext[:, 1:-1, :-1]
        * wet_ext[:, 1:-1, 1:]
        * (
            north_vel[:, 1:-1, :-1]
            + force_scale * (press_ext[:, 1:-1, :-1] - press_ext[:, 1:-1, 1:])
        )
    )
    velocity_next = jnp.stack([east_full[:, 1:], north_full[:, :, 1:]])
    east_total = jnp.sum(east_full, axis=0) / east_full.shape[0]
    north_total = jnp.sum(north_full, axis=0) / north_full.shape[0]
    divergence = east_total[1:] - east_total[:-1] + north_total[:, 1:] - north_total[:, :-1]
    forcing = ocean * (source_scale * rainfall_runoff_input - divergence_scale * divergence)
    return (velocity_next, forcing)


def chebyshev(forcing, depth_root, total_fn):
    diag = damping + depth_root * total_fn(depth_root)
    inverse = 1.0 / diag
    update = inverse * forcing / cheb_gamma
    iterate = update
    omega = 2.0 / cheb_gamma
    for step in range(1, ITERS):
        residual = forcing - (diag * iterate - depth_root * total_fn(depth_root * iterate))
        omega = 1.0 / (cheb_gamma - omega / (4.0 * cheb_alpha * cheb_alpha))
        update = omega * inverse * residual + (cheb_gamma * omega - 1.0) * update
        iterate = iterate + update
    return iterate


def tile_total(field):
    return neighbor_total(padded_2(field, (("gx", 0), ("gy", 1)), 1))


def local(
    thermal_departure,
    current_speeds,
    mixing_coefficient,
    seawater_indicator,
    submerged_layer_tally,
    rainfall_runoff_input,
):
    layer_tally_grid, parallel_extent, meridian_extent = thermal_departure.shape
    total_y = meridian_extent * lax.axis_size("gy")
    latitude = lax.axis_index("gy") * meridian_extent + jnp.arange(meridian_extent)
    inner = (latitude > 0) & (latitude < total_y - 1)
    ocean_int = jnp.where(inner[None, :], seawater_indicator, 0)
    ocean = ocean_int.astype(jnp.float32)
    levels = jnp.arange(layer_tally_grid)[:, None, None]
    submerged_indicator = ((levels < submerged_layer_tally[None]) & (ocean_int[None] == 1)).astype(
        jnp.float32
    )
    joined_quantities = jnp.stack(
        [
            thermal_departure,
            current_speeds[0],
            current_speeds[1],
            mixing_coefficient * submerged_indicator,
        ]
    )
    extended = padded_2(joined_quantities, (("gx", 2), ("gy", 3)), 1)
    temp_next, pressure = tracer_update(extended)
    press_ext = padded_2(pressure, (("gx", 1), ("gy", 2)), 1)
    velocity_next, forcing = momentum_update(extended, press_ext, ocean, rainfall_runoff_input)
    depth_root = jnp.sqrt(
        (submerged_layer_tally * ocean_int).astype(jnp.float32) / layer_tally_grid
    )
    surface = chebyshev(forcing, depth_root, tile_total)
    return (temp_next, velocity_next, surface)


def solution(mesh):
    placed = (
        P(None, "gx", "gy"),
        P(None, None, "gx", "gy"),
        P(None, "gx", "gy"),
        P("gx", "gy"),
        P("gx", "gy"),
        P("gx", "gy"),
    )
    return jax.shard_map(
        local,
        mesh=mesh,
        in_specs=placed,
        out_specs=(P(None, "gx", "gy"), P(None, None, "gx", "gy"), P("gx", "gy")),
        check_vma=False,
    )
```

profile of v0, /device:TPU:0, one launch (start us, length us, event | category | flops | bytes accessed | tf_op | source)
XLA Modules:
  0.0 220.3 jit_solution(17108026548651424286)
XLA Ops:
  1.5 2.3 %select_bitcast_fusion = f32[1,40,64,256]{3,2,1,0:T(8,128)S(1)} fusion(f32[40,64,256]{2,1,0:T(8,128)} %param.8, s32[64,256]{1,0:T(8,128)} %param.10, pred[64,256]{1,0:T(8,128)(4,1)S(1)} %select_compare_fusion), kind=kLoop, calls=%fused_computation.40 | loop fusion | flops 1966080 | bytes 5324800 | tf_op jit(solution)/shard_map/stack | solution.py:159
  6.3 2.9 %collective-permute-start.1 = (f32[4,40,1,256]{3,2,1,0:T(1,128)S(1)}, f32[4,40,1,256]{3,2,1,0:T(1,128)S(1)}, u32[]{:S(2)}, u32[]{:S(2)}) collective-permute-start(f32[4,40,1,256]{3,2,1,0:T(1,128)S(1)} %get-tuple-element.121), channel_id=1, source_target_pairs={{16,0},{32,16},{48,32},{64,48},{80,64},{96,80},{112,96},{0,112},{1... | collective-permute-start | bytes 491528 | tf_op jit(solution)/shard_map/ppermute | solution.py:29
  9.8 2.3 %collective-permute-done.8 = f32[1,256]{1,0:T(1,128)S(1)} collective-permute-done((f32[1,256]{1,0:T(1,128)S(1)}, f32[1,256]{1,0:T(1,128)S(1)}, u32[]{:S(2)}, u32[]{:S(2)}) %collective-permute-start.8) | collective-permute-done | bytes 1056 | tf_op jit(solution)/shard_map/ppermute | solution.py:29
  14.1 5.6 %pad_maximum_fusion.1 = f32[4,40,66,256]{3,2,1,0:T(8,128)} fusion(f32[4,40,1,256]{3,2,1,0:T(1,128)S(1)} %collective-permute-done.1, f32[1,40,64,256]{3,2,1,0:T(8,128)S(1)} %select_bitcast_fusion, f32[2,40,64,256]{3,2,1,0:T(8,128)S(1)} %copy-done.1, f32[1,40,64,256]{3,2,1,0:T(8,128)S(1)} %bitcast.19, f32[4,40,1,256]{3,2,1,0:T(1,128)S(1)} %collective-permute-done), kind=kLoop, calls=%fused_computation.1 | loop fusion | flops 10813440 | bytes 21626880 | tf_op jit(solution)/shard_map/concatenate | solution.py:25
  19.7 10.2 %fusion.156 = (f32[4,40,66,1]{3,2,1,0:T(8,128)}, f32[4,40,66,1]{3,2,1,0:T(8,128)}) fusion(f32[4,40,66,256]{3,2,1,0:T(8,128)} %pad_maximum_fusion.1), kind=kLoop, calls=%fused_computation.410 | loop fusion | bytes 168960 | tf_op jit(solution)/shard_map/slice | solution.py:24
  30.0 3.8 %copy.9 = f32[4,40,66,1]{2,1,3,0:T(8,128)S(1)} copy(f32[4,40,66,1]{3,2,1,0:T(8,128)} %get-tuple-element.118) | data formatting | bytes 84480 | tf_op jit(solution)/shard_map/slice | solution.py:24
  33.7 1.7 collective-permute-start.2
  35.5 3.8 %copy.10 = f32[4,40,66,1]{2,1,3,0:T(8,128)S(1)} copy(f32[4,40,66,1]{3,2,1,0:T(8,128)} %get-tuple-element.119) | data formatting | bytes 84480 | tf_op jit(solution)/shard_map/slice | solution.py:23
  39.3 5.0 %collective-permute-start.3 = (f32[4,40,66,1]{2,1,3,0:T(8,128)S(1)}, f32[4,40,66,1]{2,1,3,0:T(8,128)S(1)}, u32[]{:S(2)}, u32[]{:S(2)}) collective-permute-start(f32[4,40,66,1]{2,1,3,0:T(8,128)S(1)} %copy.10), channel_id=1, source_target_pairs={{1,0},{2,1},{3,2},{4,3},{5,4},{6,5},{7,6},{8,7},{9,8},{10,9},{11,1... | collective-permute-start | bytes 126728 | tf_op jit(solution)/shard_map/ppermute | solution.py:29
  44.9 2.0 collective-permute-start.10
  46.9 3.7 %copy.11 = f32[4,40,66,1]{3,2,1,0:T(8,128)} copy(f32[4,40,66,1]{2,1,3,0:T(8,128)S(1)} %collective-permute-done.2) | data formatting | bytes 84480 | tf_op jit(solution)/shard_map/ppermute | solution.py:27
  50.7 3.6 %copy.12 = f32[4,40,66,1]{3,2,1,0:T(8,128)} copy(f32[4,40,66,1]{2,1,3,0:T(8,128)S(1)} %collective-permute-done.3) | data formatting | bytes 84480 | tf_op jit(solution)/shard_map/ppermute | solution.py:29
  54.3 18.7 %pad_maximum_fusion = f32[4,40,66,258]{3,2,1,0:T(8,128)} fusion(f32[4,40,66,1]{3,2,1,0:T(8,128)} %copy.12, f32[4,40,1,256]{3,2,1,0:T(1,128)S(1)} %collective-permute-done.1, f32[1,40,64,256]{3,2,1,0:T(8,128)S(1)} %select_bitcast_fusion, f32[2,40,64,256]{3,2,1,0:T(8,128)} %param.7, f32[1,40,64,256]{3,2,1,0:T(8,128)} %bitcast.18, ...), kind=kLoop, calls=%fused_computation | loop fusion | flops 16346880 | bytes 21795840 | tf_op jit(solution)/shard_map/concatenate | solution.py:25
  73.0 8.8 %slice_bitcast_fusion.1 = (f32[40,66,258]{2,1,0:T(8,128)S(1)}, f32[40,66,258]{2,1,0:T(8,128)S(1)}, f32[40,66,258]{2,1,0:T(8,128)}, f32[40,66,258]{2,1,0:T(8,128)S(1)}) fusion(f32[4,40,66,258]{3,2,1,0:T(8,128)} %pad_maximum_fusion), kind=kLoop, calls=%fused_computation.4 | loop fusion | bytes 21795840 | tf_op jit(solution)/shard_map/squeeze | solution.py:72
  81.9 5.7 %compare_convert_fusion = f32[40,66,258]{2,1,0:T(8,128)S(1)} fusion(f32[4,40,66,258]{3,2,1,0:T(8,128)} %pad_maximum_fusion), kind=kLoop, calls=%fused_computation.7 | loop fusion | flops 1362240 | bytes 5448960 | tf_op jit(solution)/shard_map/convert_element_type | solution.py:74
  87.6 5.5 %fusion.5 = f32[40,65,256]{2,1,0:T(8,128)} fusion(f32[40,66,258]{2,1,0:T(8,128)S(1)} %get-tuple-element.117, f32[40,66,258]{2,1,0:T(8,128)S(1)} %get-tuple-element.114, f32[40,66,258]{2,1,0:T(8,128)S(1)} %compare_convert_fusion), kind=kLoop, calls=%fused_computation.23 | loop fusion | flops 4659200 | bytes 15974400 | tf_op jit(solution)/shard_map/add | solution.py:78
  93.1 5.1 %fusion.4 = f32[40,64,257]{2,1,0:T(8,128)} fusion(f32[40,66,258]{2,1,0:T(8,128)S(1)} %get-tuple-element.117, f32[40,66,258]{2,1,0:T(8,128)S(1)} %get-tuple-element.115, f32[40,66,258]{2,1,0:T(8,128)S(1)} %compare_convert_fusion), kind=kLoop, calls=%fused_computation.19 | loop fusion | flops 4605440 | bytes 15790080 | tf_op jit(solution)/shard_map/add | solution.py:82
  98.2 8.7 %fusion.10 = f32[40,64,256]{2,1,0:T(8,128)} fusion(f32[40,64,257]{2,1,0:T(8,128)} %fusion.4, f32[40,65,256]{2,1,0:T(8,128)} %fusion.5, f32[40,66,258]{2,1,0:T(8,128)S(1)} %compare_convert_fusion, f32[40,66,258]{2,1,0:T(8,128)S(1)} %get-tuple-element.117), kind=kLoop, calls=%fused_computation.35 | loop fusion | flops 3932160 | bytes 18350080 | tf_op jit(solution)/shard_map/sub | solution.py:88
  106.9 4.2 %fusion.68 = (f32[1,64,256]{2,1,0:T(8,128)S(1)}, f32[1,64,256]{2,1,0:T(8,128)S(1)}, f32[1,64,256]{2,1,0:T(8,128)S(1)}, f32[1,64,256]{2,1,0:T(8,128)S(1)}, f32[1,...) fusion(f32[40,64,256]{2,1,0:T(8,128)} %fusion.10, ...), kind=kLoop, calls=%fused_computation.209 | loop fusion | flops 4866048 | bytes 9699328 | tf_op jit(solution)/shard_map/div | solution.py:62
  111.2 2.6 %constant_dynamic-update-slice_fusion.39 = (f32[40,64,256]{2,1,0:T(8,128)S(1)}, f32[1,64,256]{2,1,0:T(8,128)S(1)}, f32[1,64,256]{2,1,0:T(8,128)S(1)}, f32[1,64,2...) fusion(f32[40,66,258]{2,1,0:T(8,128)} %get-tuple-element.116, ...), kind=kLoop, calls=%fused_computation.102 | loop fusion | flops 1966079 | bytes 7798784
  118.1 2.9 %collective-permute-start.5 = (f32[40,1,256]{2,1,0:T(1,128)S(1)}, f32[40,1,256]{2,1,0:T(1,128)S(1)}, u32[]{:S(2)}, u32[]{:S(2)}) collective-permute-start(f32[40,1,256]{2,1,0:T(1,128)S(1)} %get-tuple-element.125), channel_id=1, source_target_pairs={{16,0},{32,16},{48,32},{64,48},{80,64},{96,80},{112,96},{0,112},{1... | collective-permute-start | bytes 122888 | tf_op jit(solution)/shard_map/ppermute | solution.py:29
  123.1 2.1 fusion.157
  125.1 1.9 copy.13
  127.1 1.9 copy.15
  129.0 5.4 %collective-permute-start.7 = (f32[40,66,1]{1,0,2:T(8,128)S(1)}, f32[40,66,1]{1,0,2:T(8,128)S(1)}, u32[]{:S(2)}, u32[]{:S(2)}) collective-permute-start(f32[40,66,1]{1,0,2:T(8,128)S(1)} %copy.15), channel_id=1, source_target_pairs={{1,0},{2,1},{3,2},{4,3},{5,4},{6,5},{7,6},{8,7},{9,8},{10,9},{11,1... | collective-permute-start | bytes 31688 | tf_op jit(solution)/shard_map/ppermute | solution.py:29
  134.4 8.5 %fusion.117 = (f32[65,256]{1,0:T(8,128)S(1)}, f32[40,65,256]{2,1,0:T(8,128)}) fusion(f32[40,1,256]{2,1,0:T(1,128)S(1)} %collective-permute-done.5, f32[40,64,256]{2,1,0:T(8,128)S(1)} %subtract_multiply_fusion, f32[40,1,256]{2,1,0:T(1,128)S(1)} %collective-permute-done.4, f32[40,66,258]{2,1,0:T(8,128)} %copy-done.3, f32[40,66,258]{2,1,0:T(8,128)} %copy-done), kind=kLoop, calls=%fused_computation.408 | loop fusion | flops 5308160 | bytes 13419520 | tf_op jit(solution)/shard_map/reduce_sum | solution.py:116
  146.3 9.0 %fusion.119 = (f32[64,257]{1,0:T(8,128)S(1)}, f32[40,64,257]{2,1,0:T(8,128)S(1)}) fusion(f32[40,66,1]{2,1,0:T(8,128)} %copy.16, f32[40,1,256]{2,1,0:T(1,128)S(1)} %collective-permute-done.5, f32[40,64,256]{2,1,0:T(8,128)S(1)} %subtract_multiply_fusion, f32[40,1,256]{2,1,0:T(1,128)S(1)} %collective-permute-done.4, f32[40,66,1]{2,1,0:T(8,128)} %copy.14, ...), kind=kLoop, calls=%fused_computation.409 | loop fusion | flops 7878592 | bytes 13316992 | tf_op jit(solution)/shard_map/reduce_sum | solution.py:117
  155.6 2.7 %collective-permute-start.12 = (f32[1,256]{1,0:T(1,128)S(1)}, f32[1,256]{1,0:T(1,128)S(1)}, u32[]{:S(2)}, u32[]{:S(2)}) collective-permute-start(f32[1,256]{1,0:T(1,128)S(1)} %get-tuple-element.159), channel_id=1, source_target_pairs={{16,0},{32,16},{48,32},{64,48},{80,64},{96,80},{112,96},{0,112},{1... | collective-permute-start | bytes 3080 | tf_op jit(solution)/shard_map/ppermute | solution.py:29
  159.5 2.9 %collective-permute-done.13 = f32[1,256]{1,0:T(1,128)S(1)} collective-permute-done((f32[1,256]{1,0:T(1,128)S(1)}, f32[1,256]{1,0:T(1,128)S(1)}, u32[]{:S(2)}, u32[]{:S(2)}) %collective-permute-start.13) | collective-permute-done | bytes 1056 | tf_op jit(solution)/shard_map/ppermute | solution.py:27
  162.5 1.7 collective-permute-start.14
  164.6 1.9 collective-permute-done.14
  166.5 5.1 %collective-permute-done.15 = f32[66,1]{1,0:T(8,128)S(1)} collective-permute-done((f32[66,1]{1,0:T(8,128)S(1)}, f32[66,1]{1,0:T(8,128)S(1)}, u32[]{:S(2)}, u32[]{:S(2)}) %collective-permute-start.15) | collective-permute-done | bytes 296 | tf_op jit(solution)/shard_map/ppermute | solution.py:27
  173.2 2.9 %collective-permute-done.17 = f32[1,256]{1,0:T(1,128)S(1)} collective-permute-done((f32[1,256]{1,0:T(1,128)S(1)}, f32[1,256]{1,0:T(1,128)S(1)}, u32[]{:S(2)}, u32[]{:S(2)}) %collective-permute-start.17) | collective-permute-done | bytes 1056 | tf_op jit(solution)/shard_map/ppermute | solution.py:27
  176.2 2.0 collective-permute-start.19
  178.2 1.9 collective-permute-done.18
  180.1 3.4 %collective-permute-done.19 = f32[66,1]{1,0:T(8,128)S(1)} collective-permute-done((f32[66,1]{1,0:T(8,128)S(1)}, f32[66,1]{1,0:T(8,128)S(1)}, u32[]{:S(2)}, u32[]{:S(2)}) %collective-permute-start.19) | collective-permute-done | bytes 296 | tf_op jit(solution)/shard_map/ppermute | solution.py:27
  185.1 2.9 %collective-permute-done.21 = f32[1,256]{1,0:T(1,128)S(1)} collective-permute-done((f32[1,256]{1,0:T(1,128)S(1)}, f32[1,256]{1,0:T(1,128)S(1)}, u32[]{:S(2)}, u32[]{:S(2)}) %collective-permute-start.21) | collective-permute-done | bytes 1056 | tf_op jit(solution)/shard_map/ppermute | solution.py:27
  188.2 2.0 collective-permute-start.23
  190.2 1.9 collective-permute-done.22
  192.1 3.4 %collective-permute-done.23 = f32[66,1]{1,0:T(8,128)S(1)} collective-permute-done((f32[66,1]{1,0:T(8,128)S(1)}, f32[66,1]{1,0:T(8,128)S(1)}, u32[]{:S(2)}, u32[]{:S(2)}) %collective-permute-start.23) | collective-permute-done | bytes 296 | tf_op jit(solution)/shard_map/ppermute | solution.py:27
  197.1 2.9 %collective-permute-done.25 = f32[1,256]{1,0:T(1,128)S(1)} collective-permute-done((f32[1,256]{1,0:T(1,128)S(1)}, f32[1,256]{1,0:T(1,128)S(1)}, u32[]{:S(2)}, u32[]{:S(2)}) %collective-permute-start.25) | collective-permute-done | bytes 1056 | tf_op jit(solution)/shard_map/ppermute | solution.py:27
  200.1 2.0 collective-permute-start.27
  202.1 1.9 collective-permute-done.26
  204.1 3.4 %collective-permute-done.27 = f32[66,1]{1,0:T(8,128)S(1)} collective-permute-done((f32[66,1]{1,0:T(8,128)S(1)}, f32[66,1]{1,0:T(8,128)S(1)}, u32[]{:S(2)}, u32[]{:S(2)}) %collective-permute-start.27) | collective-permute-done | bytes 296 | tf_op jit(solution)/shard_map/ppermute | solution.py:27
  209.3 2.7 %collective-permute-done.29 = f32[1,256]{1,0:T(1,128)S(1)} collective-permute-done((f32[1,256]{1,0:T(1,128)S(1)}, f32[1,256]{1,0:T(1,128)S(1)}, u32[]{:S(2)}, u32[]{:S(2)}) %collective-permute-start.29) | collective-permute-done | bytes 1056 | tf_op jit(solution)/shard_map/ppermute | solution.py:27
  212.1 2.0 collective-permute-start.31
  214.1 2.7 %pad_maximum_fusion.2 = f32[2,40,64,256]{3,2,1,0:T(8,128)} fusion(f32[1,40,64,256]{3,2,1,0:T(8,128)S(1)} %get-tuple-element.163, f32[1,40,64,256]{3,2,1,0:T(8,128)S(1)} %get-tuple-element.164), kind=kLoop, calls=%fused_computation.2 | loop fusion | flops 1310720 | bytes 10485760 | tf_op jit(solution)/shard_map/stack | solution.py:115
  216.8 2.6 %collective-permute-done.31 = f32[66,1]{1,0:T(8,128)S(1)} collective-permute-done((f32[66,1]{1,0:T(8,128)S(1)}, f32[66,1]{1,0:T(8,128)S(1)}, u32[]{:S(2)}, u32[]{:S(2)}) %collective-permute-start.31) | collective-permute-done | bytes 296 | tf_op jit(solution)/shard_map/ppermute | solution.py:27
  (150 shorter events, 25.6 us)
Async XLA Ops:
  0.6 8.6 %copy-start.14 = (pred[256]{0:T(512)(128)(4,1)}, pred[256]{0:T(512)(128)(4,1)S(1)}, u32[]{:S(2)}) copy-start(pred[256]{0:T(512)(128)(4,1)S(1)} %compare_and_fusion) | copy-start | bytes 772
  1.5 3.3 %copy-start.1 = (f32[2,40,64,256]{3,2,1,0:T(8,128)S(1)}, f32[2,40,64,256]{3,2,1,0:T(8,128)}, u32[]{:S(2)}) copy-start(f32[2,40,64,256]{3,2,1,0:T(8,128)} %param.7) | copy-start | bytes 15728644
  4.8 4.4 %copy-start.7 = (s32[64,256]{1,0:T(8,128)S(1)}, s32[64,256]{1,0:T(8,128)}, u32[]{:S(2)}) copy-start(s32[64,256]{1,0:T(8,128)} %param.9) | copy-start | bytes 196612
  4.8 4.4 %copy-start.8 = (s32[64,256]{1,0:T(8,128)S(1)}, s32[64,256]{1,0:T(8,128)}, u32[]{:S(2)}) copy-start(s32[64,256]{1,0:T(8,128)} %param.10) | copy-start | bytes 196612
  4.8 9.3 %copy-start.4 = (f32[40,64,256]{2,1,0:T(8,128)S(1)}, f32[40,64,256]{2,1,0:T(8,128)}, u32[]{:S(2)}) copy-start(f32[40,64,256]{2,1,0:T(8,128)} %param.6) | copy-start | bytes 7864324
  6.3 7.3 %collective-permute-start = (f32[4,40,1,256]{3,2,1,0:T(1,128)S(1)}, f32[4,40,1,256]{3,2,1,0:T(1,128)S(1)}, u32[]{:S(2)}, u32[]{:S(2)}) collective-permute-start(f32[4,40,1,256]{3,2,1,0:T(1,128)S(1)} %get-tuple-element.120), channel_id=1, source_target_pairs={{0,16},{16,32},{32,48},{48,64},{64,80},{80,96},{96,112},{112,0},{1... | collective-permute-start | bytes 491528 | tf_op jit(solution)/shard_map/ppermute | solution.py:27
  6.3 7.8 %collective-permute-start.1 = (f32[4,40,1,256]{3,2,1,0:T(1,128)S(1)}, f32[4,40,1,256]{3,2,1,0:T(1,128)S(1)}, u32[]{:S(2)}, u32[]{:S(2)}) collective-permute-start(f32[4,40,1,256]{3,2,1,0:T(1,128)S(1)} %get-tuple-element.121), channel_id=1, source_target_pairs={{16,0},{32,16},{48,32},{64,48},{80,64},{96,80},{112,96},{0,112},{1... | collective-permute-start | bytes 491528 | tf_op jit(solution)/shard_map/ppermute | solution.py:29
  9.3 2.8 %collective-permute-start.8 = (f32[1,256]{1,0:T(1,128)S(1)}, f32[1,256]{1,0:T(1,128)S(1)}, u32[]{:S(2)}, u32[]{:S(2)}) collective-permute-start(f32[1,256]{1,0:T(1,128)S(1)} %get-tuple-element.161), channel_id=1, source_target_pairs={{16,0},{32,16},{48,32},{64,48},{80,64},{96,80},{112,96},{0,112},{1... | collective-permute-start | bytes 3080 | tf_op jit(solution)/shard_map/ppermute | solution.py:29
  9.3 4.2 %collective-permute-start.9 = (f32[1,256]{1,0:T(1,128)S(1)}, f32[1,256]{1,0:T(1,128)S(1)}, u32[]{:S(2)}, u32[]{:S(2)}) collective-permute-start(f32[1,256]{1,0:T(1,128)S(1)} %get-tuple-element.160), channel_id=1, source_target_pairs={{0,16},{16,32},{32,48},{48,64},{64,80},{80,96},{96,112},{112,0},{1... | collective-permute-start | bytes 3080 | tf_op jit(solution)/shard_map/ppermute | solution.py:27
  12.1 1.5 copy-start.10
  13.5 0.6 copy-start.12
  33.7 13.2 %collective-permute-start.2 = (f32[4,40,66,1]{2,1,3,0:T(8,128)S(1)}, f32[4,40,66,1]{2,1,3,0:T(8,128)S(1)}, u32[]{:S(2)}, u32[]{:S(2)}) collective-permute-start(f32[4,40,66,1]{2,1,3,0:T(8,128)S(1)} %copy.9), channel_id=1, source_target_pairs={{0,1},{1,2},{2,3},{3,4},{4,5},{5,6},{6,7},{7,8},{8,9},{9,10},{10,1... | collective-permute-start | bytes 126728 | tf_op jit(solution)/shard_map/ppermute | solution.py:27
  39.3 11.4 %collective-permute-start.3 = (f32[4,40,66,1]{2,1,3,0:T(8,128)S(1)}, f32[4,40,66,1]{2,1,3,0:T(8,128)S(1)}, u32[]{:S(2)}, u32[]{:S(2)}) collective-permute-start(f32[4,40,66,1]{2,1,3,0:T(8,128)S(1)} %copy.10), channel_id=1, source_target_pairs={{1,0},{2,1},{3,2},{4,3},{5,4},{6,5},{7,6},{8,7},{9,8},{10,9},{11,1... | collective-permute-start | bytes 126728 | tf_op jit(solution)/shard_map/ppermute | solution.py:29
  44.9 76.1 %collective-permute-start.10 = (f32[66,1]{1,0:T(8,128)}, f32[66,1]{1,0:T(8,128)S(1)}, u32[]{:S(2)}, u32[]{:S(2)}) collective-permute-start(f32[66,1]{1,0:T(8,128)} %get-tuple-element.136), channel_id=1, source_target_pairs={{1,0},{2,1},{3,2},{4,3},{5,4},{6,5},{7,6},{8,7},{9,8},{10,9},{11,1... | collective-permute-start | bytes 800 | tf_op jit(solution)/shard_map/ppermute | solution.py:29
  46.9 74.1 %collective-permute-start.11 = (f32[66,1]{1,0:T(8,128)S(1)}, f32[66,1]{1,0:T(8,128)}, u32[]{:S(2)}, u32[]{:S(2)}) collective-permute-start(f32[66,1]{1,0:T(8,128)S(1)} %get-tuple-element.137), channel_id=1, source_target_pairs={{0,1},{1,2},{2,3},{3,4},{4,5},{5,6},{6,7},{7,8},{8,9},{9,10},{10,1... | collective-permute-start | bytes 800 | tf_op jit(solution)/shard_map/ppermute | solution.py:27
  81.9 5.7 %copy-start.3 = (f32[40,66,258]{2,1,0:T(8,128)}, f32[40,66,258]{2,1,0:T(8,128)S(1)}, u32[]{:S(2)}) copy-start(f32[40,66,258]{2,1,0:T(8,128)S(1)} %get-tuple-element.114) | copy-start | bytes 8173444
  81.9 11.2 %copy-start.2 = (f32[40,66,258]{2,1,0:T(8,128)}, f32[40,66,258]{2,1,0:T(8,128)S(1)}, u32[]{:S(2)}) copy-start(f32[40,66,258]{2,1,0:T(8,128)S(1)} %get-tuple-element.115) | copy-start | bytes 8173444
  87.6 10.7 %copy-start = (f32[40,66,258]{2,1,0:T(8,128)}, f32[40,66,258]{2,1,0:T(8,128)S(1)}, u32[]{:S(2)}) copy-start(f32[40,66,258]{2,1,0:T(8,128)S(1)} %compare_convert_fusion) | copy-start | bytes 8173444
  116.5 1.5 copy-start.5
  116.5 4.5 %copy-start.11 = (f32[1,256]{1,0:T(1,128)S(1)}, f32[1,256]{1,0:T(1,128)}, u32[]{:S(2)}) copy-start(f32[1,256]{1,0:T(1,128)} %copy-done.10) | copy-start | bytes 3076
  116.5 4.5 %copy-start.13 = (f32[1,256]{1,0:T(1,128)S(1)}, f32[1,256]{1,0:T(1,128)}, u32[]{:S(2)}) copy-start(f32[1,256]{1,0:T(1,128)} %copy-done.12) | copy-start | bytes 3076
  118.0 4.6 %collective-permute-start.4 = (f32[40,1,256]{2,1,0:T(1,128)S(1)}, f32[40,1,256]{2,1,0:T(1,128)S(1)}, u32[]{:S(2)}, u32[]{:S(2)}) collective-permute-start(f32[40,1,256]{2,1,0:T(1,128)S(1)} %get-tuple-element.124), channel_id=1, source_target_pairs={{0,16},{16,32},{32,48},{48,64},{64,80},{80,96},{96,112},{112,0},{1... | collective-permute-start | bytes 122888 | tf_op jit(solution)/shard_map/ppermute | solution.py:27
  118.1 4.6 %collective-permute-start.5 = (f32[40,1,256]{2,1,0:T(1,128)S(1)}, f32[40,1,256]{2,1,0:T(1,128)S(1)}, u32[]{:S(2)}, u32[]{:S(2)}) collective-permute-start(f32[40,1,256]{2,1,0:T(1,128)S(1)} %get-tuple-element.125), channel_id=1, source_target_pairs={{16,0},{32,16},{48,32},{64,48},{80,64},{96,80},{112,96},{0,112},{1... | collective-permute-start | bytes 122888 | tf_op jit(solution)/shard_map/ppermute | solution.py:29
  127.0 15.9 %collective-permute-start.6 = (f32[40,66,1]{1,0,2:T(8,128)S(1)}, f32[40,66,1]{1,0,2:T(8,128)S(1)}, u32[]{:S(2)}, u32[]{:S(2)}) collective-permute-start(f32[40,66,1]{1,0,2:T(8,128)S(1)} %copy.13), channel_id=1, source_target_pairs={{0,1},{1,2},{2,3},{3,4},{4,5},{5,6},{6,7},{7,8},{8,9},{9,10},{10,1... | collective-permute-start | bytes 31688 | tf_op jit(solution)/shard_map/ppermute | solution.py:27
  129.0 15.7 %collective-permute-start.7 = (f32[40,66,1]{1,0,2:T(8,128)S(1)}, f32[40,66,1]{1,0,2:T(8,128)S(1)}, u32[]{:S(2)}, u32[]{:S(2)}) collective-permute-start(f32[40,66,1]{1,0,2:T(8,128)S(1)} %copy.15), channel_id=1, source_target_pairs={{1,0},{2,1},{3,2},{4,3},{5,4},{6,5},{7,6},{8,7},{9,8},{10,9},{11,1... | collective-permute-start | bytes 31688 | tf_op jit(solution)/shard_map/ppermute | solution.py:29
  146.3 9.0 %copy-start.9 = (f32[64,256]{1,0:T(8,128)S(1)}, f32[64,256]{1,0:T(8,128)}, u32[]{:S(2)}) copy-start(f32[64,256]{1,0:T(8,128)} %param.11) | copy-start | bytes 196612
  146.3 9.1 %copy-start.15 = (pred[256]{0:T(512)(128)(4,1)S(1)}, pred[256]{0:T(512)(128)(4,1)}, u32[]{:S(2)}) copy-start(pred[256]{0:T(512)(128)(4,1)} %copy-done.14) | copy-start | bytes 772
  155.6 4.0 %collective-permute-start.12 = (f32[1,256]{1,0:T(1,128)S(1)}, f32[1,256]{1,0:T(1,128)S(1)}, u32[]{:S(2)}, u32[]{:S(2)}) collective-permute-start(f32[1,256]{1,0:T(1,128)S(1)} %get-tuple-element.159), channel_id=1, source_target_pairs={{16,0},{32,16},{48,32},{64,48},{80,64},{96,80},{112,96},{0,112},{1... | collective-permute-start | bytes 3080 | tf_op jit(solution)/shard_map/ppermute | solution.py:29
  158.2 4.2 %collective-permute-start.13 = (f32[1,256]{1,0:T(1,128)S(1)}, f32[1,256]{1,0:T(1,128)S(1)}, u32[]{:S(2)}, u32[]{:S(2)}) collective-permute-start(f32[1,256]{1,0:T(1,128)S(1)} %get-tuple-element.158), channel_id=1, source_target_pairs={{0,16},{16,32},{32,48},{48,64},{64,80},{80,96},{96,112},{112,0},{1... | collective-permute-start | bytes 3080 | tf_op jit(solution)/shard_map/ppermute | solution.py:27
  162.5 4.0 %collective-permute-start.14 = (f32[66,1]{1,0:T(8,128)S(1)}, f32[66,1]{1,0:T(8,128)S(1)}, u32[]{:S(2)}, u32[]{:S(2)}) collective-permute-start(f32[66,1]{1,0:T(8,128)S(1)} %get-tuple-element.134), channel_id=1, source_target_pairs={{1,0},{2,1},{3,2},{4,3},{5,4},{6,5},{7,6},{8,7},{9,8},{10,9},{11,1... | collective-permute-start | bytes 800 | tf_op jit(solution)/shard_map/ppermute | solution.py:29
  164.3 7.3 %collective-permute-start.15 = (f32[66,1]{1,0:T(8,128)S(1)}, f32[66,1]{1,0:T(8,128)S(1)}, u32[]{:S(2)}, u32[]{:S(2)}) collective-permute-start(f32[66,1]{1,0:T(8,128)S(1)} %get-tuple-element.135), channel_id=1, source_target_pairs={{0,1},{1,2},{2,3},{3,4},{4,5},{5,6},{6,7},{7,8},{8,9},{9,10},{10,1... | collective-permute-start | bytes 800 | tf_op jit(solution)/shard_map/ppermute | solution.py:27
  171.8 36.5 %copy-start.6 = (f32[40,65,256]{2,1,0:T(8,128)S(1)}, f32[40,65,256]{2,1,0:T(8,128)}, u32[]{:S(2)}) copy-start(f32[40,65,256]{2,1,0:T(8,128)} %get-tuple-element.18) | copy-start | bytes 7987204
  171.8 1.3 collective-permute-start.16
  171.9 4.2 %collective-permute-start.17 = (f32[1,256]{1,0:T(1,128)S(1)}, f32[1,256]{1,0:T(1,128)S(1)}, u32[]{:S(2)}, u32[]{:S(2)}) collective-permute-start(f32[1,256]{1,0:T(1,128)S(1)} %get-tuple-element.156), channel_id=1, source_target_pairs={{0,16},{16,32},{32,48},{48,64},{64,80},{80,96},{96,112},{112,0},{1... | collective-permute-start | bytes 3080 | tf_op jit(solution)/shard_map/ppermute | solution.py:27
  176.2 4.0 %collective-permute-start.18 = (f32[66,1]{1,0:T(8,128)S(1)}, f32[66,1]{1,0:T(8,128)S(1)}, u32[]{:S(2)}, u32[]{:S(2)}) collective-permute-start(f32[66,1]{1,0:T(8,128)S(1)} %get-tuple-element.132), channel_id=1, source_target_pairs={{1,0},{2,1},{3,2},{4,3},{5,4},{6,5},{7,6},{8,7},{9,8},{10,9},{11,1... | collective-permute-start | bytes 800 | tf_op jit(solution)/shard_map/ppermute | solution.py:29
  176.2 7.3 %collective-permute-start.19 = (f32[66,1]{1,0:T(8,128)S(1)}, f32[66,1]{1,0:T(8,128)S(1)}, u32[]{:S(2)}, u32[]{:S(2)}) collective-permute-start(f32[66,1]{1,0:T(8,128)S(1)} %get-tuple-element.133), channel_id=1, source_target_pairs={{0,1},{1,2},{2,3},{3,4},{4,5},{5,6},{6,7},{7,8},{8,9},{9,10},{10,1... | collective-permute-start | bytes 800 | tf_op jit(solution)/shard_map/ppermute | solution.py:27
  183.8 1.3 collective-permute-start.20
  183.8 4.2 %collective-permute-start.21 = (f32[1,256]{1,0:T(1,128)S(1)}, f32[1,256]{1,0:T(1,128)S(1)}, u32[]{:S(2)}, u32[]{:S(2)}) collective-permute-start(f32[1,256]{1,0:T(1,128)S(1)} %get-tuple-element.154), channel_id=1, source_target_pairs={{0,16},{16,32},{32,48},{48,64},{64,80},{80,96},{96,112},{112,0},{1... | collective-permute-start | bytes 3080 | tf_op jit(solution)/shard_map/ppermute | solution.py:27
  188.1 4.0 %collective-permute-start.22 = (f32[66,1]{1,0:T(8,128)S(1)}, f32[66,1]{1,0:T(8,128)S(1)}, u32[]{:S(2)}, u32[]{:S(2)}) collective-permute-start(f32[66,1]{1,0:T(8,128)S(1)} %get-tuple-element.130), channel_id=1, source_target_pairs={{1,0},{2,1},{3,2},{4,3},{5,4},{6,5},{7,6},{8,7},{9,8},{10,9},{11,1... | collective-permute-start | bytes 800 | tf_op jit(solution)/shard_map/ppermute | solution.py:29
  188.2 7.3 %collective-permute-start.23 = (f32[66,1]{1,0:T(8,128)S(1)}, f32[66,1]{1,0:T(8,128)S(1)}, u32[]{:S(2)}, u32[]{:S(2)}) collective-permute-start(f32[66,1]{1,0:T(8,128)S(1)} %get-tuple-element.131), channel_id=1, source_target_pairs={{0,1},{1,2},{2,3},{3,4},{4,5},{5,6},{6,7},{7,8},{8,9},{9,10},{10,1... | collective-permute-start | bytes 800 | tf_op jit(solution)/shard_map/ppermute | solution.py:27
  195.8 1.3 collective-permute-start.24
  195.8 4.2 %collective-permute-start.25 = (f32[1,256]{1,0:T(1,128)S(1)}, f32[1,256]{1,0:T(1,128)S(1)}, u32[]{:S(2)}, u32[]{:S(2)}) collective-permute-start(f32[1,256]{1,0:T(1,128)S(1)} %get-tuple-element.152), channel_id=1, source_target_pairs={{0,16},{16,32},{32,48},{48,64},{64,80},{80,96},{96,112},{112,0},{1... | collective-permute-start | bytes 3080 | tf_op jit(solution)/shard_map/ppermute | solution.py:27
  200.1 4.0 %collective-permute-start.26 = (f32[66,1]{1,0:T(8,128)S(1)}, f32[66,1]{1,0:T(8,128)S(1)}, u32[]{:S(2)}, u32[]{:S(2)}) collective-permute-start(f32[66,1]{1,0:T(8,128)S(1)} %get-tuple-element.128), channel_id=1, source_target_pairs={{1,0},{2,1},{3,2},{4,3},{5,4},{6,5},{7,6},{8,7},{9,8},{10,9},{11,1... | collective-permute-start | bytes 800 | tf_op jit(solution)/shard_map/ppermute | solution.py:29
  200.1 7.3 %collective-permute-start.27 = (f32[66,1]{1,0:T(8,128)S(1)}, f32[66,1]{1,0:T(8,128)S(1)}, u32[]{:S(2)}, u32[]{:S(2)}) collective-permute-start(f32[66,1]{1,0:T(8,128)S(1)} %get-tuple-element.129), channel_id=1, source_target_pairs={{0,1},{1,2},{2,3},{3,4},{4,5},{5,6},{6,7},{7,8},{8,9},{9,10},{10,1... | collective-permute-start | bytes 800 | tf_op jit(solution)/shard_map/ppermute | solution.py:27
  207.7 1.5 collective-permute-start.28
  207.8 4.2 %collective-permute-start.29 = (f32[1,256]{1,0:T(1,128)S(1)}, f32[1,256]{1,0:T(1,128)S(1)}, u32[]{:S(2)}, u32[]{:S(2)}) collective-permute-start(f32[1,256]{1,0:T(1,128)S(1)} %get-tuple-element.150), channel_id=1, source_target_pairs={{0,16},{16,32},{32,48},{48,64},{64,80},{80,96},{96,112},{112,0},{1... | collective-permute-start | bytes 3080 | tf_op jit(solution)/shard_map/ppermute | solution.py:27
  212.1 4.8 %collective-permute-start.30 = (f32[66,1]{1,0:T(8,128)S(1)}, f32[66,1]{1,0:T(8,128)S(1)}, u32[]{:S(2)}, u32[]{:S(2)}) collective-permute-start(f32[66,1]{1,0:T(8,128)S(1)} %get-tuple-element.126), channel_id=1, source_target_pairs={{1,0},{2,1},{3,2},{4,3},{5,4},{6,5},{7,6},{8,7},{9,8},{10,9},{11,1... | collective-permute-start | bytes 800 | tf_op jit(solution)/shard_map/ppermute | solution.py:29
  212.1 7.3 %collective-permute-start.31 = (f32[66,1]{1,0:T(8,128)S(1)}, f32[66,1]{1,0:T(8,128)S(1)}, u32[]{:S(2)}, u32[]{:S(2)}) collective-permute-start(f32[66,1]{1,0:T(8,128)S(1)} %get-tuple-element.127), channel_id=1, source_target_pairs={{0,1},{1,2},{2,3},{3,4},{4,5},{5,6},{6,7},{7,8},{8,9},{9,10},{10,1... | collective-permute-start | bytes 800 | tf_op jit(solution)/shard_map/ppermute | solution.py:27
where the time goes:
time: 221 us; the launch traced here: 220 us
  other arithmetic  87.3 us (40%)
  waiting for transfers between devices  48.2 us (22%)
  local copies, waits for them, and re-layouts  48 us (22%)
  starting transfers between devices  35.5 us (16%)
    ppermute x16, waiting for transfers between devices, padded_2(): lax.ppermute(tail, axis, [(i, (i + 1) % count) for i in range(count)])  34.5 us
    concatenate x15, other arithmetic, padded_2(): jnp.concatenate([lax.ppermute(tail, axis, [(i, (i + 1) % count) for i in...  26.1 us
    ppermute x16, starting transfers between devices, padded_2(): lax.ppermute(head, axis, [((i + 1) % count, i) for i in range(count)])  22.9 us
    slice x11, local copies, waits for them, and re-layouts, padded_2(): lax.slice_in_dim(cells, cells.shape[dim] - width, cells.shape[dim], axis=...  18.1 us
    ppermute x16, waiting for transfers between devices, padded_2(): lax.ppermute(head, axis, [((i + 1) % count, i) for i in range(count)])  13.7 us
    ppermute x16, starting transfers between devices, padded_2(): lax.ppermute(tail, axis, [(i, (i + 1) % count) for i in range(count)])  12.7 us
    reduce_sum x1, other arithmetic, momentum_update(): north_total = jnp.sum(north_full, axis=0) / north_full.shape[0]  9.02 us
    squeeze x1, local copies, waits for them, and re-layouts, tracer_update(): east_vel = extended[1]  8.85 us
  transfers between devices with their start and end apart: 32, of which 21 were waited for; matrix products, arithmetic and copies ran while one was open for 41% of the time, Pallas kernels for 0%

commit v1 on v0

v1 whole, which is shorter than its diff:
```python
import jax
import jax.numpy as jnp
from jax import lax
from jax.experimental import pallas as pl
from jax.experimental.pallas import tpu as pltpu
from jax.sharding import PartitionSpec as P

ITERS = 6
LEVELS = 40
ROWS = 64
COLS = 256
BLOCKS = ROWS // 8
CHUNK = 8
CHUNKS = LEVELS // CHUNK

damping = 0.05
lower_bound = 0.02
upper_bound = 2.0
cheb_alpha = 2.0 / (upper_bound - lower_bound)
cheb_gamma = (upper_bound + lower_bound) / 2.0
advect_scale = 0.4
force_scale = 4.0
source_scale = 0.5
divergence_scale = 4.0
PRESS = force_scale / LEVELS
DIVERGE = divergence_scale / LEVELS

VMEM = pl.BlockSpec(memory_space=pltpu.VMEM)
ANY = pl.BlockSpec(memory_space=pl.ANY)
SMEM = pl.BlockSpec(memory_space=pltpu.SMEM)
F32 = jnp.float32
TILES = [(b, h) for b in range(BLOCKS) for h in range(2)]


def shape(*dims):
    return jax.ShapeDtypeStruct(dims, F32)


def params():
    return pltpu.CompilerParams(vmem_limit_bytes=40 * 1024 * 1024)


def lane_id(rows=8):
    return lax.broadcasted_iota(jnp.int32, (rows, 128), 1)


def row_id():
    return lax.broadcasted_iota(jnp.int32, (8, 128), 0)


def rows_of(b):
    return slice(8 * b, 8 * b + 8)


def lanes_of(h):
    return slice(128 * h, 128 * h + 128)


def tiles_of(ref, *lead):
    return {(b, h): ref[(*lead, rows_of(b), lanes_of(h))] for b, h in TILES}


def next_row(x, after, last):
    turned = {t: pltpu.roll(x[t], 7, 0) for t in TILES}
    return {
        (b, h): jnp.where(last, after[h] if b == BLOCKS - 1 else turned[b + 1, h], turned[b, h])
        for b, h in TILES
    }


def prev_row(x, before, first):
    turned = {t: pltpu.roll(x[t], 1, 0) for t in TILES}
    return {
        (b, h): jnp.where(first, before[h] if b == 0 else turned[b - 1, h], turned[b, h])
        for b, h in TILES
    }


def next_col(x, after, last):
    turned = {t: pltpu.roll(x[t], 127, 1) for t in TILES}
    return {
        (b, h): jnp.where(last, after[b] if h == 1 else turned[b, 1], turned[b, h])
        for b, h in TILES
    }


def prev_col(x, before, first):
    turned = {t: pltpu.roll(x[t], 1, 1) for t in TILES}
    return {
        (b, h): jnp.where(first, before[b] if h == 0 else turned[b, 0], turned[b, h])
        for b, h in TILES
    }


def spread(ref, k, h):
    return jnp.broadcast_to(ref[h, pl.ds(k, 1), :], (8, 128))


def pack_kernel(
    tile_y, temp, speeds, sea, tally,
    count_out, to_east, to_west, to_north, to_south,
    t_low, t_high, v_high, t_top, t_end, u_end, sems,
):
    copies = [
        pltpu.make_async_copy(temp.at[:, :, pl.ds(0, 128)], t_low, sems.at[0]),
        pltpu.make_async_copy(temp.at[:, :, pl.ds(128, 128)], t_high, sems.at[1]),
        pltpu.make_async_copy(speeds.at[1, :, :, pl.ds(128, 128)], v_high, sems.at[2]),
        pltpu.make_async_copy(temp.at[:, pl.ds(0, 8), :], t_top, sems.at[3]),
        pltpu.make_async_copy(temp.at[:, pl.ds(ROWS - 8, 8), :], t_end, sems.at[4]),
        pltpu.make_async_copy(speeds.at[0, :, pl.ds(ROWS - 8, 8), :], u_end, sems.at[5]),
    ]
    for copy in copies:
        copy.start()
    latitude = tile_y[0] * COLS + lax.broadcasted_iota(jnp.int32, (ROWS, COLS), 1)
    inner = (latitude > 0) & (latitude < tile_y[1] - 1)
    count = jnp.where(inner & (sea[...] == 1), tally[...], 0).astype(F32)
    count_out[...] = count
    for h in range(2):
        to_east[h, 80:86, :] = count[ROWS - 6 :, lanes_of(h)]
        to_east[h, 86:88, :] = jnp.zeros((2, 128), F32)
        to_west[h, 40:46, :] = count[:6, lanes_of(h)]
        to_west[h, 46:48, :] = jnp.zeros((2, 128), F32)
    lane = lane_id(ROWS)

    def gather(ref, column, start, total):
        for k in range(LEVELS):
            total = jnp.where(
                lane == start + k, pltpu.roll(ref[k], (start + k - column) % 128, 1), total
            )
        return total

    copies[0].wait()
    to_south[...] = gather(
        t_low, 0, 0, pltpu.roll(count[:, :128], 40, 1)
    )
    copies[1].wait()
    total = gather(t_high, 127, 0, pltpu.roll(count[:, 128:], (80 - 127) % 128, 1))
    copies[2].wait()
    to_north[...] = gather(v_high, 127, 40, total)
    copies[3].wait()
    copies[4].wait()
    copies[5].wait()
    for h in range(2):
        to_west[h, 0:40, :] = t_top[:, 0, lanes_of(h)]
        to_east[h, 0:40, :] = t_end[:, 7, lanes_of(h)]
        to_east[h, 40:80, :] = u_end[:, 7, lanes_of(h)]


def pack(tile_y, temp, speeds, sea, tally):
    return pl.pallas_call(
        pack_kernel,
        out_shape=(
            shape(ROWS, COLS), shape(2, 88, 128), shape(2, 48, 128), shape(ROWS, 128), shape(ROWS, 128)
        ),
        in_specs=[SMEM, ANY, ANY, VMEM, VMEM],
        out_specs=(VMEM,) * 5,
        scratch_shapes=[
            pltpu.VMEM((LEVELS, ROWS, 128), F32),
            pltpu.VMEM((LEVELS, ROWS, 128), F32),
            pltpu.VMEM((LEVELS, ROWS, 128), F32),
            pltpu.VMEM((LEVELS, 8, COLS), F32),
            pltpu.VMEM((LEVELS, 8, COLS), F32),
            pltpu.VMEM((LEVELS, 8, COLS), F32),
            pltpu.SemaphoreType.DMA((6,)),
        ],
        compiler_params=params(),
        name="pack",
    )(tile_y, temp, speeds, sea, tally)


def column_kernel(
    temp, speeds, mix, count, rain, west, east_in, south, north_in,
    temp_out, speeds_out, force_out, to_east, to_west, q_row, q_col, sides,
    tb, ub, vb, mb, east_lim, north_lim, south_lim, west_lim, run, in_sems, out_sems,
):
    def load(which, c):
        part = pl.ds(c * CHUNK, CHUNK)
        source, target = (
            (mix, mb), (temp, tb), (speeds.at[0], ub), (speeds.at[1], vb)
        )[which]
        return pltpu.make_async_copy(source.at[part], target.at[part], in_sems.at[which, c])

    def store(which, c):
        part = pl.ds(c * CHUNK, CHUNK)
        source, target = (
            (tb, temp_out), (ub, speeds_out.at[0]), (vb, speeds_out.at[1])
        )[which]
        return pltpu.make_async_copy(source.at[part], target.at[part], out_sems.at[which, c])

    for c in range(CHUNKS):
        for which in range(4):
            load(which, c).start()

    lane = lane_id()
    row = row_id()
    first_row, last_row = row == 0, row == 7
    first_lane, last_lane = lane == 0, lane == 127

    counts = tiles_of(count)
    after = {h: jnp.broadcast_to(east_in[h, 40:41, :], (8, 128)) for h in range(2)}
    before = {h: jnp.broadcast_to(west[h, 85:86, :], (8, 128)) for h in range(2)}
    ahead = next_row(counts, after, last_row)
    for b, h in TILES:
        east_lim[rows_of(b), lanes_of(h)] = jnp.minimum(counts[b, h], ahead[b, h])
    for h in range(2):
        west_lim[:, lanes_of(h)] = jnp.minimum(counts[0, h], before[h])
    after = {b: pltpu.roll(north_in[rows_of(b), :], 127 - 40, 1) for b in range(BLOCKS)}
    ahead = next_col(counts, after, last_lane)
    for b, h in TILES:
        north_lim[rows_of(b), lanes_of(h)] = jnp.minimum(counts[b, h], ahead[b, h])
    for b in range(BLOCKS):
        south_lim[rows_of(b), :] = jnp.minimum(
            counts[b, 0], pltpu.roll(south[rows_of(b), :], 128 - 80, 1)
        )

    zero = jnp.zeros((8, 128), F32)

    def forward(k):
        level = k.astype(F32)
        masked = jnp.where(k == 0, F32(1e9), level)
        t = tiles_of(tb, k)
        u = tiles_of(ub, k)
        v = tiles_of(vb, k)
        wet = tiles_of(count)
        t_after = {h: spread(east_in, k, h) for h in range(2)}
        ahead = next_row(t, t_after, last_row)
        flux = {
            i: jnp.where(level < east_lim[rows_of(i[0]), lanes_of(i[1])], u[i], 0.0)
            * jnp.where(u[i] > 0.0, t[i], ahead[i])
            for i in TILES
        }
        edge = {}
        for h in range(2):
            speed = spread(west, k + 40, h)
            edge[h] = jnp.where(level < west_lim[:, lanes_of(h)], speed, 0.0) * jnp.where(
                speed > 0.0, spread(west, k, h), t[0, h]
            )
        behind = prev_row(flux, edge, first_row)
        change = {i: flux[i] - behind[i] for i in TILES}
        t_after = {b: pltpu.roll(north_in[rows_of(b), :], 127 - k, 1) for b in range(BLOCKS)}
        ahead = next_col(t, t_after, last_lane)
        flux = {
            i: jnp.where(level < north_lim[rows_of(i[0]), lanes_of(i[1])], v[i], 0.0)
            * jnp.where(v[i] > 0.0, t[i], ahead[i])
            for i in TILES
        }
        edge = {}
        for b in range(BLOCKS):
            held = south[rows_of(b), :]
            speed = pltpu.roll(held, 88 - k, 1)
            edge[b] = jnp.where(level < south_lim[rows_of(b), :], speed, 0.0) * jnp.where(
                speed > 0.0, pltpu.roll(held, 128 - k, 1), t[b, 0]
            )
        behind = prev_col(flux, edge, first_lane)
        below_at = jnp.minimum(k + 1, LEVELS - 1)
        above_at = jnp.maximum(k - 1, 0)
        for i in TILES:
            at = (rows_of(i[0]), lanes_of(i[1]))
            total = change[i] + (flux[i] - behind[i])
            source = t[i] - jnp.where(level < wet[i], advect_scale * total, 0.0)
            a = jnp.where(masked < wet[i], mb[(k, *at)], 0.0)
            below = jnp.where(level + 1.0 < wet[i], mb[(below_at, *at)], 0.0)
            factor = mb[(above_at, *at)]
            value = tb[(above_at, *at)]
            pivot = (1.0 + below) + (a - a * factor)
            inverse = pl.reciprocal(pivot, approx=True)
            inverse = inverse * (2.0 - pivot * inverse)
            tb[(k, *at)] = (source + a * value) * inverse
            mb[(k, *at)] = below * inverse

    load(0, 0).wait()

    def forward_chunk(c, _):
        @pl.when(c < CHUNKS - 1)
        def _():
            load(0, c + 1).wait()

        for which in range(1, 4):
            load(which, c).wait()

        def step(k, _):
            forward(k)
            return 0

        return lax.fori_loop(c * CHUNK, (c + 1) * CHUNK, step, 0)

    lax.fori_loop(0, CHUNKS, forward_chunk, 0)

    def back_chunk(c_up, x):
        c = CHUNKS - 1 - c_up

        def step(n, x):
            k = c * CHUNK + (CHUNK - 1 - n)
            out = []
            for i, below in zip(TILES, x):
                at = (k, rows_of(i[0]), lanes_of(i[1]))
                value = tb[at] + mb[at] * below
                tb[at] = value
                out.append(value)
            return tuple(out)

        x = lax.fori_loop(0, CHUNK, step, x)
        store(0, c).start()
        return x

    lax.fori_loop(0, CHUNKS, back_chunk, tuple(zero for _ in TILES))

    run[...] = jnp.zeros_like(run)
    q_col[...] = jnp.zeros_like(q_col)

    def momentum(k, carry):
        level = k.astype(F32)
        east_sum, north_sum, row_sum, col_sum = carry
        q = {}
        for i in TILES:
            at = (rows_of(i[0]), lanes_of(i[1]))
            half = 0.5 * tb[(k, *at)]
            q[i] = run[at] + half
            run[at] = q[i] + half
        for h in range(2):
            q_row[h, pl.ds(k, 1), :] = q[0, h][0:1]
        ahead = next_row(q, {h: zero for h in range(2)}, last_row)
        east_new = []
        for i, total in zip(TILES, east_sum):
            at = (rows_of(i[0]), lanes_of(i[1]))
            speed = jnp.where(
                level < east_lim[at], ub[(k, *at)] - PRESS * (q[i] - ahead[i]), 0.0
            )
            ub[(k, *at)] = speed
            east_new.append(total + speed)
        ahead = next_col(q, {b: zero for b in range(BLOCKS)}, last_lane)
        north_new = []
        for i, total in zip(TILES, north_sum):
            at = (rows_of(i[0]), lanes_of(i[1]))
            speed = jnp.where(
                level < north_lim[at], vb[(k, *at)] - PRESS * (q[i] - ahead[i]), 0.0
            )
            vb[(k, *at)] = speed
            north_new.append(total + speed)
        row_new = tuple(
            row_sum[h] + jnp.where(level < west_lim[:, lanes_of(h)], PRESS * q[0, h], 0.0)
            for h in range(2)
        )
        col_new = []
        for b in range(BLOCKS):
            col_new.append(
                col_sum[b] + jnp.where(level < south_lim[rows_of(b), :], PRESS * q[b, 0], 0.0)
            )
            q_col[rows_of(b), :] = jnp.where(
                lane == k, pltpu.roll(q[b, 0], k, 1), q_col[rows_of(b), :]
            )
        return tuple(east_new), tuple(north_new), row_new, tuple(col_new)

    def momentum_chunk(c, carry):
        carry = lax.fori_loop(c * CHUNK, (c + 1) * CHUNK, momentum, carry)
        store(1, c).start()
        store(2, c).start()
        return carry

    blank = tuple(zero for _ in TILES)
    east_sum, north_sum, row_sum, col_sum = lax.fori_loop(
        0, CHUNKS, momentum_chunk, (blank, blank, (zero, zero), (zero,) * BLOCKS)
    )

    east_sum = dict(zip(TILES, east_sum))
    north_sum = dict(zip(TILES, north_sum))
    east_before = prev_row(east_sum, row_sum, first_row)
    north_before = prev_col(north_sum, col_sum, first_lane)
    for i in TILES:
        at = (rows_of(i[0]), lanes_of(i[1]))
        divergence = (east_sum[i] - east_before[i]) + (north_sum[i] - north_before[i])
        force_out[at] = jnp.where(
            count[at] > 0.0, source_scale * rain[at] - DIVERGE * divergence, 0.0
        )
    for b in range(BLOCKS):
        sides[rows_of(b), :] = jnp.where(
            first_lane,
            pltpu.roll(north_sum[b, 1], 1, 1),
            jnp.where(last_lane, pltpu.roll(col_sum[b], 127, 1), 0.0),
        )
    to_east[0:8, 0:COLS] = pltpu.roll(force_out[ROWS - 8 : ROWS, :], 5, 0)
    to_east[0:8, COLS:] = pltpu.roll(sides[ROWS - 8 : ROWS, :], 5, 0)
    to_west[0:8, 0:COLS] = force_out[0:8, :]
    to_west[0:8, COLS:] = sides[0:8, :]
    for h in range(2):
        to_east[5:6, lanes_of(h)] = east_sum[BLOCKS - 1, h][7:8]
        to_west[5:6, lanes_of(h)] = row_sum[h][0:1]

    for c in range(CHUNKS):
        for which in range(3):
            store(which, c).wait()


def columns(temp, speeds, mix, count, rain, west, east_in, south, north_in):
    block = pltpu.VMEM((LEVELS, ROWS, COLS), F32)
    return pl.pallas_call(
        column_kernel,
        out_shape=(
            shape(LEVELS, ROWS, COLS), shape(2, LEVELS, ROWS, COLS), shape(ROWS, COLS),
            shape(8, COLS + 128), shape(8, COLS + 128), shape(2, LEVELS, 128),
            shape(ROWS, 128), shape(ROWS, 128),
        ),
        in_specs=[ANY, ANY, ANY] + [VMEM] * 6,
        out_specs=(ANY, ANY) + (VMEM,) * 6,
        scratch_shapes=[
            block, block, block, block,
            pltpu.VMEM((ROWS, COLS), F32), pltpu.VMEM((ROWS, COLS), F32),
            pltpu.VMEM((ROWS, 128), F32), pltpu.VMEM((8, COLS), F32),
            pltpu.VMEM((ROWS, COLS), F32),
            pltpu.SemaphoreType.DMA((4, CHUNKS)), pltpu.SemaphoreType.DMA((3, CHUNKS)),
        ],
        compiler_params=params(),
        name="columns",
    )(temp, speeds, mix, count, rain, west, east_in, south, north_in)


def mend_kernel(
    speeds, q_row, q_col, count, east_in, north_in, speeds_out, rows, cols, sems
):
    row_part = (0, slice(None), pl.ds(ROWS - 8, 8), slice(None))
    col_part = (1, slice(None), slice(None), pl.ds(128, 128))
    load_rows = pltpu.make_async_copy(speeds.at[row_part], rows, sems.at[0])
    load_cols = pltpu.make_async_copy(speeds.at[col_part], cols, sems.at[1])
    load_rows.start()
    load_cols.start()
    last_row = row_id() == 7
    load_rows.wait()
    for h in range(2):
        limit = jnp.minimum(
            count[ROWS - 8 :, lanes_of(h)], jnp.broadcast_to(east_in[h, 40:41, :], (8, 128))
        )
        limit = jnp.where(last_row, limit, 0.0)
        for k in range(LEVELS):
            rows[k, :, lanes_of(h)] = rows[k, :, lanes_of(h)] + jnp.where(
                float(k) < limit, PRESS * spread(q_row, k, h), 0.0
            )
    save_rows = pltpu.make_async_copy(rows, speeds_out.at[row_part], sems.at[2])
    save_rows.start()
    last_lane = lane_id(ROWS) == 127
    limit = jnp.minimum(count[:, 128:], pltpu.roll(north_in[...], 127 - 40, 1))
    limit = jnp.where(last_lane, limit, 0.0)
    load_cols.wait()
    for k in range(LEVELS):
        cols[k] = cols[k] + jnp.where(
            float(k) < limit, PRESS * pltpu.roll(q_col[...], 127 - k, 1), 0.0
        )
    save_cols = pltpu.make_async_copy(cols, speeds_out.at[col_part], sems.at[3])
    save_cols.start()
    save_rows.wait()
    save_cols.wait()


def mend(speeds, q_row, q_col, count, east_in, north_in):
    return pl.pallas_call(
        mend_kernel,
        out_shape=shape(2, LEVELS, ROWS, COLS),
        in_specs=[ANY] + [VMEM] * 5,
        out_specs=ANY,
        scratch_shapes=[
            pltpu.VMEM((LEVELS, 8, COLS), F32),
            pltpu.VMEM((LEVELS, ROWS, 128), F32),
            pltpu.SemaphoreType.DMA((4,)),
        ],
        input_output_aliases={0: 0},
        compiler_params=params(),
        name="mend",
    )(speeds, q_row, q_col, count, east_in, north_in)


EXT = ROWS + 16


def edges_kernel(
    force, sides, count, west, east_in, own_east, own_west, from_west, from_east,
    force_ext, count_ext, sides_ext, to_north, to_south,
):
    zeros8 = jnp.zeros((8, COLS), F32)
    count_ext[0:8, :] = zeros8
    for h in range(2):
        count_ext[2:8, lanes_of(h)] = west[h, 80:86, :]
    count_ext[8 : 8 + ROWS, :] = count[...]
    count_ext[8 + ROWS :, :] = zeros8
    for h in range(2):
        count_ext[8 + ROWS : 14 + ROWS, lanes_of(h)] = east_in[h, 40:46, :]
    sides_ext[0:8, :] = jnp.zeros((8, 128), F32)
    sides_ext[3:8, :] = from_west[0:5, COLS:]
    sides_ext[8 : 8 + ROWS, :] = sides[...]
    sides_ext[8 + ROWS :, :] = jnp.zeros((8, 128), F32)
    sides_ext[8 + ROWS : 13 + ROWS, :] = from_east[0:5, COLS:]
    force_ext[0:8, :] = zeros8
    force_ext[3:8, :] = from_west[0:5, 0:COLS]
    force_ext[8 : 8 + ROWS, :] = force[...]
    force_ext[8 + ROWS :, :] = zeros8
    force_ext[8 + ROWS : 13 + ROWS, :] = from_east[0:5, 0:COLS]

    def add(at, amount):
        force_ext[at : at + 1, :] = force_ext[at : at + 1, :] + jnp.where(
            count_ext[at : at + 1, :] > 0.0, DIVERGE * amount, 0.0
        )

    add(7, -own_west[5:6, 0:COLS])
    add(8, from_west[5:6, 0:COLS])
    add(7 + ROWS, -from_east[5:6, 0:COLS])
    add(8 + ROWS, own_east[5:6, 0:COLS])
    lane = lane_id(EXT)
    side = sides_ext[...]
    to_north[...] = jnp.where(
        lane >= 123,
        force_ext[:, 128:],
        jnp.where(lane == 0, side, pltpu.roll(count_ext[:, 128:], 122, 1)),
    )
    to_south[...] = jnp.where(
        lane < 5,
        force_ext[:, :128],
        jnp.where(lane == 127, side, pltpu.roll(count_ext[:, :128], 8, 1)),
    )


def edges(*args):
    return pl.pallas_call(
        edges_kernel,
        out_shape=(
            shape(EXT, COLS), shape(EXT, COLS), shape(EXT, 128), shape(EXT, 128), shape(EXT, 128)
        ),
        in_specs=[VMEM] * 9,
        out_specs=(VMEM,) * 5,
        compiler_params=params(),
        name="edges",
    )(*args)


def chebyshev_kernel(force_ext, count_ext, sides_ext, south, north, out):
    lane = lane_id(EXT)
    count_side = jnp.where(
        lane >= 122,
        pltpu.roll(south[...], 6, 1),
        jnp.where(lane < 6, pltpu.roll(north[...], 120, 1), 0.0),
    )
    force_side = jnp.where(
        lane >= 123, south[...], jnp.where(lane < 5, north[...], 0.0)
    )
    side = sides_ext[...]
    low, high = force_ext[:, :128], force_ext[:, 128:]
    low = low + jnp.where(
        (lane == 0) & (count_ext[:, :128] > 0.0), DIVERGE * south[...], 0.0
    )
    high = high - jnp.where(
        (lane == 127) & (count_ext[:, 128:] > 0.0), DIVERGE * north[...], 0.0
    )
    force_side = force_side + jnp.where(
        (lane == 0) & (count_side > 0.0), DIVERGE * side, 0.0
    )
    force_side = force_side - jnp.where(
        (lane == 127) & (count_side > 0.0), DIVERGE * side, 0.0
    )
    force = jnp.concatenate([low, high, force_side], axis=1)
    count = jnp.concatenate([count_ext[...], count_side], axis=1)
    root = jnp.sqrt(count * (1.0 / LEVELS))
    wide = COLS + 128

    def total(field):
        sideways = pltpu.roll(field, 1, 1) + pltpu.roll(field, wide - 1, 1)
        mixed = field + 0.5 * sideways
        return sideways + (pltpu.roll(mixed, 1, 0) + pltpu.roll(mixed, EXT - 1, 0))

    diag = damping + root * total(root)
    inverse = 1.0 / diag
    update = inverse * force * (1.0 / cheb_gamma)
    iterate = update
    omega = 2.0 / cheb_gamma
    for step in range(1, ITERS):
        residual = force - (diag * iterate - root * total(root * iterate))
        omega = 1.0 / (cheb_gamma - omega / (4.0 * cheb_alpha * cheb_alpha))
        update = omega * inverse * residual + (cheb_gamma * omega - 1.0) * update
        iterate = iterate + update
    out[...] = iterate[8 : 8 + ROWS, 0:COLS]


def chebyshev(*args):
    return pl.pallas_call(
        chebyshev_kernel,
        out_shape=shape(ROWS, COLS),
        in_specs=[VMEM] * 5,
        out_specs=VMEM,
        compiler_params=params(),
        name="chebyshev",
    )(*args)


def shift(array, axis, step):
    count = lax.axis_size(axis)
    return lax.ppermute(array, axis, [(i, (i + step) % count) for i in range(count)])


def local(
    thermal_departure,
    current_speeds,
    mixing_coefficient,
    seawater_indicator,
    submerged_layer_tally,
    rainfall_runoff_input,
):
    tile_y = jnp.stack(
        [lax.axis_index("gy"), jnp.int32(lax.axis_size("gy") * COLS)]
    ).astype(jnp.int32)
    count, to_east, to_west, to_north, to_south = pack(
        tile_y, thermal_departure, current_speeds,
        seawater_indicator, submerged_layer_tally,
    )
    south = shift(to_north, "gy", 1)
    north = shift(to_south, "gy", -1)
    west = shift(to_east, "gx", 1)
    east = shift(to_west, "gx", -1)
    temp_next, speeds, force, own_east, own_west, q_row, q_col, sides = columns(
        thermal_departure, current_speeds, mixing_coefficient, count,
        rainfall_runoff_input, west, east, south, north,
    )
    from_west = shift(own_east, "gx", 1)
    from_east = shift(own_west, "gx", -1)
    q_north = shift(q_col, "gy", -1)
    q_east = shift(q_row, "gx", -1)
    force_ext, count_ext, sides_ext, to_north, to_south = edges(
        force, sides, count, west, east, own_east, own_west, from_west, from_east
    )
    from_south = shift(to_north, "gy", 1)
    from_north = shift(to_south, "gy", -1)
    velocity_next = mend(speeds, q_east, q_north, count, east, north)
    surface = chebyshev(force_ext, count_ext, sides_ext, from_south, from_north)
    return (temp_next, velocity_next, surface)


def solution(mesh):
    placed = (
        P(None, "gx", "gy"),
        P(None, None, "gx", "gy"),
        P(None, "gx", "gy"),
        P("gx", "gy"),
        P("gx", "gy"),
        P("gx", "gy"),
    )
    return jax.shard_map(
        local,
        mesh=mesh,
        in_specs=placed,
        out_specs=(P(None, "gx", "gy"), P(None, None, "gx", "gy"), P("gx", "gy")),
        check_vma=False,
    )
```

time: 221 us -> 59 us (0.27)
  other arithmetic: 87.3 us -> 0.08 us
  waiting for transfers between devices: 48.2 us -> 5.24 us
  local copies, waits for them, and re-layouts: 48 us -> 5.91 us
  Pallas kernels: 0 us -> 26.7 us
  starting transfers between devices: 35.5 us -> 19.9 us
    ppermute x32 -> x10, waiting for transfers between devices: 48.2 us -> 5.24 us  [shift(): lax.ppermute(array, axis, [(i, (i + step) % count) for i in range(count)])]
    pallas_call x0 -> x5, Pallas kernels: none -> 26.7 us  [the longest x1 19.7 us: columns(): pl.pallas_call(column_kernel, out_shape=(shape(LEVELS, ROWS, COLS), shape...]
    concatenate x15 -> x0, other arithmetic: 26.1 us -> none  [padded_2(): jnp.concatenate([lax.ppermute(tail, axis, [(i, (i + 1) % count) for i in...]
    slice x19 -> x0, local copies, waits for them, and re-layouts: 24.7 us -> none  [the longest x11 18.1 us: padded_2(): lax.slice_in_dim(cells, cells.shape[dim] - width, cells.shape[dim], axis=...]
    reduce_sum x2 -> x0, other arithmetic: 17.6 us -> none  [the longest x1 9.02 us: momentum_update(): north_total = jnp.sum(north_full, axis=0) / north_full.shape[0]]
    ppermute x32 -> x10, starting transfers between devices: 35.5 us -> 19.9 us  [shift(): lax.ppermute(array, axis, [(i, (i + step) % count) for i in range(count)])]
    add x3 -> x0, other arithmetic: 11.4 us -> none  [the longest x1 5.52 us: tracer_update(): jnp.maximum(east_open, 0.0) * temp_ext[:, :-1, 1:-1]]
    ppermute x4 -> x0, local copies, waits for them, and re-layouts: 10.8 us -> none  [the longest x2 5.47 us: padded_2(): lax.ppermute(tail, axis, [(i, (i + 1) % count) for i in range(count)])]
  transfers between devices with their start and end apart: 32 -> 10, of which waited for: 21 -> 3; matrix products, arithmetic and copies ran while one was open for 41% -> 0% of each run, Pallas kernels for 0% -> 5%
where the time goes in v1:
time: 59 us; the launch traced here: 58.7 us
  Pallas kernels  26.7 us (45%)
  starting transfers between devices  19.9 us (34%)
  local copies, waits for them, and re-layouts  5.91 us (10%)
  waiting for transfers between devices  5.24 us (9%)
  between operations  0.74 us (1%)
    ppermute x10, starting transfers between devices, shift(): lax.ppermute(array, axis, [(i, (i + step) % count) for i in range(count)])  19.9 us
    pallas_call x1, Pallas kernels, columns(): pl.pallas_call(column_kernel, out_shape=(shape(LEVELS, ROWS, COLS), shape...  19.7 us
    unnamed x14, local copies, waits for them, and re-layouts  5.91 us
    ppermute x10, waiting for transfers between devices, shift(): lax.ppermute(array, axis, [(i, (i + step) % count) for i in range(count)])  5.24 us
    pallas_call x1, Pallas kernels, mend(): pl.pallas_call(mend_kernel, out_shape=shape(2, LEVELS, ROWS, COLS), in_sp...  2.93 us
    pallas_call x1, Pallas kernels, pack(): pl.pallas_call(pack_kernel, out_shape=(shape(ROWS, COLS), shape(2, 88, 12...  2.28 us
    pallas_call x1, Pallas kernels, chebyshev(): pl.pallas_call(chebyshev_kernel, out_shape=shape(ROWS, COLS), in_specs=[V...  1.72 us
  transfers between devices with their start and end apart: 10, of which 3 were waited for; matrix products, arithmetic and copies ran while one was open for 0% of the time, Pallas kernels for 5%

profile of v1, /device:TPU:0, one launch (start us, length us, event | category | flops | bytes accessed | tf_op | source)
XLA Modules:
  0.0 58.7 jit_solution(15805532990305426818)
XLA Ops:
  0.6 0.1 pad_add_fusion.tile_y
  0.7 0.0 copy-start
  0.7 2.5 %copy-done = f32[2,40,64,256]{3,2,1,0:T(8,128)S(1)} copy-done((f32[2,40,64,256]{3,2,1,0:T(8,128)S(1)}, f32[2,40,64,256]{3,2,1,0:T(8,128)}, u32[]{:S(2)}) %copy-start) | copy-done | bytes 5242904
  3.2 0.0 copy-start.2
  3.2 1.7 %copy-done.2 = f32[40,64,256]{2,1,0:T(8,128)S(1)} copy-done((f32[40,64,256]{2,1,0:T(8,128)S(1)}, f32[40,64,256]{2,1,0:T(8,128)}, u32[]{:S(2)}) %copy-start.2) | copy-done | bytes 2621464
  4.9 0.0 copy-start.4
  4.9 0.8 %copy-done.4 = s32[64,256]{1,0:T(8,128)S(1)} copy-done((s32[64,256]{1,0:T(8,128)S(1)}, s32[64,256]{1,0:T(8,128)}, u32[]{:S(2)}) %copy-start.4) | copy-done | bytes 65560
  5.8 0.0 copy-start.5
  5.8 0.8 %copy-done.5 = s32[64,256]{1,0:T(8,128)S(1)} copy-done((s32[64,256]{1,0:T(8,128)S(1)}, s32[64,256]{1,0:T(8,128)}, u32[]{:S(2)}) %copy-start.5) | copy-done | bytes 65560
  6.6 0.0 copy-start.1
  6.6 0.0 copy-start.3
  6.6 0.0 copy-start.6
  6.6 2.3 %pack.1 = (f32[64,256]{1,0:T(8,128)S(1)}, f32[2,88,128]{2,1,0:T(8,128)S(1)}, f32[2,48,128]{2,1,0:T(8,128)S(1)}, f32[64,128]{1,0:T(8,128)S(1)}, f32[64,128]{1,0:T(8,128)S(1)}) custom-call(s32[2]{0:T(128)S(1)} %pad_add_fusion.tile_y, f32[40,64,256]{2,1,0:T(8,128)S(1)} %copy-done.2, f32[2,40,64,256]{3,2,1,0:T(8,128)S(1)} %copy-done, s32[64,256]{1,0:T(8,128)S(1)} %copy-done.4, ...), custom_call_target="tpu_custom_call" | custom-call | tf_op jit(solution)/shard_map/pack/pallas_call | solution.py:150
  8.9 0.0 collective-permute-start
  8.9 2.9 %collective-permute-start.1 = (f32[2,48,128]{2,1,0:T(8,128)S(1)}, f32[2,48,128]{2,1,0:T(8,128)S(1)}, u32[]{:S(2)}, u32[]{:S(2)}) collective-permute-start(f32[2,48,128]{2,1,0:T(8,128)S(1)} %get-tuple-element.23), channel_id=1, source_target_pairs={{0,112},{16,0},{32,16},{48,32},{64,48},{80,64},{96,80},{112,96},{1... | collective-permute-start | bytes 147464 | tf_op jit(solution)/shard_map/ppermute | solution.py:592
  11.9 1.7 %collective-permute-start.2 = (f32[64,128]{1,0:T(8,128)S(1)}, f32[64,128]{1,0:T(8,128)S(1)}, u32[]{:S(2)}, u32[]{:S(2)}) collective-permute-start(f32[64,128]{1,0:T(8,128)S(1)} %get-tuple-element.24), channel_id=1, source_target_pairs={{0,1},{1,2},{2,3},{3,4},{4,5},{5,6},{6,7},{7,8},{8,9},{9,10},{10,1... | collective-permute-start | bytes 98312 | tf_op jit(solution)/shard_map/ppermute | solution.py:592
  13.5 4.9 %collective-permute-start.3 = (f32[64,128]{1,0:T(8,128)S(1)}, f32[64,128]{1,0:T(8,128)S(1)}, u32[]{:S(2)}, u32[]{:S(2)}) collective-permute-start(f32[64,128]{1,0:T(8,128)S(1)} %get-tuple-element.25), channel_id=1, source_target_pairs={{0,15},{1,0},{2,1},{3,2},{4,3},{5,4},{6,5},{7,6},{8,7},{9,8},{10,9... | collective-permute-start | bytes 98312 | tf_op jit(solution)/shard_map/ppermute | solution.py:592
  18.5 1.9 %collective-permute-done.2.south = f32[64,128]{1,0:T(8,128)S(1)} collective-permute-done((f32[64,128]{1,0:T(8,128)S(1)}, f32[64,128]{1,0:T(8,128)S(1)}, u32[]{:S(2)}, u32[]{:S(2)}) %collective-permute-start.2) | collective-permute-done | bytes 32800 | tf_op jit(solution)/shard_map/ppermute | solution.py:592
  20.3 0.0 collective-permute-done.3.north_in
  20.3 0.0 collective-permute-done.1.east_in
  20.3 0.0 collective-permute-done.west
  20.4 0.0 copy-done.1
  20.4 0.0 copy-done.3
  20.4 0.0 copy-done.6
  20.4 19.7 %columns.1 = (f32[40,64,256]{2,1,0:T(8,128)}, f32[2,40,64,256]{3,2,1,0:T(8,128)}, f32[64,256]{1,0:T(8,128)S(1)}, f32[8,384]{1,0:T(8,128)S(1)}, f32[8,384]{1,0:T(...) custom-call(f32[40,64,256]{2,1,0:T(8,128)S(1)} %copy-done.2, ...), custom_call_target="tpu_custom_call" | custom-call | tf_op jit(solution)/shard_map/columns/pallas_call | solution.py:396
  40.1 0.0 collective-permute-start.6
  40.1 2.9 %collective-permute-start.7 = (f32[8,384]{1,0:T(8,128)S(1)}, f32[8,384]{1,0:T(8,128)S(1)}, u32[]{:S(2)}, u32[]{:S(2)}) collective-permute-start(f32[8,384]{1,0:T(8,128)S(1)} %get-tuple-element.33.own_west), channel_id=1, source_target_pairs={{0,112},{16,0},{32,16},{48,32},{64,48},{80,64},{96,80},{112,96},{1... | collective-permute-start | bytes 36872 | tf_op jit(solution)/shard_map/ppermute | solution.py:592
  43.1 0.0 collective-permute-start.4
  43.1 1.3 %collective-permute-done.6.from_west = f32[8,384]{1,0:T(8,128)S(1)} collective-permute-done((f32[8,384]{1,0:T(8,128)S(1)}, f32[8,384]{1,0:T(8,128)S(1)}, u32[]{:S(2)}, u32[]{:S(2)}) %collective-permute-start.6) | collective-permute-done | bytes 12320 | tf_op jit(solution)/shard_map/ppermute | solution.py:592
  44.4 0.0 collective-permute-done.7.from_east
  44.5 0.1 edges.1
  44.6 0.1 collective-permute-start.8
  44.7 5.4 %collective-permute-start.9 = (f32[80,128]{1,0:T(8,128)S(1)}, f32[80,128]{1,0:T(8,128)S(1)}, u32[]{:S(2)}, u32[]{:S(2)}) collective-permute-start(f32[80,128]{1,0:T(8,128)S(1)} %get-tuple-element.38), channel_id=1, source_target_pairs={{0,15},{1,0},{2,1},{3,2},{4,3},{5,4},{6,5},{7,6},{8,7},{9,8},{10,9... | collective-permute-start | bytes 122888 | tf_op jit(solution)/shard_map/ppermute | solution.py:592
  50.1 1.9 %collective-permute-start.5 = (f32[64,128]{1,0:T(8,128)S(1)}, f32[64,128]{1,0:T(8,128)S(1)}, u32[]{:S(2)}, u32[]{:S(2)}) collective-permute-start(f32[64,128]{1,0:T(8,128)S(1)} %get-tuple-element.29), channel_id=1, source_target_pairs={{0,15},{1,0},{2,1},{3,2},{4,3},{5,4},{6,5},{7,6},{8,7},{9,8},{10,9... | collective-permute-start | bytes 98312 | tf_op jit(solution)/shard_map/ppermute | solution.py:592
  52.0 2.0 %collective-permute-done.5.q_col = f32[64,128]{1,0:T(8,128)S(1)} collective-permute-done((f32[64,128]{1,0:T(8,128)S(1)}, f32[64,128]{1,0:T(8,128)S(1)}, u32[]{:S(2)}, u32[]{:S(2)}) %collective-permute-start.5) | collective-permute-done | bytes 32800 | tf_op jit(solution)/shard_map/ppermute | solution.py:592
  54.0 0.0 collective-permute-done.4.q_row
  54.0 2.9 %mend.1 = f32[2,40,64,256]{3,2,1,0:T(8,128)} custom-call(f32[2,40,64,256]{3,2,1,0:T(8,128)} %get-tuple-element.27.speeds, f32[2,40,128]{2,1,0:T(8,128)S(1)} %collective-permute-done.4.q_row, f32[64,128]{1,0:T(8,128)S(1)} %collective-permute-done.5.q_col, f32[64,256]{1,0:T(8,128)S(1)} %get-tuple-element.21.count, ...), custom_call_target="tpu_custom_call", output_to_operand_aliasing={{}: (0, {})} | custom-call | tf_op jit(solution)/shard_map/mend/pallas_call | solution.py:454
  56.9 0.0 collective-permute-done.8.south
  56.9 0.0 collective-permute-done.9.north
  56.9 1.7 %chebyshev.1 = f32[64,256]{1,0:T(8,128)} custom-call(f32[80,256]{1,0:T(8,128)S(1)} %get-tuple-element.34.force_ext, f32[80,256]{1,0:T(8,128)S(1)} %get-tuple-element.35.count_ext, f32[80,128]{1,0:T(8,128)S(1)} %get-tuple-element.36.sides_ext, f32[80,128]{1,0:T(8,128)S(1)} %collective-permute-done.8.south, f32[80,128]{1,0:T(8,128)S(1)} %collective-permute-done.9.north), custom_call_target="tpu_custom_call" | custom-call | tf_op jit(solution)/shard_map/chebyshev/pallas_call | solution.py:580
Async XLA Ops:
  0.7 2.5 %copy-start = (f32[2,40,64,256]{3,2,1,0:T(8,128)S(1)}, f32[2,40,64,256]{3,2,1,0:T(8,128)}, u32[]{:S(2)}) copy-start(f32[2,40,64,256]{3,2,1,0:T(8,128)} %speeds.3) | copy-start | bytes 15728644
  3.2 1.7 %copy-start.2 = (f32[40,64,256]{2,1,0:T(8,128)S(1)}, f32[40,64,256]{2,1,0:T(8,128)}, u32[]{:S(2)}) copy-start(f32[40,64,256]{2,1,0:T(8,128)} %temp.3) | copy-start | bytes 7864324
  4.9 0.8 %copy-start.4 = (s32[64,256]{1,0:T(8,128)S(1)}, s32[64,256]{1,0:T(8,128)}, u32[]{:S(2)}) copy-start(s32[64,256]{1,0:T(8,128)} %sea.1) | copy-start | bytes 196612
  5.8 0.8 %copy-start.5 = (s32[64,256]{1,0:T(8,128)S(1)}, s32[64,256]{1,0:T(8,128)}, u32[]{:S(2)}) copy-start(s32[64,256]{1,0:T(8,128)} %tally.1) | copy-start | bytes 196612
  6.6 13.7 %copy-start.1 = (f32[2,40,64,256]{3,2,1,0:T(8,128)S(1)}, f32[2,40,64,256]{3,2,1,0:T(8,128)}, u32[]{:S(2)}) copy-start(f32[2,40,64,256]{3,2,1,0:T(8,128)} %speeds.3) | copy-start | bytes 15728644
  6.6 13.7 %copy-start.3 = (f32[40,64,256]{2,1,0:T(8,128)S(1)}, f32[40,64,256]{2,1,0:T(8,128)}, u32[]{:S(2)}) copy-start(f32[40,64,256]{2,1,0:T(8,128)} %mix.1) | copy-start | bytes 7864324
  6.6 13.8 %copy-start.6 = (f32[64,256]{1,0:T(8,128)S(1)}, f32[64,256]{1,0:T(8,128)}, u32[]{:S(2)}) copy-start(f32[64,256]{1,0:T(8,128)} %rain.1) | copy-start | bytes 196612
  8.9 11.4 %collective-permute-start = (f32[2,88,128]{2,1,0:T(8,128)S(1)}, f32[2,88,128]{2,1,0:T(8,128)S(1)}, u32[]{:S(2)}, u32[]{:S(2)}) collective-permute-start(f32[2,88,128]{2,1,0:T(8,128)S(1)} %get-tuple-element.22), channel_id=1, source_target_pairs={{0,16},{16,32},{32,48},{48,64},{64,80},{80,96},{96,112},{112,0},{1... | collective-permute-start | bytes 270344 | tf_op jit(solution)/shard_map/ppermute | solution.py:592
  8.9 11.4 %collective-permute-start.1 = (f32[2,48,128]{2,1,0:T(8,128)S(1)}, f32[2,48,128]{2,1,0:T(8,128)S(1)}, u32[]{:S(2)}, u32[]{:S(2)}) collective-permute-start(f32[2,48,128]{2,1,0:T(8,128)S(1)} %get-tuple-element.23), channel_id=1, source_target_pairs={{0,112},{16,0},{32,16},{48,32},{64,48},{80,64},{96,80},{112,96},{1... | collective-permute-start | bytes 147464 | tf_op jit(solution)/shard_map/ppermute | solution.py:592
  11.9 8.5 %collective-permute-start.2 = (f32[64,128]{1,0:T(8,128)S(1)}, f32[64,128]{1,0:T(8,128)S(1)}, u32[]{:S(2)}, u32[]{:S(2)}) collective-permute-start(f32[64,128]{1,0:T(8,128)S(1)} %get-tuple-element.24), channel_id=1, source_target_pairs={{0,1},{1,2},{2,3},{3,4},{4,5},{5,6},{6,7},{7,8},{8,9},{9,10},{10,1... | collective-permute-start | bytes 98312 | tf_op jit(solution)/shard_map/ppermute | solution.py:592
  13.5 6.8 %collective-permute-start.3 = (f32[64,128]{1,0:T(8,128)S(1)}, f32[64,128]{1,0:T(8,128)S(1)}, u32[]{:S(2)}, u32[]{:S(2)}) collective-permute-start(f32[64,128]{1,0:T(8,128)S(1)} %get-tuple-element.25), channel_id=1, source_target_pairs={{0,15},{1,0},{2,1},{3,2},{4,3},{5,4},{6,5},{7,6},{8,7},{9,8},{10,9... | collective-permute-start | bytes 98312 | tf_op jit(solution)/shard_map/ppermute | solution.py:592
  40.1 4.3 %collective-permute-start.6 = (f32[8,384]{1,0:T(8,128)S(1)}, f32[8,384]{1,0:T(8,128)S(1)}, u32[]{:S(2)}, u32[]{:S(2)}) collective-permute-start(f32[8,384]{1,0:T(8,128)S(1)} %get-tuple-element.32.own_east), channel_id=1, source_target_pairs={{0,16},{16,32},{32,48},{48,64},{64,80},{80,96},{96,112},{112,0},{1... | collective-permute-start | bytes 36872 | tf_op jit(solution)/shard_map/ppermute | solution.py:592
  40.1 4.3 %collective-permute-start.7 = (f32[8,384]{1,0:T(8,128)S(1)}, f32[8,384]{1,0:T(8,128)S(1)}, u32[]{:S(2)}, u32[]{:S(2)}) collective-permute-start(f32[8,384]{1,0:T(8,128)S(1)} %get-tuple-element.33.own_west), channel_id=1, source_target_pairs={{0,112},{16,0},{32,16},{48,32},{64,48},{80,64},{96,80},{112,96},{1... | collective-permute-start | bytes 36872 | tf_op jit(solution)/shard_map/ppermute | solution.py:592
  43.1 10.9 %collective-permute-start.4 = (f32[2,40,128]{2,1,0:T(8,128)S(1)}, f32[2,40,128]{2,1,0:T(8,128)S(1)}, u32[]{:S(2)}, u32[]{:S(2)}) collective-permute-start(f32[2,40,128]{2,1,0:T(8,128)S(1)} %get-tuple-element.28), channel_id=1, source_target_pairs={{0,112},{16,0},{32,16},{48,32},{64,48},{80,64},{96,80},{112,96},{1... | collective-permute-start | bytes 122888 | tf_op jit(solution)/shard_map/ppermute | solution.py:592
  44.6 12.3 %collective-permute-start.8 = (f32[80,128]{1,0:T(8,128)S(1)}, f32[80,128]{1,0:T(8,128)S(1)}, u32[]{:S(2)}, u32[]{:S(2)}) collective-permute-start(f32[80,128]{1,0:T(8,128)S(1)} %get-tuple-element.37), channel_id=1, source_target_pairs={{0,1},{1,2},{2,3},{3,4},{4,5},{5,6},{6,7},{7,8},{8,9},{9,10},{10,1... | collective-permute-start | bytes 122888 | tf_op jit(solution)/shard_map/ppermute | solution.py:592
  44.7 12.3 %collective-permute-start.9 = (f32[80,128]{1,0:T(8,128)S(1)}, f32[80,128]{1,0:T(8,128)S(1)}, u32[]{:S(2)}, u32[]{:S(2)}) collective-permute-start(f32[80,128]{1,0:T(8,128)S(1)} %get-tuple-element.38), channel_id=1, source_target_pairs={{0,15},{1,0},{2,1},{3,2},{4,3},{5,4},{6,5},{7,6},{8,7},{9,8},{10,9... | collective-permute-start | bytes 122888 | tf_op jit(solution)/shard_map/ppermute | solution.py:592
  50.1 3.9 %collective-permute-start.5 = (f32[64,128]{1,0:T(8,128)S(1)}, f32[64,128]{1,0:T(8,128)S(1)}, u32[]{:S(2)}, u32[]{:S(2)}) collective-permute-start(f32[64,128]{1,0:T(8,128)S(1)} %get-tuple-element.29), channel_id=1, source_target_pairs={{0,15},{1,0},{2,1},{3,2},{4,3},{5,4},{6,5},{7,6},{8,7},{9,8},{10,9... | collective-permute-start | bytes 98312 | tf_op jit(solution)/shard_map/ppermute | solution.py:592

commit v2 on v1

v2 whole, which is shorter than its diff:
```python
import jax
import jax.numpy as jnp
from jax import lax
from jax.experimental import pallas as pl
from jax.experimental.pallas import tpu as pltpu
from jax.sharding import PartitionSpec as P

ITERS = 6
LIMIT_PACK = 40
LIMIT_INTERIOR = 40
LIMIT_COLUMNS = 24
LEVELS = 40
ROWS = 64
COLS = 256
BLOCKS = ROWS // 8
CHUNK = 8
CHUNKS = LEVELS // CHUNK

damping = 0.05
lower_bound = 0.02
upper_bound = 2.0
cheb_alpha = 2.0 / (upper_bound - lower_bound)
cheb_gamma = (upper_bound + lower_bound) / 2.0
advect_scale = 0.4
force_scale = 4.0
source_scale = 0.5
divergence_scale = 4.0
PRESS = force_scale / LEVELS
DIVERGE = divergence_scale / LEVELS

VMEM = pl.BlockSpec(memory_space=pltpu.VMEM)
ANY = pl.BlockSpec(memory_space=pl.ANY)
HBM = pl.BlockSpec(memory_space=pltpu.HBM)
F32 = jnp.float32
TILES = [(b, h) for b in range(BLOCKS) for h in range(2)]


def shape(*dims):
    return jax.ShapeDtypeStruct(dims, F32)


def params(mebibytes=40):
    return pltpu.CompilerParams(vmem_limit_bytes=int(mebibytes * 1024 * 1024))


def lane_id(rows=8):
    return lax.broadcasted_iota(jnp.int32, (rows, 128), 1)


def row_id():
    return lax.broadcasted_iota(jnp.int32, (8, 128), 0)


def rows_of(b):
    return slice(8 * b, 8 * b + 8)


def lanes_of(h):
    return slice(128 * h, 128 * h + 128)


def tiles_of(ref, *lead):
    return {(b, h): ref[(*lead, rows_of(b), lanes_of(h))] for b, h in TILES}


def next_row(x, after, last):
    turned = {t: pltpu.roll(x[t], 7, 0) for t in TILES}
    return {
        (b, h): jnp.where(last, after[h] if b == BLOCKS - 1 else turned[b + 1, h], turned[b, h])
        for b, h in TILES
    }


def prev_row(x, before, first):
    turned = {t: pltpu.roll(x[t], 1, 0) for t in TILES}
    return {
        (b, h): jnp.where(first, before[h] if b == 0 else turned[b - 1, h], turned[b, h])
        for b, h in TILES
    }


def next_col(x, after, last):
    turned = {t: pltpu.roll(x[t], 127, 1) for t in TILES}
    return {
        (b, h): jnp.where(last, after[b] if h == 1 else turned[b, 1], turned[b, h])
        for b, h in TILES
    }


def prev_col(x, before, first):
    turned = {t: pltpu.roll(x[t], 1, 1) for t in TILES}
    return {
        (b, h): jnp.where(first, before[b] if h == 0 else turned[b, 0], turned[b, h])
        for b, h in TILES
    }


def spread(ref, k, h):
    return jnp.broadcast_to(ref[h, pl.ds(k, 1), :], (8, 128))


def pack_kernel(
    temp, speeds, sea_in, tally_in,
    count_out, to_east, to_west, to_north, to_south,
    t_low, t_high, v_high, t_top, t_end, u_end, sea, tally, sems,
):
    copies = [
        pltpu.make_async_copy(sea_in, sea, sems.at[6]),
        pltpu.make_async_copy(tally_in, tally, sems.at[7]),
        pltpu.make_async_copy(temp.at[:, :, pl.ds(0, 128)], t_low, sems.at[0]),
        pltpu.make_async_copy(temp.at[:, :, pl.ds(128, 128)], t_high, sems.at[1]),
        pltpu.make_async_copy(speeds.at[1, :, :, pl.ds(128, 128)], v_high, sems.at[2]),
        pltpu.make_async_copy(temp.at[:, pl.ds(0, 8), :], t_top, sems.at[3]),
        pltpu.make_async_copy(temp.at[:, pl.ds(ROWS - 8, 8), :], t_end, sems.at[4]),
        pltpu.make_async_copy(speeds.at[0, :, pl.ds(ROWS - 8, 8), :], u_end, sems.at[5]),
    ]
    for copy in copies:
        copy.start()
    copies[0].wait()
    copies[1].wait()
    copies = copies[2:]
    latitude = lax.axis_index("gy") * COLS + lax.broadcasted_iota(jnp.int32, (ROWS, COLS), 1)
    inner = (latitude > 0) & (latitude < lax.axis_size("gy") * COLS - 1)
    count = jnp.where(inner & (sea[...] == 1), tally[...], 0).astype(F32)
    count_out[...] = count
    for h in range(2):
        to_east[h, 80:86, :] = count[ROWS - 6 :, lanes_of(h)]
        to_east[h, 86:88, :] = jnp.zeros((2, 128), F32)
        to_west[h, 40:46, :] = count[:6, lanes_of(h)]
        to_west[h, 46:48, :] = jnp.zeros((2, 128), F32)
    lane = lane_id(ROWS)

    def gather(ref, column, start, total):
        for k in range(LEVELS):
            total = jnp.where(
                lane == start + k, pltpu.roll(ref[k], (start + k - column) % 128, 1), total
            )
        return total

    copies[0].wait()
    to_south[...] = gather(
        t_low, 0, 0, pltpu.roll(count[:, :128], 40, 1)
    )
    copies[1].wait()
    total = gather(t_high, 127, 0, pltpu.roll(count[:, 128:], (80 - 127) % 128, 1))
    copies[2].wait()
    to_north[...] = gather(v_high, 127, 40, total)
    copies[3].wait()
    copies[4].wait()
    copies[5].wait()
    for h in range(2):
        to_west[h, 0:40, :] = t_top[:, 0, lanes_of(h)]
        to_east[h, 0:40, :] = t_end[:, 7, lanes_of(h)]
        to_east[h, 40:80, :] = u_end[:, 7, lanes_of(h)]


def pack(temp, speeds, sea, tally):
    return pl.pallas_call(
        pack_kernel,
        out_shape=(
            shape(ROWS, COLS), shape(2, 88, 128), shape(2, 48, 128), shape(ROWS, 128), shape(ROWS, 128)
        ),
        in_specs=[HBM, HBM, HBM, HBM],
        out_specs=(VMEM,) * 5,
        scratch_shapes=[
            pltpu.VMEM((LEVELS, ROWS, 128), F32),
            pltpu.VMEM((LEVELS, ROWS, 128), F32),
            pltpu.VMEM((LEVELS, ROWS, 128), F32),
            pltpu.VMEM((LEVELS, 8, COLS), F32),
            pltpu.VMEM((LEVELS, 8, COLS), F32),
            pltpu.VMEM((LEVELS, 8, COLS), F32),
            pltpu.VMEM((ROWS, COLS), jnp.int32),
            pltpu.VMEM((ROWS, COLS), jnp.int32),
            pltpu.SemaphoreType.DMA((8,)),
        ],
        compiler_params=params(LIMIT_PACK),
        name="pack",
    )(temp, speeds, sea, tally)


UNROLL_IN = 2
UNROLL_FWD = 2
UNROLL_BACK = 4
UNROLL_MOM = 4


def interior_kernel(
    temp, speeds, mix, count,
    source_out, inverse_out, link_out, u_out, v_out,
    tb, mb, east_lim, north_lim, sems,
):
    def load(which, c):
        part = pl.ds(c * CHUNK, CHUNK)
        origin, target = (
            (mix, mb), (temp, tb), (speeds.at[0], u_out), (speeds.at[1], v_out)
        )[which]
        return pltpu.make_async_copy(origin.at[part], target.at[part], sems.at[which, c])

    for c in range(CHUNKS):
        for which in range(4):
            load(which, c).start()

    lane, row = lane_id(), row_id()
    first_row, last_row = row == 0, row == 7
    first_lane, last_lane = lane == 0, lane == 127
    zero = jnp.zeros((8, 128), F32)
    pair = range(2)

    counts = tiles_of(count)
    ahead = next_row(counts, [zero, zero], last_row)
    for b, h in TILES:
        east_lim[rows_of(b), lanes_of(h)] = jnp.minimum(counts[b, h], ahead[b, h])
    ahead = next_col(counts, [zero] * BLOCKS, last_lane)
    for b, h in TILES:
        north_lim[rows_of(b), lanes_of(h)] = jnp.minimum(counts[b, h], ahead[b, h])

    def level_step(k, factors, links):
        level = k.astype(F32)
        below_at = jnp.minimum(k + 1, LEVELS - 1)
        t_next = [tb[k, rows_of(0), lanes_of(h)] for h in pair]
        turned_next = [pltpu.roll(t_next[h], 7, 0) for h in pair]
        flux_turned = [zero, zero]
        new_factors, new_links = [], []
        for b in range(BLOCKS):
            rows = rows_of(b)
            t, turned = t_next, turned_next
            if b < BLOCKS - 1:
                t_next = [tb[k, rows_of(b + 1), lanes_of(h)] for h in pair]
                turned_next = [pltpu.roll(t_next[h], 7, 0) for h in pair]
            u = [u_out[k, rows, lanes_of(h)] for h in pair]
            v = [v_out[k, rows, lanes_of(h)] for h in pair]
            change = []
            for h in pair:
                ahead = jnp.where(last_row, turned_next[h], turned[h])
                flux = jnp.where(level < east_lim[rows, lanes_of(h)], u[h], 0.0) * jnp.where(
                    u[h] > 0.0, t[h], ahead
                )
                flux_before, flux_turned[h] = flux_turned[h], pltpu.roll(flux, 1, 0)
                change.append(flux - jnp.where(first_row, flux_before, flux_turned[h]))
            left = [pltpu.roll(t[h], 127, 1) for h in pair]
            ahead = [jnp.where(last_lane, left[1], left[0]), left[1]]
            flux = [
                jnp.where(level < north_lim[rows, lanes_of(h)], v[h], 0.0)
                * jnp.where(v[h] > 0.0, t[h], ahead[h])
                for h in pair
            ]
            right = [pltpu.roll(flux[h], 1, 1) for h in pair]
            behind = [jnp.where(first_lane, 0.0, right[0]), jnp.where(first_lane, right[0], right[1])]
            for h in pair:
                n = 2 * b + h
                at = (k, rows, lanes_of(h))
                wet = count[rows, lanes_of(h)]
                total = change[h] + (flux[h] - behind[h])
                source_out[at] = t[h] - jnp.where(level < wet, advect_scale * total, 0.0)
                a = links[n]
                below = jnp.where(
                    level + 1.0 < wet, mb[below_at, rows, lanes_of(h)], 0.0
                )
                pivot = (1.0 + below) + (a - a * factors[n])
                inverse = pl.reciprocal(pivot, approx=True)
                inverse = inverse * (2.0 - pivot * inverse)
                inverse_out[at] = inverse
                link_out[at] = a
                new_factors.append(below * inverse)
                new_links.append(below)
        return tuple(new_factors), tuple(new_links)

    load(0, 0).wait()

    def chunk_step(c, carry):
        @pl.when(c < CHUNKS - 1)
        def _():
            load(0, c + 1).wait()

        for which in range(1, 4):
            load(which, c).wait()

        def step(m, carry):
            for n in range(UNROLL_IN):
                carry = level_step(c * CHUNK + m * UNROLL_IN + n, *carry)
            return carry

        return lax.fori_loop(0, CHUNK // UNROLL_IN, step, carry)

    blank = tuple(zero for _ in TILES)
    lax.fori_loop(0, CHUNKS, chunk_step, (blank, blank))


def interior(temp, speeds, mix, count):
    block = shape(LEVELS, ROWS, COLS)
    scratch = pltpu.VMEM((LEVELS, ROWS, COLS), F32)
    return pl.pallas_call(
        interior_kernel,
        out_shape=(block,) * 5,
        in_specs=[ANY, ANY, ANY, VMEM],
        out_specs=(VMEM,) * 5,
        scratch_shapes=[
            scratch, scratch,
            pltpu.VMEM((ROWS, COLS), F32), pltpu.VMEM((ROWS, COLS), F32),
            pltpu.SemaphoreType.DMA((4, CHUNKS)),
        ],
        cost_estimate=pl.CostEstimate(
            flops=30 * LEVELS * ROWS * COLS, bytes_accessed=16 * LEVELS * ROWS * COLS,
            transcendentals=0,
        ),
        compiler_params=params(LIMIT_INTERIOR),
        name="interior",
    )(temp, speeds, mix, count)


def column_kernel(
    source, inverse, link, u_in, v_in, count, rain, own_east, own_west, own_north, own_south,
    west, east, south, north,
    temp_out, speeds_out, force_out, to_east, to_west, q_col, sides, u_end, v_high,
    solved, u_new, v_low, row_low, row_high, col_low, col_high,
    east_lim, north_lim, south_lim, west_lim, run, u_sum, v_sum, out_sems,
):
    def store(which, c):
        part = pl.ds(c * CHUNK, CHUNK)
        origin, target = (
            (solved.at[part], temp_out.at[part]),
            (u_new.at[part], speeds_out.at[0, part, pl.ds(0, ROWS - 8), :]),
            (v_low.at[part], speeds_out.at[1, part, :, pl.ds(0, 128)]),
        )[which]
        return pltpu.make_async_copy(origin, target, out_sems.at[which, c])

    lane, row = lane_id(), row_id()
    first_row, last_row = row == 0, row == 7
    first_lane, last_lane = lane == 0, lane == 127
    zero = jnp.zeros((8, 128), F32)
    pair = range(2)

    counts = tiles_of(count)
    after = [jnp.broadcast_to(east[h, 40:41, :], (8, 128)) for h in pair]
    before = [jnp.broadcast_to(west[h, 85:86, :], (8, 128)) for h in pair]
    ahead = next_row(counts, after, last_row)
    for b, h in TILES:
        east_lim[rows_of(b), lanes_of(h)] = jnp.minimum(counts[b, h], ahead[b, h])
    for h in pair:
        west_lim[:, lanes_of(h)] = jnp.minimum(counts[0, h], before[h])
    after = [pltpu.roll(north[rows_of(b), :], 127 - 40, 1) for b in range(BLOCKS)]
    ahead = next_col(counts, after, last_lane)
    for b, h in TILES:
        north_lim[rows_of(b), lanes_of(h)] = jnp.minimum(counts[b, h], ahead[b, h])
    for b in range(BLOCKS):
        south_lim[rows_of(b), :] = jnp.minimum(
            counts[b, 0], pltpu.roll(south[rows_of(b), :], 128 - 80, 1)
        )

    depth = lax.broadcasted_iota(jnp.int32, (LEVELS, 128), 0).astype(F32)
    for h in pair:
        speed = west[h, 40:80, :]
        row_low[h] = (
            advect_scale
            * jnp.where(depth < west_lim[0:1, lanes_of(h)], speed, 0.0)
            * jnp.where(speed > 0.0, west[h, 0:40, :], own_west[h, 0:40, :])
        )
        speed = own_east[h, 40:80, :]
        row_high[h] = (
            -advect_scale
            * jnp.where(depth < east_lim[ROWS - 1 : ROWS, lanes_of(h)], speed, 0.0)
            * jnp.where(speed > 0.0, own_east[h, 0:40, :], east[h, 0:40, :])
        )
    depth = lane.astype(F32)
    for b in range(BLOCKS):
        rows = rows_of(b)
        limit = jnp.broadcast_to(south_lim[rows, 0:1], (8, 128))
        speed = pltpu.roll(south[rows, :], 128 - 40, 1)
        col_low[rows, :] = (
            advect_scale
            * jnp.where(depth < limit, speed, 0.0)
            * jnp.where(speed > 0.0, south[rows, :], own_south[rows, :])
        )
        limit = jnp.broadcast_to(north_lim[rows, COLS - 1 : COLS], (8, 128))
        speed = pltpu.roll(own_north[rows, :], 128 - 40, 1)
        col_high[rows, :] = (
            -advect_scale
            * jnp.where(depth < limit, speed, 0.0)
            * jnp.where(speed > 0.0, own_north[rows, :], north[rows, :])
        )

    def forward(k, values):
        out = []
        low = [jnp.where(first_row, spread(row_low, k, h), 0.0) for h in pair]
        high = [jnp.where(last_row, spread(row_high, k, h), 0.0) for h in pair]
        for b in range(BLOCKS):
            rows = rows_of(b)
            add = [
                jnp.where(first_lane, pltpu.roll(col_low[rows, :], 128 - k, 1), 0.0),
                jnp.where(last_lane, pltpu.roll(col_high[rows, :], 127 - k, 1), 0.0),
            ]
            for h in pair:
                at = (k, rows, lanes_of(h))
                total = source[at] + add[h]
                if b == 0:
                    total = total + low[h]
                if b == BLOCKS - 1:
                    total = total + high[h]
                value = (total + link[at] * values[2 * b + h]) * inverse[at]
                solved[at] = value
                out.append(value)
        return tuple(out)

    blank = tuple(zero for _ in TILES)

    def forward_step(m, values):
        for n in range(UNROLL_FWD):
            values = forward(m * UNROLL_FWD + n, values)
        return values

    lax.fori_loop(0, LEVELS // UNROLL_FWD, forward_step, blank)

    def back_chunk(c_up, linked):
        c = CHUNKS - 1 - c_up

        def step(m, linked):
            for n in range(UNROLL_BACK):
                k = c * CHUNK + (CHUNK - 1 - m * UNROLL_BACK - n)
                out = []
                for i, below in zip(TILES, linked):
                    at = (k, rows_of(i[0]), lanes_of(i[1]))
                    value = solved[at] + inverse[at] * below
                    solved[at] = value
                    out.append(link[at] * value)
                linked = tuple(out)
            return linked

        linked = lax.fori_loop(0, CHUNK // UNROLL_BACK, step, linked)
        store(0, c).start()
        return linked

    lax.fori_loop(0, CHUNKS, back_chunk, blank)

    run[...] = jnp.zeros_like(run)
    u_sum[...] = jnp.zeros_like(u_sum)
    v_sum[...] = jnp.zeros_like(v_sum)
    q_col[...] = jnp.zeros_like(q_col)
    many = range(UNROLL_MOM)

    def momentum(m, _):
        first = m * UNROLL_MOM
        levels = [first + n for n in many]
        depths = [k.astype(F32) for k in levels]

        def running(b):
            out = []
            for h in pair:
                at = (rows_of(b), lanes_of(h))
                total = run[at]
                qs = []
                for k in levels:
                    half = 0.5 * solved[(k, *at)]
                    qs.append(total + half)
                    total = qs[-1] + half
                run[at] = total
                out.append(qs)
            return out

        q_next = running(0)
        turned_next = [[pltpu.roll(q, 7, 0) for q in q_next[h]] for h in pair]
        for h in pair:
            for n in many:
                to_west[pl.ds(24 + 40 * h + levels[n], 1), :] = q_next[h][n][0:1]
        for b in range(BLOCKS):
            rows = rows_of(b)
            q, turned = q_next, turned_next
            if b < BLOCKS - 1:
                q_next = running(b + 1)
                turned_next = [[pltpu.roll(x, 7, 0) for x in q_next[h]] for h in pair]
            else:
                turned_next = [[zero] * UNROLL_MOM] * 2
            left = [[pltpu.roll(x, 127, 1) for x in q[h]] for h in pair]
            column = q_col[rows, :]
            for n in many:
                column = jnp.where(lane == levels[n], pltpu.roll(q[0][n], levels[n], 1), column)
            q_col[rows, :] = column
            for h in pair:
                at = (rows, lanes_of(h))
                limit = east_lim[at]
                total = u_sum[at]
                for n in many:
                    ahead = jnp.where(last_row, turned_next[h][n], turned[h][n])
                    speed = jnp.where(
                        depths[n] < limit, u_in[(levels[n], *at)] - PRESS * (q[h][n] - ahead), 0.0
                    )
                    if b < BLOCKS - 1:
                        u_new[(levels[n], *at)] = speed
                    else:
                        u_end[levels[n], :, lanes_of(h)] = speed
                    total = total + speed
                u_sum[at] = total
                limit = north_lim[at]
                total = v_sum[at]
                for n in many:
                    ahead = jnp.where(last_lane, left[1][n] if h == 0 else 0.0, left[h][n])
                    speed = jnp.where(
                        depths[n] < limit, v_in[(levels[n], *at)] - PRESS * (q[h][n] - ahead), 0.0
                    )
                    if h == 0:
                        v_low[levels[n], rows, :] = speed
                    else:
                        v_high[levels[n], rows, :] = speed
                    total = total + speed
                v_sum[at] = total
        return 0

    def momentum_chunk(c, _):
        per = CHUNK // UNROLL_MOM
        lax.fori_loop(c * per, (c + 1) * per, momentum, 0)
        store(1, c).start()
        store(2, c).start()
        return 0

    lax.fori_loop(0, CHUNKS, momentum_chunk, 0)

    depth = lax.broadcasted_iota(jnp.int32, (LEVELS, 128), 0).astype(F32)
    row_sum = []
    for h in pair:
        part = jnp.where(
            depth < west_lim[0:1, lanes_of(h)], PRESS * to_west[24 + 40 * h : 64 + 40 * h, :], 0.0
        )
        row_sum.append(
            jnp.broadcast_to(jnp.sum(part, axis=0, keepdims=True), (8, 128))
        )
    depth = lane.astype(F32)
    col_sum = []
    for b in range(BLOCKS):
        rows = rows_of(b)
        limit = jnp.broadcast_to(south_lim[rows, 0:1], (8, 128))
        part = jnp.where(depth < limit, PRESS * q_col[rows, :], 0.0)
        col_sum.append(jnp.broadcast_to(jnp.sum(part, axis=1, keepdims=True), (8, 128)))

    east_sum, north_sum = tiles_of(u_sum), tiles_of(v_sum)
    east_before = prev_row(east_sum, row_sum, first_row)
    north_before = prev_col(north_sum, col_sum, first_lane)
    for i in TILES:
        at = (rows_of(i[0]), lanes_of(i[1]))
        divergence = (east_sum[i] - east_before[i]) + (north_sum[i] - north_before[i])
        force_out[at] = jnp.where(
            count[at] > 0.0, source_scale * rain[at] - DIVERGE * divergence, 0.0
        )
    for b in range(BLOCKS):
        sides[rows_of(b), :] = jnp.where(
            first_lane,
            pltpu.roll(north_sum[b, 1], 1, 1),
            jnp.where(last_lane, col_sum[b], 0.0),
        )
    for h in pair:
        to_east[rows_of(h), :] = pltpu.roll(force_out[ROWS - 8 : ROWS, lanes_of(h)], 5, 0)
        to_east[8 * h + 5 : 8 * h + 6, :] = east_sum[BLOCKS - 1, h][7:8]
        to_west[rows_of(h), :] = force_out[0:8, lanes_of(h)]
        to_west[8 * h + 5 : 8 * h + 6, :] = row_sum[h][0:1]
    to_east[16:24, :] = pltpu.roll(sides[ROWS - 8 : ROWS, :], 5, 0)
    to_west[16:24, :] = sides[0:8, :]

    for c in range(CHUNKS):
        for which in range(3):
            store(which, c).wait()


def columns(*args):
    return pl.pallas_call(
        column_kernel,
        out_shape=(
            shape(LEVELS, ROWS, COLS), shape(2, LEVELS, ROWS, COLS), shape(ROWS, COLS),
            shape(24, 128), shape(104, 128), shape(ROWS, 128), shape(ROWS, 128),
            shape(LEVELS, 8, COLS), shape(LEVELS, ROWS, 128),
        ),
        in_specs=[VMEM] * 15,
        out_specs=(ANY, ANY) + (VMEM,) * 7,
        scratch_shapes=[
            pltpu.VMEM((LEVELS, ROWS, COLS), F32),
            pltpu.VMEM((LEVELS, ROWS - 8, COLS), F32),
            pltpu.VMEM((LEVELS, ROWS, 128), F32),
            pltpu.VMEM((2, LEVELS, 128), F32), pltpu.VMEM((2, LEVELS, 128), F32),
            pltpu.VMEM((ROWS, 128), F32), pltpu.VMEM((ROWS, 128), F32),
            pltpu.VMEM((ROWS, COLS), F32), pltpu.VMEM((ROWS, COLS), F32),
            pltpu.VMEM((ROWS, 128), F32), pltpu.VMEM((8, COLS), F32),
            pltpu.VMEM((ROWS, COLS), F32), pltpu.VMEM((ROWS, COLS), F32),
            pltpu.VMEM((ROWS, COLS), F32),
            pltpu.SemaphoreType.DMA((3, CHUNKS)),
        ],
        compiler_params=params(LIMIT_COLUMNS),
        name="columns",
    )(*args)


EXT = ROWS + 16


def edges_kernel(
    force, sides, q_col, count, west, east_in, own_east, own_west, from_west, from_east,
    force_ext, count_ext, sides_ext, to_north, to_south,
):
    zeros8 = jnp.zeros((8, COLS), F32)
    count_ext[0:8, :] = zeros8
    for h in range(2):
        count_ext[2:8, lanes_of(h)] = west[h, 80:86, :]
    count_ext[8 : 8 + ROWS, :] = count[...]
    count_ext[8 + ROWS :, :] = zeros8
    for h in range(2):
        count_ext[8 + ROWS : 14 + ROWS, lanes_of(h)] = east_in[h, 40:46, :]
    sides_ext[0:8, :] = jnp.zeros((8, 128), F32)
    sides_ext[3:8, :] = from_west[16:21, :]
    sides_ext[8 : 8 + ROWS, :] = sides[...]
    sides_ext[8 + ROWS :, :] = jnp.zeros((8, 128), F32)
    sides_ext[8 + ROWS : 13 + ROWS, :] = from_east[16:21, :]
    force_ext[0:8, :] = zeros8
    for h in range(2):
        force_ext[3:8, lanes_of(h)] = from_west[8 * h : 8 * h + 5, :]
    force_ext[8 : 8 + ROWS, :] = force[...]
    force_ext[8 + ROWS :, :] = zeros8
    for h in range(2):
        force_ext[8 + ROWS : 13 + ROWS, lanes_of(h)] = from_east[8 * h : 8 * h + 5, :]

    def add(at, sign, ref):
        for h in range(2):
            place = (slice(at, at + 1), lanes_of(h))
            force_ext[place] = force_ext[place] + jnp.where(
                count_ext[place] > 0.0, sign * DIVERGE * ref[8 * h + 5 : 8 * h + 6, :], 0.0
            )

    add(7, -1.0, own_west)
    add(8, 1.0, from_west)
    add(7 + ROWS, -1.0, from_east)
    add(8 + ROWS, 1.0, own_east)
    lane = lane_id(EXT)
    side = sides_ext[...]
    to_north[...] = jnp.where(
        lane >= 123,
        force_ext[:, 128:],
        jnp.where(lane == 0, side, pltpu.roll(count_ext[:, 128:], 122, 1)),
    )
    to_south[...] = jnp.where(
        lane < 5,
        force_ext[:, :128],
        jnp.where(lane == 127, side, pltpu.roll(count_ext[:, :128], 8, 1)),
    )
    lane = lane_id(ROWS)
    to_south[8 : 8 + ROWS, :] = jnp.where(
        (lane >= 64) & (lane < 64 + LEVELS),
        pltpu.roll(q_col[...], 64, 1),
        to_south[8 : 8 + ROWS, :],
    )


def edges(*args):
    return pl.pallas_call(
        edges_kernel,
        out_shape=(
            shape(EXT, COLS), shape(EXT, COLS), shape(EXT, 128), shape(EXT, 128), shape(EXT, 128)
        ),
        in_specs=[VMEM] * 10,
        out_specs=(VMEM,) * 5,
        compiler_params=params(LIMIT_COLUMNS),
        name="edges",
    )(*args)


def final_kernel(
    speeds, u_end, v_high, from_east, count, east,
    force_ext, count_ext, sides_ext, south, north,
    speeds_out, out, u_fix, v_fix, sems,
):
    last_row = row_id() == 7
    for h in range(2):
        limit = jnp.minimum(
            count[ROWS - 8 :, lanes_of(h)], jnp.broadcast_to(east[h, 40:41, :], (8, 128))
        )
        limit = jnp.where(last_row, limit, 0.0)
        for k in range(LEVELS):
            at = 24 + 40 * h + k
            u_fix[k, :, lanes_of(h)] = u_end[k, :, lanes_of(h)] + jnp.where(
                float(k) < limit,
                PRESS * jnp.broadcast_to(from_east[at : at + 1, :], (8, 128)),
                0.0,
            )
    save_rows = pltpu.make_async_copy(
        u_fix, speeds_out.at[0, :, pl.ds(ROWS - 8, 8), :], sems.at[0]
    )
    save_rows.start()
    last_lane = lane_id(8) == 127
    for b in range(BLOCKS):
        rows = rows_of(b)
        held = north[8 * b + 8 : 8 * b + 16, :]
        limit = jnp.minimum(count[rows, 128:], pltpu.roll(held, 127 - 8, 1))
        limit = jnp.where(last_lane, limit, 0.0)
        for k in range(LEVELS):
            v_fix[k, rows, :] = v_high[k, rows, :] + jnp.where(
                float(k) < limit, PRESS * pltpu.roll(held, 63 - k, 1), 0.0
            )
    save_cols = pltpu.make_async_copy(
        v_fix, speeds_out.at[1, :, :, pl.ds(128, 128)], sems.at[1]
    )
    save_cols.start()
    lane = lane_id(EXT)
    count_side = jnp.where(
        lane >= 122,
        pltpu.roll(south[...], 6, 1),
        jnp.where(lane < 6, pltpu.roll(north[...], 120, 1), 0.0),
    )
    force_side = jnp.where(
        lane >= 123, south[...], jnp.where(lane < 5, north[...], 0.0)
    )
    side = sides_ext[...]
    low, high = force_ext[:, :128], force_ext[:, 128:]
    low = low + jnp.where(
        (lane == 0) & (count_ext[:, :128] > 0.0), DIVERGE * south[...], 0.0
    )
    high = high - jnp.where(
        (lane == 127) & (count_ext[:, 128:] > 0.0), DIVERGE * north[...], 0.0
    )
    force_side = force_side + jnp.where(
        (lane == 0) & (count_side > 0.0), DIVERGE * side, 0.0
    )
    force_side = force_side - jnp.where(
        (lane == 127) & (count_side > 0.0), DIVERGE * side, 0.0
    )
    force = jnp.concatenate([low, high, force_side], axis=1)
    count = jnp.concatenate([count_ext[...], count_side], axis=1)
    root = jnp.sqrt(count * (1.0 / LEVELS))
    wide = COLS + 128

    def total(field):
        sideways = pltpu.roll(field, 1, 1) + pltpu.roll(field, wide - 1, 1)
        mixed = field + 0.5 * sideways
        return sideways + (pltpu.roll(mixed, 1, 0) + pltpu.roll(mixed, EXT - 1, 0))

    diag = damping + root * total(root)
    inverse = 1.0 / diag
    update = inverse * force * (1.0 / cheb_gamma)
    iterate = update
    omega = 2.0 / cheb_gamma
    for step in range(1, ITERS):
        residual = force - (diag * iterate - root * total(root * iterate))
        omega = 1.0 / (cheb_gamma - omega / (4.0 * cheb_alpha * cheb_alpha))
        update = omega * inverse * residual + (cheb_gamma * omega - 1.0) * update
        iterate = iterate + update
    out[...] = iterate[8 : 8 + ROWS, 0:COLS]
    save_rows.wait()
    save_cols.wait()


def final(*args):
    return pl.pallas_call(
        final_kernel,
        out_shape=(shape(2, LEVELS, ROWS, COLS), shape(ROWS, COLS)),
        in_specs=[ANY] + [VMEM] * 10,
        out_specs=(ANY, VMEM),
        scratch_shapes=[
            pltpu.VMEM((LEVELS, 8, COLS), F32),
            pltpu.VMEM((LEVELS, ROWS, 128), F32),
            pltpu.SemaphoreType.DMA((2,)),
        ],
        input_output_aliases={0: 0},
        compiler_params=params(LIMIT_COLUMNS),
        name="final",
    )(*args)


def shift(array, axis, step):
    count = lax.axis_size(axis)
    return lax.ppermute(array, axis, [(i, (i + step) % count) for i in range(count)])


def local(
    thermal_departure,
    current_speeds,
    mixing_coefficient,
    seawater_indicator,
    submerged_layer_tally,
    rainfall_runoff_input,
):
    count, to_east, to_west, to_north, to_south = pack(
        *(
            pltpu.with_memory_space_constraint(x, pltpu.HBM)
            for x in (
                thermal_departure, current_speeds, seawater_indicator, submerged_layer_tally
            )
        )
    )
    south = shift(to_north, "gy", 1)
    north = shift(to_south, "gy", -1)
    west = shift(to_east, "gx", 1)
    east = shift(to_west, "gx", -1)
    inside = interior(thermal_departure, current_speeds, mixing_coefficient, count)
    temp_next, speeds, force, own_east, own_west, q_col, sides, u_end, v_high = columns(
        *inside, count, rainfall_runoff_input, to_east, to_west, to_north, to_south,
        west, east, south, north,
    )
    from_west = shift(own_east, "gx", 1)
    from_east = shift(own_west, "gx", -1)
    force_ext, count_ext, sides_ext, north_edge, south_edge = edges(
        force, sides, q_col, count, west, east, own_east, own_west, from_west, from_east
    )
    from_south = shift(north_edge, "gy", 1)
    from_north = shift(south_edge, "gy", -1)
    velocity_next, surface = final(
        speeds, u_end, v_high, from_east, count, east,
        force_ext, count_ext, sides_ext, from_south, from_north,
    )
    return (temp_next, velocity_next, surface)


def solution(mesh):
    placed = (
        P(None, "gx", "gy"),
        P(None, None, "gx", "gy"),
        P(None, "gx", "gy"),
        P("gx", "gy"),
        P("gx", "gy"),
        P("gx", "gy"),
    )
    return jax.shard_map(
        local,
        mesh=mesh,
        in_specs=placed,
        out_specs=(P(None, "gx", "gy"), P(None, None, "gx", "gy"), P("gx", "gy")),
        check_vma=False,
    )
```

time: 59 us -> 40.6 us (0.69)
  Pallas kernels: 26.7 us -> 18.5 us
  local copies, waits for them, and re-layouts: 5.91 us -> 0.01 us
  starting transfers between devices: 19.9 us -> 15.5 us
  waiting for transfers between devices: 5.24 us -> 5.84 us
    pallas_call x1, Pallas kernels: 19.7 us -> 5.8 us  [columns(): pl.pallas_call(column_kernel, out_shape=(shape(LEVELS, ROWS, COLS), shape...]
    unnamed x14 -> x2, local copies, waits for them, and re-layouts: 5.91 us -> 0.01 us
    pallas_call x2, Pallas kernels: 4.65 us -> 9.83 us  [the longest x1 6.53 us: interior(): pl.pallas_call(interior_kernel, out_shape=(block,) * 5, in_specs=[ANY, AN...]
    ppermute x10 -> x8, starting transfers between devices: 19.9 us -> 15.5 us  [shift(): lax.ppermute(array, axis, [(i, (i + step) % count) for i in range(count)])]
    ppermute x10 -> x8, waiting for transfers between devices: 5.24 us -> 5.84 us  [shift(): lax.ppermute(array, axis, [(i, (i + step) % count) for i in range(count)])]
  transfers between devices with their start and end apart: 10 -> 8, of which waited for: 3 -> 2; matrix products, arithmetic and copies ran while one was open for 0% -> 0% of each run, Pallas kernels for 5% -> 16%
where the time goes in v2:
time: 40.6 us; the launch traced here: 40.5 us
  Pallas kernels  18.5 us (46%)
  starting transfers between devices  15.5 us (38%)
  waiting for transfers between devices  5.84 us (14%)
  between operations  0.73 us (2%)
    ppermute x8, starting transfers between devices, shift(): lax.ppermute(array, axis, [(i, (i + step) % count) for i in range(count)])  15.5 us
    pallas_call x1, Pallas kernels, interior(): pl.pallas_call(interior_kernel, out_shape=(block,) * 5, in_specs=[ANY, AN...  6.53 us
    ppermute x8, waiting for transfers between devices, shift(): lax.ppermute(array, axis, [(i, (i + step) % count) for i in range(count)])  5.84 us
    pallas_call x1, Pallas kernels, columns(): pl.pallas_call(column_kernel, out_shape=(shape(LEVELS, ROWS, COLS), shape...  5.8 us
    pallas_call x1, Pallas kernels, final(): pl.pallas_call(final_kernel, out_shape=(shape(2, LEVELS, ROWS, COLS), sha...  3.3 us
    pallas_call x1, Pallas kernels, pack(): pl.pallas_call(pack_kernel, out_shape=(shape(ROWS, COLS), shape(2, 88, 12...  2.78 us
  transfers between devices with their start and end apart: 8, of which 2 were waited for; matrix products, arithmetic and copies ran while one was open for 0% of the time, Pallas kernels for 16%

profile of v2, /device:TPU:0, one launch (start us, length us, event | category | flops | bytes accessed | tf_op | source)
XLA Modules:
  0.0 40.5 jit_solution(10630239736117765693)
XLA Ops:
  0.6 2.8 %pack.1 = (f32[64,256]{1,0:T(8,128)S(1)}, f32[2,88,128]{2,1,0:T(8,128)S(1)}, f32[2,48,128]{2,1,0:T(8,128)S(1)}, f32[64,128]{1,0:T(8,128)S(1)}, f32[64,128]{1,0:T(8,128)S(1)}) custom-call(f32[40,64,256]{2,1,0:T(8,128)} %temp.3, f32[2,40,64,256]{3,2,1,0:T(8,128)} %speeds.3, s32[64,256]{1,0:T(8,128)} %sea_in.1, s32[64,256]{1,0:T(8,128)} %tally_in.1), custom_call_target="tpu_custom_call" | custom-call | tf_op jit(solution)/shard_map/pack/pallas_call | solution.py:158
  3.4 0.0 collective-permute-start
  3.4 2.9 %collective-permute-start.1 = (f32[2,48,128]{2,1,0:T(8,128)S(1)}, f32[2,48,128]{2,1,0:T(8,128)S(1)}, u32[]{:S(2)}, u32[]{:S(2)}) collective-permute-start(f32[2,48,128]{2,1,0:T(8,128)S(1)} %get-tuple-element.36.own_west), channel_id=1, source_target_pairs={{0,112},{16,0},{32,16},{48,32},{64,48},{80,64},{96,80},{112,96},{1... | collective-permute-start | bytes 147464 | tf_op jit(solution)/shard_map/ppermute | solution.py:763
  6.4 1.7 %collective-permute-start.2 = (f32[64,128]{1,0:T(8,128)S(1)}, f32[64,128]{1,0:T(8,128)S(1)}, u32[]{:S(2)}, u32[]{:S(2)}) collective-permute-start(f32[64,128]{1,0:T(8,128)S(1)} %get-tuple-element.37.own_north), channel_id=1, source_target_pairs={{0,1},{1,2},{2,3},{3,4},{4,5},{5,6},{6,7},{7,8},{8,9},{9,10},{10,1... | collective-permute-start | bytes 98312 | tf_op jit(solution)/shard_map/ppermute | solution.py:763
  8.0 4.9 %collective-permute-start.3 = (f32[64,128]{1,0:T(8,128)S(1)}, f32[64,128]{1,0:T(8,128)S(1)}, u32[]{:S(2)}, u32[]{:S(2)}) collective-permute-start(f32[64,128]{1,0:T(8,128)S(1)} %get-tuple-element.38.own_south), channel_id=1, source_target_pairs={{0,15},{1,0},{2,1},{3,2},{4,3},{5,4},{6,5},{7,6},{8,7},{9,8},{10,9... | collective-permute-start | bytes 98312 | tf_op jit(solution)/shard_map/ppermute | solution.py:763
  13.0 0.0 copy-start
  13.0 6.5 %interior.1 = (f32[40,64,256]{2,1,0:T(8,128)S(1)}, f32[40,64,256]{2,1,0:T(8,128)S(1)}, f32[40,64,256]{2,1,0:T(8,128)S(1)}, f32[40,64,256]{2,1,0:T(8,128)S(1)}, f32[40,64,256]{2,1,0:T(8,128)S(1)}) custom-call(f32[40,64,256]{2,1,0:T(8,128)} %temp.3, f32[2,40,64,256]{3,2,1,0:T(8,128)} %speeds.3, f32[40,64,256]{2,1,0:T(8,128)} %mix.1, ...), custom_call_target="tpu_custom_call" | custom-call | flops 19660800 | bytes 10485760 | tf_op jit(solution)/shard_map/interior/pallas_call | solution.py:292
  19.5 0.0 collective-permute-done.2.south
  19.5 0.0 collective-permute-done.3.north
  19.5 0.0 collective-permute-done.1.east.east_in
  19.5 0.0 collective-permute-done.west
  19.5 0.0 copy-done
  19.6 5.8 %columns.1 = (f32[40,64,256]{2,1,0:T(8,128)}, f32[2,40,64,256]{3,2,1,0:T(8,128)}, f32[64,256]{1,0:T(8,128)S(1)}, f32[24,128]{1,0:T(8,128)S(1)}, f32[104,128]{1,0...) custom-call(f32[40,64,256]{2,1,0:T(8,128)S(1)} %get-tuple-element.30, ...), custom_call_target="tpu_custom_call" | custom-call | tf_op jit(solution)/shard_map/columns/pallas_call | solution.py:562
  25.4 0.0 collective-permute-start.4
  25.4 0.5 %collective-permute-start.5 = (f32[24,128]{1,0:T(8,128)S(1)}, f32[24,128]{1,0:T(8,128)S(1)}, u32[]{:S(2)}, u32[]{:S(2)}) collective-permute-start(f32[24,128]{1,0:T(8,128)S(1)} %get-tuple-element.47.own_east), channel_id=1, source_target_pairs={{0,16},{16,32},{32,48},{48,64},{64,80},{80,96},{96,112},{112,0},{1... | collective-permute-start | bytes 36872 | tf_op jit(solution)/shard_map/ppermute | solution.py:763
  25.9 3.8 %collective-permute-done.5.from_west = f32[24,128]{1,0:T(8,128)S(1)} collective-permute-done((f32[24,128]{1,0:T(8,128)S(1)}, f32[24,128]{1,0:T(8,128)S(1)}, u32[]{:S(2)}, u32[]{:S(2)}) %collective-permute-start.5) | collective-permute-done | bytes 12320 | tf_op jit(solution)/shard_map/ppermute | solution.py:763
  29.7 0.0 collective-permute-done.4.from_east
  29.7 0.1 edges.1
  29.8 0.1 collective-permute-start.6
  29.9 5.3 %collective-permute-start.7 = (f32[80,128]{1,0:T(8,128)S(1)}, f32[80,128]{1,0:T(8,128)S(1)}, u32[]{:S(2)}, u32[]{:S(2)}) collective-permute-start(f32[80,128]{1,0:T(8,128)S(1)} %get-tuple-element.52), channel_id=1, source_target_pairs={{0,15},{1,0},{2,1},{3,2},{4,3},{5,4},{6,5},{7,6},{8,7},{9,8},{10,9... | collective-permute-start | bytes 122888 | tf_op jit(solution)/shard_map/ppermute | solution.py:763
  35.3 2.0 %collective-permute-done.6.south = f32[80,128]{1,0:T(8,128)S(1)} collective-permute-done((f32[80,128]{1,0:T(8,128)S(1)}, f32[80,128]{1,0:T(8,128)S(1)}, u32[]{:S(2)}, u32[]{:S(2)}) %collective-permute-start.6) | collective-permute-done | bytes 40992 | tf_op jit(solution)/shard_map/ppermute | solution.py:763
  37.2 0.0 collective-permute-done.7.north
  37.2 3.3 %final.1 = (f32[2,40,64,256]{3,2,1,0:T(8,128)}, f32[64,256]{1,0:T(8,128)}) custom-call(f32[2,40,64,256]{3,2,1,0:T(8,128)} %get-tuple-element.40.speeds, f32[40,8,256]{2,1,0:T(8,128)S(1)} %get-tuple-element.41.u_end, f32[40,64,128]{2,1,0:T(8,128)S(1)} %get-tuple-element.42.v_high, ...), custom_call_target="tpu_custom_call", output_to_operand_aliasing={{0}: (0, {})} | custom-call | tf_op jit(solution)/shard_map/final/pallas_call | solution.py:745
Async XLA Ops:
  3.4 16.1 %collective-permute-start = (f32[2,88,128]{2,1,0:T(8,128)S(1)}, f32[2,88,128]{2,1,0:T(8,128)S(1)}, u32[]{:S(2)}, u32[]{:S(2)}) collective-permute-start(f32[2,88,128]{2,1,0:T(8,128)S(1)} %get-tuple-element.35.own_east), channel_id=1, source_target_pairs={{0,16},{16,32},{32,48},{48,64},{64,80},{80,96},{96,112},{112,0},{1... | collective-permute-start | bytes 270344 | tf_op jit(solution)/shard_map/ppermute | solution.py:763
  3.4 16.1 %collective-permute-start.1 = (f32[2,48,128]{2,1,0:T(8,128)S(1)}, f32[2,48,128]{2,1,0:T(8,128)S(1)}, u32[]{:S(2)}, u32[]{:S(2)}) collective-permute-start(f32[2,48,128]{2,1,0:T(8,128)S(1)} %get-tuple-element.36.own_west), channel_id=1, source_target_pairs={{0,112},{16,0},{32,16},{48,32},{64,48},{80,64},{96,80},{112,96},{1... | collective-permute-start | bytes 147464 | tf_op jit(solution)/shard_map/ppermute | solution.py:763
  6.4 13.1 %collective-permute-start.2 = (f32[64,128]{1,0:T(8,128)S(1)}, f32[64,128]{1,0:T(8,128)S(1)}, u32[]{:S(2)}, u32[]{:S(2)}) collective-permute-start(f32[64,128]{1,0:T(8,128)S(1)} %get-tuple-element.37.own_north), channel_id=1, source_target_pairs={{0,1},{1,2},{2,3},{3,4},{4,5},{5,6},{6,7},{7,8},{8,9},{9,10},{10,1... | collective-permute-start | bytes 98312 | tf_op jit(solution)/shard_map/ppermute | solution.py:763
  8.0 11.5 %collective-permute-start.3 = (f32[64,128]{1,0:T(8,128)S(1)}, f32[64,128]{1,0:T(8,128)S(1)}, u32[]{:S(2)}, u32[]{:S(2)}) collective-permute-start(f32[64,128]{1,0:T(8,128)S(1)} %get-tuple-element.38.own_south), channel_id=1, source_target_pairs={{0,15},{1,0},{2,1},{3,2},{4,3},{5,4},{6,5},{7,6},{8,7},{9,8},{10,9... | collective-permute-start | bytes 98312 | tf_op jit(solution)/shard_map/ppermute | solution.py:763
  13.0 6.6 %copy-start = (f32[64,256]{1,0:T(8,128)S(1)}, f32[64,256]{1,0:T(8,128)}, u32[]{:S(2)}) copy-start(f32[64,256]{1,0:T(8,128)} %rain.1) | copy-start | bytes 196612
  25.4 4.4 %collective-permute-start.4 = (f32[104,128]{1,0:T(8,128)S(1)}, f32[104,128]{1,0:T(8,128)S(1)}, u32[]{:S(2)}, u32[]{:S(2)}) collective-permute-start(f32[104,128]{1,0:T(8,128)S(1)} %get-tuple-element.43.own_west), channel_id=1, source_target_pairs={{0,112},{16,0},{32,16},{48,32},{64,48},{80,64},{96,80},{112,96},{1... | collective-permute-start | bytes 159752 | tf_op jit(solution)/shard_map/ppermute | solution.py:763
  25.4 4.3 %collective-permute-start.5 = (f32[24,128]{1,0:T(8,128)S(1)}, f32[24,128]{1,0:T(8,128)S(1)}, u32[]{:S(2)}, u32[]{:S(2)}) collective-permute-start(f32[24,128]{1,0:T(8,128)S(1)} %get-tuple-element.47.own_east), channel_id=1, source_target_pairs={{0,16},{16,32},{32,48},{48,64},{64,80},{80,96},{96,112},{112,0},{1... | collective-permute-start | bytes 36872 | tf_op jit(solution)/shard_map/ppermute | solution.py:763
  29.8 7.4 %collective-permute-start.6 = (f32[80,128]{1,0:T(8,128)S(1)}, f32[80,128]{1,0:T(8,128)S(1)}, u32[]{:S(2)}, u32[]{:S(2)}) collective-permute-start(f32[80,128]{1,0:T(8,128)S(1)} %get-tuple-element.51), channel_id=1, source_target_pairs={{0,1},{1,2},{2,3},{3,4},{4,5},{5,6},{6,7},{7,8},{8,9},{9,10},{10,1... | collective-permute-start | bytes 122888 | tf_op jit(solution)/shard_map/ppermute | solution.py:763
  29.9 7.3 %collective-permute-start.7 = (f32[80,128]{1,0:T(8,128)S(1)}, f32[80,128]{1,0:T(8,128)S(1)}, u32[]{:S(2)}, u32[]{:S(2)}) collective-permute-start(f32[80,128]{1,0:T(8,128)S(1)} %get-tuple-element.52), channel_id=1, source_target_pairs={{0,15},{1,0},{2,1},{3,2},{4,3},{5,4},{6,5},{7,6},{8,7},{9,8},{10,9... | collective-permute-start | bytes 122888 | tf_op jit(solution)/shard_map/ppermute | solution.py:763

commit v3 on v2

--- a/solution.py
+++ b/solution.py
@@ -178,10 +178,10 @@
     )(temp, speeds, sea, tally)
 
 
-UNROLL_IN = 2
-UNROLL_FWD = 2
-UNROLL_BACK = 4
-UNROLL_MOM = 4
+UNROLL_IN = 4
+UNROLL_FWD = 20
+UNROLL_BACK = 20
+UNROLL_MOM = 5
 
 
 def interior_kernel(
@@ -308,61 +308,42 @@
     )(temp, speeds, mix, count)
 
 
-def column_kernel(
-    source, inverse, link, u_in, v_in, count, rain, own_east, own_west, own_north, own_south,
-    west, east, south, north,
-    temp_out, speeds_out, force_out, to_east, to_west, q_col, sides, u_end, v_high,
-    solved, u_new, v_low, row_low, row_high, col_low, col_high,
-    east_lim, north_lim, south_lim, west_lim, run, u_sum, v_sum, out_sems,
-):
-    def store(which, c):
-        part = pl.ds(c * CHUNK, CHUNK)
-        origin, target = (
-            (solved.at[part], temp_out.at[part]),
-            (u_new.at[part], speeds_out.at[0, part, pl.ds(0, ROWS - 8), :]),
-            (v_low.at[part], speeds_out.at[1, part, :, pl.ds(0, 128)]),
-        )[which]
-        return pltpu.make_async_copy(origin, target, out_sems.at[which, c])
-
+OUTER = (0, BLOCKS - 1)
+MIDDLE = tuple(range(1, BLOCKS - 1))
+
+
+def face_limits(
+    blocks, count, west, east, south, north, east_lim, north_lim, south_lim, west_lim
+):
     lane, row = lane_id(), row_id()
-    first_row, last_row = row == 0, row == 7
-    first_lane, last_lane = lane == 0, lane == 127
-    zero = jnp.zeros((8, 128), F32)
+    last_row, last_lane = row == 7, lane == 127
+    counts = tiles_of(count)
     pair = range(2)
-
-    counts = tiles_of(count)
-    after = [jnp.broadcast_to(east[h, 40:41, :], (8, 128)) for h in pair]
-    before = [jnp.broadcast_to(west[h, 85:86, :], (8, 128)) for h in pair]
-    ahead = next_row(counts, after, last_row)
-    for b, h in TILES:
-        east_lim[rows_of(b), lanes_of(h)] = jnp.minimum(counts[b, h], ahead[b, h])
     for h in pair:
-        west_lim[:, lanes_of(h)] = jnp.minimum(counts[0, h], before[h])
-    after = [pltpu.roll(north[rows_of(b), :], 127 - 40, 1) for b in range(BLOCKS)]
-    ahead = next_col(counts, after, last_lane)
-    for b, h in TILES:
-        north_lim[rows_of(b), lanes_of(h)] = jnp.minimum(counts[b, h], ahead[b, h])
-    for b in range(BLOCKS):
-        south_lim[rows_of(b), :] = jnp.minimum(
-            counts[b, 0], pltpu.roll(south[rows_of(b), :], 128 - 80, 1)
-        )
-
-    depth = lax.broadcasted_iota(jnp.int32, (LEVELS, 128), 0).astype(F32)
-    for h in pair:
-        speed = west[h, 40:80, :]
-        row_low[h] = (
-            advect_scale
-            * jnp.where(depth < west_lim[0:1, lanes_of(h)], speed, 0.0)
-            * jnp.where(speed > 0.0, west[h, 0:40, :], own_west[h, 0:40, :])
-        )
-        speed = own_east[h, 40:80, :]
-        row_high[h] = (
-            -advect_scale
-            * jnp.where(depth < east_lim[ROWS - 1 : ROWS, lanes_of(h)], speed, 0.0)
-            * jnp.where(speed > 0.0, own_east[h, 0:40, :], east[h, 0:40, :])
-        )
-    depth = lane.astype(F32)
-    for b in range(BLOCKS):
+        before = jnp.broadcast_to(west[h, 85:86, :], (8, 128))
+        west_lim[:, lanes_of(h)] = jnp.minimum(counts[0, h], before)
+        for b in blocks:
+            if b == BLOCKS - 1:
+                after = jnp.broadcast_to(east[h, 40:41, :], (8, 128))
+            else:
+                after = pltpu.roll(counts[b + 1, h], 7, 0)
+            ahead = jnp.where(last_row, after, pltpu.roll(counts[b, h], 7, 0))
+            east_lim[rows_of(b), lanes_of(h)] = jnp.minimum(counts[b, h], ahead)
+    for b in blocks:
+        rows = rows_of(b)
+        left = [pltpu.roll(counts[b, h], 127, 1) for h in pair]
+        left.append(pltpu.roll(north[rows, :], 127 - 40, 1))
+        for h in pair:
+            ahead = jnp.where(last_lane, left[h + 1], left[h])
+            north_lim[rows, lanes_of(h)] = jnp.minimum(counts[b, h], ahead)
+        south_lim[rows, :] = jnp.minimum(counts[b, 0], pltpu.roll(south[rows, :], 128 - 80, 1))
+
+
+def column_fluxes(
+    blocks, own_north, own_south, south, north, south_lim, north_lim, col_low, col_high
+):
+    depth = lane_id().astype(F32)
+    for b in blocks:
         rows = rows_of(b)
         limit = jnp.broadcast_to(south_lim[rows, 0:1], (8, 128))
         speed = pltpu.roll(south[rows, :], 128 - 40, 1)
@@ -379,11 +360,34 @@
             * jnp.where(speed > 0.0, own_north[rows, :], north[rows, :])
         )
 
+
+def row_fluxes(own_east, own_west, west, east, west_lim, east_lim, row_low, row_high):
+    depth = lax.broadcasted_iota(jnp.int32, (LEVELS, 128), 0).astype(F32)
+    for h in range(2):
+        speed = west[h, 40:80, :]
+        row_low[h] = (
+            advect_scale
+            * jnp.where(depth < west_lim[0:1, lanes_of(h)], speed, 0.0)
+            * jnp.where(speed > 0.0, west[h, 0:40, :], own_west[h, 0:40, :])
+        )
+        speed = own_east[h, 40:80, :]
+        row_high[h] = (
+            -advect_scale
+            * jnp.where(depth < east_lim[ROWS - 1 : ROWS, lanes_of(h)], speed, 0.0)
+            * jnp.where(speed > 0.0, own_east[h, 0:40, :], east[h, 0:40, :])
+        )
+
+
+def solve(blocks, place, source, inverse, link, col_low, col_high, row_low, row_high, solved):
+    lane, row = lane_id(), row_id()
+    first_row, last_row = row == 0, row == 7
+    first_lane, last_lane = lane == 0, lane == 127
+    zero = jnp.zeros((8, 128), F32)
+    pair = range(2)
+
     def forward(k, values):
         out = []
-        low = [jnp.where(first_row, spread(row_low, k, h), 0.0) for h in pair]
-        high = [jnp.where(last_row, spread(row_high, k, h), 0.0) for h in pair]
-        for b in range(BLOCKS):
+        for n, b in enumerate(blocks):
             rows = rows_of(b)
             add = [
                 jnp.where(first_lane, pltpu.roll(col_low[rows, :], 128 - k, 1), 0.0),
@@ -393,15 +397,15 @@
                 at = (k, rows, lanes_of(h))
                 total = source[at] + add[h]
                 if b == 0:
-                    total = total + low[h]
+                    total = total + jnp.where(first_row, spread(row_low, k, h), 0.0)
                 if b == BLOCKS - 1:
-                    total = total + high[h]
-                value = (total + link[at] * values[2 * b + h]) * inverse[at]
-                solved[at] = value
+                    total = total + jnp.where(last_row, spread(row_high, k, h), 0.0)
+                value = (total + link[at] * values[2 * n + h]) * inverse[at]
+                solved[k, place(b), lanes_of(h)] = value
                 out.append(value)
         return tuple(out)
 
-    blank = tuple(zero for _ in TILES)
+    blank = (zero,) * (2 * len(blocks))
 
     def forward_step(m, values):
         for n in range(UNROLL_FWD):
@@ -410,34 +414,53 @@
 
     lax.fori_loop(0, LEVELS // UNROLL_FWD, forward_step, blank)
 
-    def back_chunk(c_up, linked):
-        c = CHUNKS - 1 - c_up
-
-        def step(m, linked):
-            for n in range(UNROLL_BACK):
-                k = c * CHUNK + (CHUNK - 1 - m * UNROLL_BACK - n)
-                out = []
-                for i, below in zip(TILES, linked):
-                    at = (k, rows_of(i[0]), lanes_of(i[1]))
-                    value = solved[at] + inverse[at] * below
-                    solved[at] = value
-                    out.append(link[at] * value)
-                linked = tuple(out)
-            return linked
-
-        linked = lax.fori_loop(0, CHUNK // UNROLL_BACK, step, linked)
-        store(0, c).start()
+    def back_step(m, linked):
+        for n in range(UNROLL_BACK):
+            k = LEVELS - 1 - m * UNROLL_BACK - n
+            out = []
+            for i, below in zip([(b, h) for b in blocks for h in pair], linked):
+                at = (k, rows_of(i[0]), lanes_of(i[1]))
+                to = (k, place(i[0]), lanes_of(i[1]))
+                value = solved[to] + inverse[at] * below
+                solved[to] = value
+                out.append(link[at] * value)
+            linked = tuple(out)
         return linked
 
-    lax.fori_loop(0, CHUNKS, back_chunk, blank)
-
-    run[...] = jnp.zeros_like(run)
-    u_sum[...] = jnp.zeros_like(u_sum)
-    v_sum[...] = jnp.zeros_like(v_sum)
-    q_col[...] = jnp.zeros_like(q_col)
+    lax.fori_loop(0, LEVELS // UNROLL_BACK, back_step, blank)
+
+
+def row_face_sum(west_lim, q_rows):
+    depth = lax.broadcasted_iota(jnp.int32, (LEVELS, 128), 0).astype(F32)
+    out = []
+    for h in range(2):
+        part = jnp.where(depth < west_lim[0:1, lanes_of(h)], PRESS * q_rows(h), 0.0)
+        out.append(jnp.broadcast_to(jnp.sum(part, axis=0, keepdims=True), (8, 128)))
+    return out
+
+
+def col_face_sum(rows, south_lim, q_col):
+    limit = jnp.broadcast_to(south_lim[rows, 0:1], (8, 128))
+    part = jnp.where(lane_id().astype(F32) < limit, PRESS * q_col[rows, :], 0.0)
+    return jnp.broadcast_to(jnp.sum(part, axis=1, keepdims=True), (8, 128))
+
+
+def momentum(
+    blocks, values, following, u_in, v_in, east_lim, north_lim, run, u_sum, v_sum, q_col,
+    keep_u, keep_v, keep_row,
+):
+    lane, row = lane_id(), row_id()
+    last_row, last_lane = row == 7, lane == 127
+    zero = jnp.zeros((8, 128), F32)
+    pair = range(2)
     many = range(UNROLL_MOM)
-
-    def momentum(m, _):
+    for b in blocks:
+        run[rows_of(b), :] = jnp.zeros((8, COLS), F32)
+        u_sum[rows_of(b), :] = jnp.zeros((8, COLS), F32)
+        v_sum[rows_of(b), :] = jnp.zeros((8, COLS), F32)
+        q_col[rows_of(b), :] = zero
+
+    def step(m, _):
         first = m * UNROLL_MOM
         levels = [first + n for n in many]
         depths = [k.astype(F32) for k in levels]
@@ -449,26 +472,30 @@
                 total = run[at]
                 qs = []
                 for k in levels:
-                    half = 0.5 * solved[(k, *at)]
+                    half = 0.5 * values(k, b, h)
                     qs.append(total + half)
                     total = qs[-1] + half
                 run[at] = total
                 out.append(qs)
             return out
 
-        q_next = running(0)
-        turned_next = [[pltpu.roll(q, 7, 0) for q in q_next[h]] for h in pair]
-        for h in pair:
-            for n in many:
-                to_west[pl.ds(24 + 40 * h + levels[n], 1), :] = q_next[h][n][0:1]
-        for b in range(BLOCKS):
+        q_next = None
+        for b in blocks:
             rows = rows_of(b)
-            q, turned = q_next, turned_next
-            if b < BLOCKS - 1:
+            if q_next is None:
+                q = running(b)
+                turned = [[pltpu.roll(x, 7, 0) for x in q[h]] for h in pair]
+            else:
+                q, turned = q_next, turned_next
+            if b == 0:
+                for h in pair:
+                    for n in many:
+                        keep_row(levels[n], h, q[h][n][0:1])
+            if following(b):
                 q_next = running(b + 1)
                 turned_next = [[pltpu.roll(x, 7, 0) for x in q_next[h]] for h in pair]
             else:
-                turned_next = [[zero] * UNROLL_MOM] * 2
+                q_next, turned_next = None, [[zero] * UNROLL_MOM] * 2
             left = [[pltpu.roll(x, 127, 1) for x in q[h]] for h in pair]
             column = q_col[rows, :]
             for n in many:
@@ -483,10 +510,7 @@
                     speed = jnp.where(
                         depths[n] < limit, u_in[(levels[n], *at)] - PRESS * (q[h][n] - ahead), 0.0
                     )
-                    if b < BLOCKS - 1:
-                        u_new[(levels[n], *at)] = speed
-                    else:
-                        u_end[levels[n], :, lanes_of(h)] = speed
+                    keep_u(levels[n], b, h, speed)
                     total = total + speed
                 u_sum[at] = total
                 limit = north_lim[at]
@@ -496,92 +520,236 @@
                     speed = jnp.where(
                         depths[n] < limit, v_in[(levels[n], *at)] - PRESS * (q[h][n] - ahead), 0.0
                     )
-                    if h == 0:
-                        v_low[levels[n], rows, :] = speed
-                    else:
-                        v_high[levels[n], rows, :] = speed
+                    keep_v(levels[n], b, h, speed)
                     total = total + speed
                 v_sum[at] = total
         return 0
 
-    def momentum_chunk(c, _):
-        per = CHUNK // UNROLL_MOM
-        lax.fori_loop(c * per, (c + 1) * per, momentum, 0)
-        store(1, c).start()
-        store(2, c).start()
-        return 0
-
-    lax.fori_loop(0, CHUNKS, momentum_chunk, 0)
-
-    depth = lax.broadcasted_iota(jnp.int32, (LEVELS, 128), 0).astype(F32)
-    row_sum = []
-    for h in pair:
-        part = jnp.where(
-            depth < west_lim[0:1, lanes_of(h)], PRESS * to_west[24 + 40 * h : 64 + 40 * h, :], 0.0
-        )
-        row_sum.append(
-            jnp.broadcast_to(jnp.sum(part, axis=0, keepdims=True), (8, 128))
-        )
-    depth = lane.astype(F32)
-    col_sum = []
-    for b in range(BLOCKS):
+    lax.fori_loop(0, LEVELS // UNROLL_MOM, step, 0)
+
+
+def forcing(blocks, u_sum, v_sum, row_sum, south_lim, q_col, count, rain, keep):
+    lane, row = lane_id(), row_id()
+    first_row, first_lane, last_lane = row == 0, lane == 0, lane == 127
+    pair = range(2)
+    for b in blocks:
         rows = rows_of(b)
-        limit = jnp.broadcast_to(south_lim[rows, 0:1], (8, 128))
-        part = jnp.where(depth < limit, PRESS * q_col[rows, :], 0.0)
-        col_sum.append(jnp.broadcast_to(jnp.sum(part, axis=1, keepdims=True), (8, 128)))
-
-    east_sum, north_sum = tiles_of(u_sum), tiles_of(v_sum)
-    east_before = prev_row(east_sum, row_sum, first_row)
-    north_before = prev_col(north_sum, col_sum, first_lane)
-    for i in TILES:
-        at = (rows_of(i[0]), lanes_of(i[1]))
-        divergence = (east_sum[i] - east_before[i]) + (north_sum[i] - north_before[i])
-        force_out[at] = jnp.where(
-            count[at] > 0.0, source_scale * rain[at] - DIVERGE * divergence, 0.0
-        )
-    for b in range(BLOCKS):
-        sides[rows_of(b), :] = jnp.where(
-            first_lane,
-            pltpu.roll(north_sum[b, 1], 1, 1),
-            jnp.where(last_lane, col_sum[b], 0.0),
-        )
-    for h in pair:
-        to_east[rows_of(h), :] = pltpu.roll(force_out[ROWS - 8 : ROWS, lanes_of(h)], 5, 0)
-        to_east[8 * h + 5 : 8 * h + 6, :] = east_sum[BLOCKS - 1, h][7:8]
-        to_west[rows_of(h), :] = force_out[0:8, lanes_of(h)]
-        to_west[8 * h + 5 : 8 * h + 6, :] = row_sum[h][0:1]
-    to_east[16:24, :] = pltpu.roll(sides[ROWS - 8 : ROWS, :], 5, 0)
-    to_west[16:24, :] = sides[0:8, :]
-
-    for c in range(CHUNKS):
-        for which in range(3):
-            store(which, c).wait()
-
-
-def columns(*args):
+        col_sum = col_face_sum(rows, south_lim, q_col)
+        u = [u_sum[rows, lanes_of(h)] for h in pair]
+        v = [v_sum[rows, lanes_of(h)] for h in pair]
+        right = [pltpu.roll(v[h], 1, 1) for h in pair]
+        v_before = [
+            jnp.where(first_lane, col_sum, right[0]), jnp.where(first_lane, right[0], right[1])
+        ]
+        tiles = []
+        for h in pair:
+            at = (rows, lanes_of(h))
+            if b == 0:
+                before = row_sum[h]
+            else:
+                before = pltpu.roll(u_sum[rows_of(b - 1), lanes_of(h)], 1, 0)
+            u_before = jnp.where(first_row, before, pltpu.roll(u[h], 1, 0))
+            divergence = (u[h] - u_before) + (v[h] - v_before[h])
+            tiles.append(
+                jnp.where(count[at] > 0.0, source_scale * rain[at] - DIVERGE * divergence, 0.0)
+            )
+        side = jnp.where(first_lane, right[1], jnp.where(last_lane, col_sum, 0.0))
+        keep(b, tiles, side)
+
+
+def outer_kernel(
+    source, inverse, link, u_in, v_in, count, rain, own_east, own_west, own_north, own_south,
+    west, east, south, north,
+    solved, to_east, to_west,
+    row_low, row_high, col_low, col_high, east_lim, north_lim, south_lim, west_lim,
+    run, u_sum, v_sum, q_col,
+):
+    face_limits(
+        OUTER, count, west, east, south, north, east_lim, north_lim, south_lim, west_lim
+    )
+    row_fluxes(own_east, own_west, west, east, west_lim, east_lim, row_low, row_high)
+    column_fluxes(
+        OUTER, own_north, own_south, south, north, south_lim, north_lim, col_low, col_high
+    )
+
+    def place(b):
+        return slice(0, 8) if b == 0 else slice(8, 16)
+
+    solve(OUTER, place, source, inverse, link, col_low, col_high, row_low, row_high, solved)
+
+    def keep_row(k, h, value):
+        to_west[pl.ds(24 + 40 * h + k, 1), :] = value
+
+    def drop(*args):
+        pass
+
+    momentum(
+        OUTER, lambda k, b, h: solved[k, place(b), lanes_of(h)], lambda b: False,
+        u_in, v_in, east_lim, north_lim, run, u_sum, v_sum, q_col, drop, drop, keep_row,
+    )
+    row_sum = row_face_sum(west_lim, lambda h: to_west[24 + 40 * h : 64 + 40 * h, :])
+    u_sum[rows_of(BLOCKS - 2), :] = jnp.zeros((8, COLS), F32)
+
+    def keep(b, tiles, side):
+        for h in range(2):
+            if b == 0:
+                to_west[rows_of(h), :] = tiles[h]
+                to_west[8 * h + 5 : 8 * h + 6, :] = row_sum[h][0:1]
+            else:
+                to_east[rows_of(h), :] = pltpu.roll(tiles[h], 5, 0)
+                to_east[8 * h + 5 : 8 * h + 6, :] = u_sum[ROWS - 1 : ROWS, lanes_of(h)]
+        if b == 0:
+            to_west[16:24, :] = side
+        else:
+            to_east[16:24, :] = pltpu.roll(side, 5, 0)
+
+    forcing(OUTER, u_sum, v_sum, row_sum, south_lim, q_col, count, rain, keep)
+
+
+def outer(*args):
+    plane = pltpu.VMEM((ROWS, COLS), F32)
+    strip = pltpu.VMEM((ROWS, 128), F32)
+    levels = pltpu.VMEM((2, LEVELS, 128), F32)
     return pl.pallas_call(
-        column_kernel,
+        outer_kernel,
+        out_shape=(shape(LEVELS, 16, COLS), shape(24, 128), shape(104, 128)),
+        in_specs=[VMEM] * 15,
+        out_specs=(VMEM,) * 3,
+        scratch_shapes=[
+            levels, levels, strip, strip, plane, plane, strip, pltpu.VMEM((8, COLS), F32),
+            plane, plane, plane, strip,
+        ],
+        compiler_params=params(LIMIT_COLUMNS),
+        name="outer",
+    )(*args)
+
+
+def middle_kernel(
+    source, inverse, link, u_in, v_in, count, rain, own_north, own_south,
+    west, east, south, north, outside, own_west,
+    solved, u_new, v_low, v_high, force_out, q_col, sides,
+    col_low, col_high, east_lim, north_lim, south_lim, west_lim, run, u_sum, v_sum,
+):
+    every = tuple(range(BLOCKS))
+    face_limits(
+        every, count, west, east, south, north, east_lim, north_lim, south_lim, west_lim
+    )
+    column_fluxes(
+        MIDDLE, own_north, own_south, south, north, south_lim, north_lim, col_low, col_high
+    )
+
+    def place(b):
+        return rows_of(b - 1)
+
+    solve(MIDDLE, place, source, inverse, link, col_low, col_high, None, None, solved)
+
+    def values(k, b, h):
+        if b == 0:
+            return outside[k, 0:8, lanes_of(h)]
+        if b == BLOCKS - 1:
+            return outside[k, 8:16, lanes_of(h)]
+        return solved[k, place(b), lanes_of(h)]
+
+    def keep_u(k, b, h, speed):
+        u_new[k, rows_of(b), lanes_of(h)] = speed
+
+    def keep_v(k, b, h, speed):
+        if h == 0:
+            v_low[k, rows_of(b), :] = speed
+        else:
+            v_high[k, rows_of(b), :] = speed
+
+    momentum(
+        every, values, lambda b: b < BLOCKS - 1, u_in, v_in, east_lim, north_lim,
+        run, u_sum, v_sum, q_col, keep_u, keep_v, lambda k, h, value: None,
+    )
+    row_sum = [
+        jnp.broadcast_to(own_west[8 * h + 5 : 8 * h + 6, :], (8, 128)) for h in range(2)
+    ]
+
+    def keep(b, tiles, side):
+        for h in range(2):
+            force_out[rows_of(b), lanes_of(h)] = tiles[h]
+        sides[rows_of(b), :] = side
+
+    forcing(every, u_sum, v_sum, row_sum, south_lim, q_col, count, rain, keep)
+
+
+def middle(*args):
+    plane = pltpu.VMEM((ROWS, COLS), F32)
+    strip = pltpu.VMEM((ROWS, 128), F32)
+    half = shape(LEVELS, ROWS, 128)
+    return pl.pallas_call(
+        middle_kernel,
         out_shape=(
-            shape(LEVELS, ROWS, COLS), shape(2, LEVELS, ROWS, COLS), shape(ROWS, COLS),
-            shape(24, 128), shape(104, 128), shape(ROWS, 128), shape(ROWS, 128),
-            shape(LEVELS, 8, COLS), shape(LEVELS, ROWS, 128),
+            shape(LEVELS, ROWS - 16, COLS), shape(LEVELS, ROWS, COLS), half, half,
+            shape(ROWS, COLS), shape(ROWS, 128), shape(ROWS, 128),
         ),
         in_specs=[VMEM] * 15,
-        out_specs=(ANY, ANY) + (VMEM,) * 7,
+        out_specs=(VMEM,) * 7,
         scratch_shapes=[
-            pltpu.VMEM((LEVELS, ROWS, COLS), F32),
-            pltpu.VMEM((LEVELS, ROWS - 8, COLS), F32),
-            pltpu.VMEM((LEVELS, ROWS, 128), F32),
-            pltpu.VMEM((2, LEVELS, 128), F32), pltpu.VMEM((2, LEVELS, 128), F32),
-            pltpu.VMEM((ROWS, 128), F32), pltpu.VMEM((ROWS, 128), F32),
-            pltpu.VMEM((ROWS, COLS), F32), pltpu.VMEM((ROWS, COLS), F32),
-            pltpu.VMEM((ROWS, 128), F32), pltpu.VMEM((8, COLS), F32),
-            pltpu.VMEM((ROWS, COLS), F32), pltpu.VMEM((ROWS, COLS), F32),
-            pltpu.VMEM((ROWS, COLS), F32),
-            pltpu.SemaphoreType.DMA((3, CHUNKS)),
+            strip, strip, plane, plane, strip, pltpu.VMEM((8, COLS), F32), plane, plane, plane,
         ],
+        cost_estimate=pl.CostEstimate(
+            flops=30 * LEVELS * ROWS * COLS, bytes_accessed=16 * LEVELS * ROWS * COLS,
+            transcendentals=0,
+        ),
         compiler_params=params(LIMIT_COLUMNS),
-        name="columns",
+        name="middle",
+    )(*args)
+
+
+def writer_kernel(
+    outside, solved, u_new, v_low, from_east, count, east, temp_out, speeds_out, u_fix, sems
+):
+    copies = [
+        (outside.at[:, pl.ds(0, 8), :], temp_out.at[:, pl.ds(0, 8), :]),
+        (outside.at[:, pl.ds(8, 8), :], temp_out.at[:, pl.ds(ROWS - 8, 8), :]),
+        (solved, temp_out.at[:, pl.ds(8, ROWS - 16), :]),
+        (u_new.at[:, pl.ds(0, ROWS - 8), :], speeds_out.at[0, :, pl.ds(0, ROWS - 8), :]),
+        (v_low, speeds_out.at[1, :, :, pl.ds(0, 128)]),
+        (u_fix, speeds_out.at[0, :, pl.ds(ROWS - 8, 8), :]),
+    ]
+    copies = [
+        pltpu.make_async_copy(origin, target, sems.at[n])
+        for n, (origin, target) in enumerate(copies)
+    ]
+    for copy in copies[:-1]:
+        copy.start()
+    last_row = row_id() == 7
+    for h in range(2):
+        limit = jnp.minimum(
+            count[ROWS - 8 :, lanes_of(h)], jnp.broadcast_to(east[h, 40:41, :], (8, 128))
+        )
+        limit = jnp.where(last_row, limit, 0.0)
+        for k in range(LEVELS):
+            at = 24 + 40 * h + k
+            u_fix[k, :, lanes_of(h)] = u_new[k, ROWS - 8 :, lanes_of(h)] + jnp.where(
+                float(k) < limit,
+                PRESS * jnp.broadcast_to(from_east[at : at + 1, :], (8, 128)),
+                0.0,
+            )
+    copies[-1].start()
+    for copy in copies:
+        copy.wait()
+
+
+def writer(*args):
+    return pl.pallas_call(
+        writer_kernel,
+        out_shape=(shape(LEVELS, ROWS, COLS), shape(2, LEVELS, ROWS, COLS)),
+        in_specs=[VMEM] * 7,
+        out_specs=(ANY, ANY),
+        scratch_shapes=[
+            pltpu.VMEM((LEVELS, 8, COLS), F32),
+            pltpu.SemaphoreType.DMA((6,)),
+        ],
+        cost_estimate=pl.CostEstimate(
+            flops=LEVELS * ROWS * COLS, bytes_accessed=12 * LEVELS * ROWS * COLS,
+            transcendentals=0,
+        ),
+        compiler_params=params(LIMIT_COLUMNS),
+        name="writer",
     )(*args)
 
 
@@ -658,27 +826,10 @@
 
 
 def final_kernel(
-    speeds, u_end, v_high, from_east, count, east,
+    speeds, v_high, count,
     force_ext, count_ext, sides_ext, south, north,
-    speeds_out, out, u_fix, v_fix, sems,
-):
-    last_row = row_id() == 7
-    for h in range(2):
-        limit = jnp.minimum(
-            count[ROWS - 8 :, lanes_of(h)], jnp.broadcast_to(east[h, 40:41, :], (8, 128))
-        )
-        limit = jnp.where(last_row, limit, 0.0)
-        for k in range(LEVELS):
-            at = 24 + 40 * h + k
-            u_fix[k, :, lanes_of(h)] = u_end[k, :, lanes_of(h)] + jnp.where(
-                float(k) < limit,
-                PRESS * jnp.broadcast_to(from_east[at : at + 1, :], (8, 128)),
-                0.0,
-            )
-    save_rows = pltpu.make_async_copy(
-        u_fix, speeds_out.at[0, :, pl.ds(ROWS - 8, 8), :], sems.at[0]
-    )
-    save_rows.start()
+    speeds_out, out, v_fix, sem,
+):
     last_lane = lane_id(8) == 127
     for b in range(BLOCKS):
         rows = rows_of(b)
@@ -690,7 +841,7 @@
                 float(k) < limit, PRESS * pltpu.roll(held, 63 - k, 1), 0.0
             )
     save_cols = pltpu.make_async_copy(
-        v_fix, speeds_out.at[1, :, :, pl.ds(128, 128)], sems.at[1]
+        v_fix, speeds_out.at[1, :, :, pl.ds(128, 128)], sem
     )
     save_cols.start()
     lane = lane_id(EXT)
@@ -737,7 +888,6 @@
         update = omega * inverse * residual + (cheb_gamma * omega - 1.0) * update
         iterate = iterate + update
     out[...] = iterate[8 : 8 + ROWS, 0:COLS]
-    save_rows.wait()
     save_cols.wait()
 
 
@@ -745,12 +895,11 @@
     return pl.pallas_call(
         final_kernel,
         out_shape=(shape(2, LEVELS, ROWS, COLS), shape(ROWS, COLS)),
-        in_specs=[ANY] + [VMEM] * 10,
+        in_specs=[ANY] + [VMEM] * 7,
         out_specs=(ANY, VMEM),
         scratch_shapes=[
-            pltpu.VMEM((LEVELS, 8, COLS), F32),
             pltpu.VMEM((LEVELS, ROWS, 128), F32),
-            pltpu.SemaphoreType.DMA((2,)),
+            pltpu.SemaphoreType.DMA,
         ],
         input_output_aliases={0: 0},
         compiler_params=params(LIMIT_COLUMNS),
@@ -784,20 +933,26 @@
     west = shift(to_east, "gx", 1)
     east = shift(to_west, "gx", -1)
     inside = interior(thermal_departure, current_speeds, mixing_coefficient, count)
-    temp_next, speeds, force, own_east, own_west, q_col, sides, u_end, v_high = columns(
+    outside, own_east, own_west = outer(
         *inside, count, rainfall_runoff_input, to_east, to_west, to_north, to_south,
         west, east, south, north,
     )
     from_west = shift(own_east, "gx", 1)
     from_east = shift(own_west, "gx", -1)
+    solved, u_new, v_low, v_high, force, q_col, sides = middle(
+        *inside, count, rainfall_runoff_input, to_north, to_south,
+        west, east, south, north, outside, own_west,
+    )
     force_ext, count_ext, sides_ext, north_edge, south_edge = edges(
         force, sides, q_col, count, west, east, own_east, own_west, from_west, from_east
     )
     from_south = shift(north_edge, "gy", 1)
     from_north = shift(south_edge, "gy", -1)
+    temp_next, speeds = writer(
+        outside, solved, u_new, v_low, from_east, count, east
+    )
     velocity_next, surface = final(
-        speeds, u_end, v_high, from_east, count, east,
-        force_ext, count_ext, sides_ext, from_south, from_north,
+        speeds, v_high, count, force_ext, count_ext, sides_ext, from_south, from_north,
     )
     return (temp_next, velocity_next, surface)
 

time: 40.6 us -> 36.5 us (0.90)
  waiting for transfers between devices: 5.84 us -> 0.42 us
  Pallas kernels: 18.5 us -> 19.7 us
    ppermute x8, waiting for transfers between devices: 5.84 us -> 0.42 us  [shift(): lax.ppermute(array, axis, [(i, (i + step) % count) for i in range(count)])]
    pallas_call x1 -> x3, Pallas kernels: 5.8 us -> 7.92 us  [the longest x1 3.43 us: middle(): pl.pallas_call(middle_kernel, out_shape=(shape(LEVELS, ROWS - 16, COLS),...]
    pallas_call x1, Pallas kernels: 6.53 us -> 5.84 us  [interior(): pl.pallas_call(interior_kernel, out_shape=(block,) * 5, in_specs=[ANY, AN...]
  transfers between devices with their start and end apart: 8 -> 8, of which waited for: 2 -> 1; matrix products, arithmetic and copies ran while one was open for 0% -> 0% of each run, Pallas kernels for 16% -> 33%
where the time goes in v3:
time: 36.5 us; the launch traced here: 36.4 us
  Pallas kernels  19.7 us (54%)
  starting transfers between devices  15.5 us (42%)
  between operations  0.76 us (2%)
  waiting for transfers between devices  0.42 us (1%)
    ppermute x8, starting transfers between devices, shift(): lax.ppermute(array, axis, [(i, (i + step) % count) for i in range(count)])  15.5 us
    pallas_call x1, Pallas kernels, interior(): pl.pallas_call(interior_kernel, out_shape=(block,) * 5, in_specs=[ANY, AN...  5.84 us
    pallas_call x1, Pallas kernels, middle(): pl.pallas_call(middle_kernel, out_shape=(shape(LEVELS, ROWS - 16, COLS),...  3.43 us
    pallas_call x1, Pallas kernels, final(): pl.pallas_call(final_kernel, out_shape=(shape(2, LEVELS, ROWS, COLS), sha...  3.07 us
    pallas_call x1, Pallas kernels, writer(): pl.pallas_call(writer_kernel, out_shape=(shape(LEVELS, ROWS, COLS), shape...  2.79 us
    pallas_call x1, Pallas kernels, pack(): pl.pallas_call(pack_kernel, out_shape=(shape(ROWS, COLS), shape(2, 88, 12...  2.78 us
    pallas_call x1, Pallas kernels, outer(): pl.pallas_call(outer_kernel, out_shape=(shape(LEVELS, 16, COLS), shape(24...  1.7 us
  transfers between devices with their start and end apart: 8, of which 1 were waited for; matrix products, arithmetic and copies ran while one was open for 0% of the time, Pallas kernels for 33%

profile of v3, /device:TPU:0, one launch (start us, length us, event | category | flops | bytes accessed | tf_op | source)
XLA Modules:
  0.0 36.4 jit_solution(18172338142587424297)
XLA Ops:
  0.6 2.8 %pack.1 = (f32[64,256]{1,0:T(8,128)S(1)}, f32[2,88,128]{2,1,0:T(8,128)S(1)}, f32[2,48,128]{2,1,0:T(8,128)S(1)}, f32[64,128]{1,0:T(8,128)S(1)}, f32[64,128]{1,0:T(8,128)S(1)}) custom-call(f32[40,64,256]{2,1,0:T(8,128)} %temp.3, f32[2,40,64,256]{3,2,1,0:T(8,128)} %speeds.3, s32[64,256]{1,0:T(8,128)} %sea_in.1, s32[64,256]{1,0:T(8,128)} %tally_in.1), custom_call_target="tpu_custom_call" | custom-call | tf_op jit(solution)/shard_map/pack/pallas_call | solution.py:158
  3.4 0.0 collective-permute-start
  3.4 2.9 %collective-permute-start.1 = (f32[2,48,128]{2,1,0:T(8,128)S(1)}, f32[2,48,128]{2,1,0:T(8,128)S(1)}, u32[]{:S(2)}, u32[]{:S(2)}) collective-permute-start(f32[2,48,128]{2,1,0:T(8,128)S(1)} %get-tuple-element.39.own_west), channel_id=1, source_target_pairs={{0,112},{16,0},{32,16},{48,32},{64,48},{80,64},{96,80},{112,96},{1... | collective-permute-start | bytes 147464 | tf_op jit(solution)/shard_map/ppermute | solution.py:912
  6.4 1.7 %collective-permute-start.2 = (f32[64,128]{1,0:T(8,128)S(1)}, f32[64,128]{1,0:T(8,128)S(1)}, u32[]{:S(2)}, u32[]{:S(2)}) collective-permute-start(f32[64,128]{1,0:T(8,128)S(1)} %get-tuple-element.40.own_north), channel_id=1, source_target_pairs={{0,1},{1,2},{2,3},{3,4},{4,5},{5,6},{6,7},{7,8},{8,9},{9,10},{10,1... | collective-permute-start | bytes 98312 | tf_op jit(solution)/shard_map/ppermute | solution.py:912
  8.0 4.9 %collective-permute-start.3 = (f32[64,128]{1,0:T(8,128)S(1)}, f32[64,128]{1,0:T(8,128)S(1)}, u32[]{:S(2)}, u32[]{:S(2)}) collective-permute-start(f32[64,128]{1,0:T(8,128)S(1)} %get-tuple-element.41.own_south), channel_id=1, source_target_pairs={{0,15},{1,0},{2,1},{3,2},{4,3},{5,4},{6,5},{7,6},{8,7},{9,8},{10,9... | collective-permute-start | bytes 98312 | tf_op jit(solution)/shard_map/ppermute | solution.py:912
  13.0 0.0 copy-start
  13.0 5.8 %interior.1 = (f32[40,64,256]{2,1,0:T(8,128)S(1)}, f32[40,64,256]{2,1,0:T(8,128)S(1)}, f32[40,64,256]{2,1,0:T(8,128)S(1)}, f32[40,64,256]{2,1,0:T(8,128)S(1)}, f32[40,64,256]{2,1,0:T(8,128)S(1)}) custom-call(f32[40,64,256]{2,1,0:T(8,128)} %temp.3, f32[2,40,64,256]{3,2,1,0:T(8,128)} %speeds.3, f32[40,64,256]{2,1,0:T(8,128)} %mix.1, ...), custom_call_target="tpu_custom_call" | custom-call | flops 19660800 | bytes 10485760 | tf_op jit(solution)/shard_map/interior/pallas_call | solution.py:292
  18.8 0.0 collective-permute-done.2.south
  18.8 0.0 collective-permute-done.3.north
  18.8 0.0 collective-permute-done.1.east.east_in
  18.9 0.0 collective-permute-done.west
  18.9 0.0 copy-done
  18.9 1.7 %outer.1 = (f32[40,16,256]{2,1,0:T(8,128)S(1)}, f32[24,128]{1,0:T(8,128)S(1)}, f32[104,128]{1,0:T(8,128)S(1)}) custom-call(f32[40,64,256]{2,1,0:T(8,128)S(1)} %get-tuple-element.33.source, f32[40,64,256]{2,1,0:T(8,128)S(1)} %get-tuple-element.34.inverse, f32[40,64,256]{2,1,0:T(8,128)S(1)} %get-tuple-element.35.link, ...), custom_call_target="tpu_custom_call" | custom-call | tf_op jit(solution)/shard_map/outer/pallas_call | solution.py:613
  20.6 0.0 collective-permute-start.4
  20.6 0.5 %collective-permute-start.5 = (f32[24,128]{1,0:T(8,128)S(1)}, f32[24,128]{1,0:T(8,128)S(1)}, u32[]{:S(2)}, u32[]{:S(2)}) collective-permute-start(f32[24,128]{1,0:T(8,128)S(1)} %get-tuple-element.53.own_east), channel_id=1, source_target_pairs={{0,16},{16,32},{32,48},{48,64},{64,80},{80,96},{96,112},{112,0},{1... | collective-permute-start | bytes 36872 | tf_op jit(solution)/shard_map/ppermute | solution.py:912
  21.1 3.4 %middle.1 = (f32[40,48,256]{2,1,0:T(8,128)S(1)}, f32[40,64,256]{2,1,0:T(8,128)S(1)}, f32[40,64,128]{2,1,0:T(8,128)S(1)}, f32[40,64,128]{2,1,0:T(8,128)S(1)}, f32...) custom-call(f32[40,64,256]{2,1,0:T(8,128)S(1)} %get-tuple-element.33.source, ...), custom_call_target="tpu_custom_call" | custom-call | flops 19660800 | bytes 10485760 | tf_op jit(solution)/shard_map/middle/pallas_call | solution.py:682
  24.5 0.4 %collective-permute-done.5.from_west = f32[24,128]{1,0:T(8,128)S(1)} collective-permute-done((f32[24,128]{1,0:T(8,128)S(1)}, f32[24,128]{1,0:T(8,128)S(1)}, u32[]{:S(2)}, u32[]{:S(2)}) %collective-permute-start.5) | collective-permute-done | bytes 12320 | tf_op jit(solution)/shard_map/ppermute | solution.py:912
  24.9 0.0 collective-permute-done.4.from_east
  25.0 0.1 edges.1
  25.1 0.1 collective-permute-start.6
  25.1 5.3 %collective-permute-start.7 = (f32[80,128]{1,0:T(8,128)S(1)}, f32[80,128]{1,0:T(8,128)S(1)}, u32[]{:S(2)}, u32[]{:S(2)}) collective-permute-start(f32[80,128]{1,0:T(8,128)S(1)} %get-tuple-element.58), channel_id=1, source_target_pairs={{0,15},{1,0},{2,1},{3,2},{4,3},{5,4},{6,5},{7,6},{8,7},{9,8},{10,9... | collective-permute-start | bytes 122888 | tf_op jit(solution)/shard_map/ppermute | solution.py:912
  30.5 2.8 %writer.1 = (f32[40,64,256]{2,1,0:T(8,128)}, f32[2,40,64,256]{3,2,1,0:T(8,128)}) custom-call(f32[40,16,256]{2,1,0:T(8,128)S(1)} %get-tuple-element.42.outside, f32[40,48,256]{2,1,0:T(8,128)S(1)} %get-tuple-element.44.solved, f32[40,64,256]{2,1,0:T(8,128)S(1)} %get-tuple-element.45.u_new, f32[40,64,128]{2,1,0:T(8,128)S(1)} %get-tuple-element.46.v_low, ...), custom_call_target="tpu_custom_call" | custom-call | flops 655360 | bytes 7864320 | tf_op jit(solution)/shard_map/writer/pallas_call | solution.py:738
  33.3 0.0 collective-permute-done.6.south
  33.3 0.0 collective-permute-done.7.north
  33.3 3.1 %final.1 = (f32[2,40,64,256]{3,2,1,0:T(8,128)}, f32[64,256]{1,0:T(8,128)}) custom-call(f32[2,40,64,256]{3,2,1,0:T(8,128)} %get-tuple-element.48.speeds, f32[40,64,128]{2,1,0:T(8,128)S(1)} %get-tuple-element.49.v_high, f32[64,256]{1,0:T(8,128)S(1)} %get-tuple-element.32.count, ...), custom_call_target="tpu_custom_call", output_to_operand_aliasing={{0}: (0, {})} | custom-call | tf_op jit(solution)/shard_map/final/pallas_call | solution.py:895
Async XLA Ops:
  3.4 15.4 %collective-permute-start = (f32[2,88,128]{2,1,0:T(8,128)S(1)}, f32[2,88,128]{2,1,0:T(8,128)S(1)}, u32[]{:S(2)}, u32[]{:S(2)}) collective-permute-start(f32[2,88,128]{2,1,0:T(8,128)S(1)} %get-tuple-element.38.own_east), channel_id=1, source_target_pairs={{0,16},{16,32},{32,48},{48,64},{64,80},{80,96},{96,112},{112,0},{1... | collective-permute-start | bytes 270344 | tf_op jit(solution)/shard_map/ppermute | solution.py:912
  3.4 15.4 %collective-permute-start.1 = (f32[2,48,128]{2,1,0:T(8,128)S(1)}, f32[2,48,128]{2,1,0:T(8,128)S(1)}, u32[]{:S(2)}, u32[]{:S(2)}) collective-permute-start(f32[2,48,128]{2,1,0:T(8,128)S(1)} %get-tuple-element.39.own_west), channel_id=1, source_target_pairs={{0,112},{16,0},{32,16},{48,32},{64,48},{80,64},{96,80},{112,96},{1... | collective-permute-start | bytes 147464 | tf_op jit(solution)/shard_map/ppermute | solution.py:912
  6.4 12.4 %collective-permute-start.2 = (f32[64,128]{1,0:T(8,128)S(1)}, f32[64,128]{1,0:T(8,128)S(1)}, u32[]{:S(2)}, u32[]{:S(2)}) collective-permute-start(f32[64,128]{1,0:T(8,128)S(1)} %get-tuple-element.40.own_north), channel_id=1, source_target_pairs={{0,1},{1,2},{2,3},{3,4},{4,5},{5,6},{6,7},{7,8},{8,9},{9,10},{10,1... | collective-permute-start | bytes 98312 | tf_op jit(solution)/shard_map/ppermute | solution.py:912
  8.0 10.8 %collective-permute-start.3 = (f32[64,128]{1,0:T(8,128)S(1)}, f32[64,128]{1,0:T(8,128)S(1)}, u32[]{:S(2)}, u32[]{:S(2)}) collective-permute-start(f32[64,128]{1,0:T(8,128)S(1)} %get-tuple-element.41.own_south), channel_id=1, source_target_pairs={{0,15},{1,0},{2,1},{3,2},{4,3},{5,4},{6,5},{7,6},{8,7},{9,8},{10,9... | collective-permute-start | bytes 98312 | tf_op jit(solution)/shard_map/ppermute | solution.py:912
  13.0 5.9 %copy-start = (f32[64,256]{1,0:T(8,128)S(1)}, f32[64,256]{1,0:T(8,128)}, u32[]{:S(2)}) copy-start(f32[64,256]{1,0:T(8,128)} %rain.3) | copy-start | bytes 196612
  20.6 4.4 %collective-permute-start.4 = (f32[104,128]{1,0:T(8,128)S(1)}, f32[104,128]{1,0:T(8,128)S(1)}, u32[]{:S(2)}, u32[]{:S(2)}) collective-permute-start(f32[104,128]{1,0:T(8,128)S(1)} %get-tuple-element.43.own_west), channel_id=1, source_target_pairs={{0,112},{16,0},{32,16},{48,32},{64,48},{80,64},{96,80},{112,96},{1... | collective-permute-start | bytes 159752 | tf_op jit(solution)/shard_map/ppermute | solution.py:912
  20.6 4.3 %collective-permute-start.5 = (f32[24,128]{1,0:T(8,128)S(1)}, f32[24,128]{1,0:T(8,128)S(1)}, u32[]{:S(2)}, u32[]{:S(2)}) collective-permute-start(f32[24,128]{1,0:T(8,128)S(1)} %get-tuple-element.53.own_east), channel_id=1, source_target_pairs={{0,16},{16,32},{32,48},{48,64},{64,80},{80,96},{96,112},{112,0},{1... | collective-permute-start | bytes 36872 | tf_op jit(solution)/shard_map/ppermute | solution.py:912
  25.1 8.2 %collective-permute-start.6 = (f32[80,128]{1,0:T(8,128)S(1)}, f32[80,128]{1,0:T(8,128)S(1)}, u32[]{:S(2)}, u32[]{:S(2)}) collective-permute-start(f32[80,128]{1,0:T(8,128)S(1)} %get-tuple-element.57), channel_id=1, source_target_pairs={{0,1},{1,2},{2,3},{3,4},{4,5},{5,6},{6,7},{7,8},{8,9},{9,10},{10,1... | collective-permute-start | bytes 122888 | tf_op jit(solution)/shard_map/ppermute | solution.py:912
  25.1 8.1 %collective-permute-start.7 = (f32[80,128]{1,0:T(8,128)S(1)}, f32[80,128]{1,0:T(8,128)S(1)}, u32[]{:S(2)}, u32[]{:S(2)}) collective-permute-start(f32[80,128]{1,0:T(8,128)S(1)} %get-tuple-element.58), channel_id=1, source_target_pairs={{0,15},{1,0},{2,1},{3,2},{4,3},{5,4},{6,5},{7,6},{8,7},{9,8},{10,9... | collective-permute-start | bytes 122888 | tf_op jit(solution)/shard_map/ppermute | solution.py:912

commit v4 on v3

--- a/solution.py
+++ b/solution.py
@@ -6,14 +6,15 @@
 from jax.sharding import PartitionSpec as P
 
 ITERS = 6
-LIMIT_PACK = 40
-LIMIT_INTERIOR = 40
-LIMIT_COLUMNS = 24
+Y_ROWS = 184
+LIMIT_PACK = 12
+LIMIT_INTERIOR = 8
+LIMIT_COLUMNS = 12
 LEVELS = 40
 ROWS = 64
 COLS = 256
 BLOCKS = ROWS // 8
-CHUNK = 8
+CHUNK = 20
 CHUNKS = LEVELS // CHUNK
 
 damping = 0.05
@@ -59,6 +60,20 @@
     return slice(128 * h, 128 * h + 128)
 
 
+def odd_place(axis):
+    return lax.axis_index(axis) % 2 == 1
+
+
+def sort_out(axis, lower, upper):
+    odd = odd_place(axis)
+    return jnp.where(odd, lower, upper), jnp.where(odd, upper, lower)
+
+
+def sort_in(axis, even_pair, odd_pair):
+    odd = odd_place(axis)
+    return jnp.where(odd, even_pair, odd_pair), jnp.where(odd, odd_pair, even_pair)
+
+
 def tiles_of(ref, *lead):
     return {(b, h): ref[(*lead, rows_of(b), lanes_of(h))] for b, h in TILES}
 
@@ -101,24 +116,34 @@
 
 def pack_kernel(
     temp, speeds, sea_in, tally_in,
-    count_out, to_east, to_west, to_north, to_south,
-    t_low, t_high, v_high, t_top, t_end, u_end, sea, tally, sems,
+    near, count_out, to_east, to_west, to_north, to_south, y_odd, y_even, x_odd, x_even,
+    v_high, u_end, sea, tally, sems, part_sems,
 ):
-    copies = [
-        pltpu.make_async_copy(sea_in, sea, sems.at[6]),
-        pltpu.make_async_copy(tally_in, tally, sems.at[7]),
-        pltpu.make_async_copy(temp.at[:, :, pl.ds(0, 128)], t_low, sems.at[0]),
-        pltpu.make_async_copy(temp.at[:, :, pl.ds(128, 128)], t_high, sems.at[1]),
-        pltpu.make_async_copy(speeds.at[1, :, :, pl.ds(128, 128)], v_high, sems.at[2]),
-        pltpu.make_async_copy(temp.at[:, pl.ds(0, 8), :], t_top, sems.at[3]),
-        pltpu.make_async_copy(temp.at[:, pl.ds(ROWS - 8, 8), :], t_end, sems.at[4]),
-        pltpu.make_async_copy(speeds.at[0, :, pl.ds(ROWS - 8, 8), :], u_end, sems.at[5]),
+    first = [
+        pltpu.make_async_copy(sea_in, sea, sems.at[0]),
+        pltpu.make_async_copy(tally_in, tally, sems.at[1]),
     ]
-    for copy in copies:
+    parts = []
+    for c in range(CHUNKS):
+        part = pl.ds(c * CHUNK, CHUNK)
+        parts.append(
+            (
+                pltpu.make_async_copy(temp.at[part], near.at[part], part_sems.at[0, c]),
+                pltpu.make_async_copy(
+                    speeds.at[1, part, :, pl.ds(128, 128)], v_high.at[part], part_sems.at[1, c]
+                ),
+            )
+        )
+    last = pltpu.make_async_copy(speeds.at[0, :, pl.ds(ROWS - 8, 8), :], u_end, sems.at[2])
+    for copy in first:
         copy.start()
-    copies[0].wait()
-    copies[1].wait()
-    copies = copies[2:]
+    for pair in parts:
+        for copy in pair:
+            copy.start()
+    last.start()
+
+    for copy in first:
+        copy.wait()
     latitude = lax.axis_index("gy") * COLS + lax.broadcasted_iota(jnp.int32, (ROWS, COLS), 1)
     inner = (latitude > 0) & (latitude < lax.axis_size("gy") * COLS - 1)
     count = jnp.where(inner & (sea[...] == 1), tally[...], 0).astype(F32)
@@ -127,55 +152,61 @@
         to_east[h, 80:86, :] = count[ROWS - 6 :, lanes_of(h)]
         to_east[h, 86:88, :] = jnp.zeros((2, 128), F32)
         to_west[h, 40:46, :] = count[:6, lanes_of(h)]
-        to_west[h, 46:48, :] = jnp.zeros((2, 128), F32)
-    lane = lane_id(ROWS)
-
-    def gather(ref, column, start, total):
-        for k in range(LEVELS):
-            total = jnp.where(
-                lane == start + k, pltpu.roll(ref[k], (start + k - column) % 128, 1), total
-            )
-        return total
-
-    copies[0].wait()
-    to_south[...] = gather(
-        t_low, 0, 0, pltpu.roll(count[:, :128], 40, 1)
-    )
-    copies[1].wait()
-    total = gather(t_high, 127, 0, pltpu.roll(count[:, 128:], (80 - 127) % 128, 1))
-    copies[2].wait()
-    to_north[...] = gather(v_high, 127, 40, total)
-    copies[3].wait()
-    copies[4].wait()
-    copies[5].wait()
+        to_west[h, 46:88, :] = jnp.zeros((42, 128), F32)
+    lane = lane_id()
+    low, high = [], []
+    for b in range(BLOCKS):
+        low.append(pltpu.roll(count[rows_of(b), :128], 40, 1))
+        high.append(pltpu.roll(count[rows_of(b), 128:], (80 - 127) % 128, 1))
+
+    for c in range(CHUNKS):
+        parts[c][0].wait()
+        parts[c][1].wait()
+        for k in range(c * CHUNK, (c + 1) * CHUNK):
+            for b in range(BLOCKS):
+                rows = rows_of(b)
+                low[b] = jnp.where(lane == k, pltpu.roll(near[k, rows, :128], k, 1), low[b])
+                high[b] = jnp.where(lane == k, pltpu.roll(near[k, rows, 128:], k + 1, 1), high[b])
+                high[b] = jnp.where(
+                    lane == k + 40, pltpu.roll(v_high[k, rows, :], k + 41, 1), high[b]
+                )
+        levels = slice(c * CHUNK, (c + 1) * CHUNK)
+        for h in range(2):
+            to_west[h, levels, :] = near[levels, 0, lanes_of(h)]
+            to_east[h, levels, :] = near[levels, ROWS - 1, lanes_of(h)]
+    for b in range(BLOCKS):
+        to_south[rows_of(b), :] = low[b]
+        to_north[rows_of(b), :] = high[b]
+        y_even[rows_of(b), :], y_odd[rows_of(b), :] = sort_out("gy", low[b], high[b])
+    y_even[ROWS:, :] = jnp.zeros((Y_ROWS - ROWS, 128), F32)
+    y_odd[ROWS:, :] = jnp.zeros((Y_ROWS - ROWS, 128), F32)
+    last.wait()
     for h in range(2):
-        to_west[h, 0:40, :] = t_top[:, 0, lanes_of(h)]
-        to_east[h, 0:40, :] = t_end[:, 7, lanes_of(h)]
         to_east[h, 40:80, :] = u_end[:, 7, lanes_of(h)]
-
-
-def pack(temp, speeds, sea, tally):
+    x_even[...], x_odd[...] = sort_out("gx", to_west[...], to_east[...])
+
+
+def pack(*args):
     return pl.pallas_call(
         pack_kernel,
         out_shape=(
-            shape(ROWS, COLS), shape(2, 88, 128), shape(2, 48, 128), shape(ROWS, 128), shape(ROWS, 128)
+            shape(LEVELS, ROWS, COLS), shape(ROWS, COLS),
+            shape(2, 88, 128), shape(2, 88, 128), shape(ROWS, 128), shape(ROWS, 128),
+            shape(Y_ROWS, 128), shape(Y_ROWS, 128), shape(2, 88, 128), shape(2, 88, 128),
         ),
-        in_specs=[HBM, HBM, HBM, HBM],
-        out_specs=(VMEM,) * 5,
+        in_specs=[HBM] * 4,
+        out_specs=(VMEM,) * 10,
         scratch_shapes=[
             pltpu.VMEM((LEVELS, ROWS, 128), F32),
-            pltpu.VMEM((LEVELS, ROWS, 128), F32),
-            pltpu.VMEM((LEVELS, ROWS, 128), F32),
-            pltpu.VMEM((LEVELS, 8, COLS), F32),
-            pltpu.VMEM((LEVELS, 8, COLS), F32),
             pltpu.VMEM((LEVELS, 8, COLS), F32),
             pltpu.VMEM((ROWS, COLS), jnp.int32),
             pltpu.VMEM((ROWS, COLS), jnp.int32),
-            pltpu.SemaphoreType.DMA((8,)),
+            pltpu.SemaphoreType.DMA((3,)),
+            pltpu.SemaphoreType.DMA((2, CHUNKS)),
         ],
         compiler_params=params(LIMIT_PACK),
         name="pack",
-    )(temp, speeds, sea, tally)
+    )(*args)
 
 
 UNROLL_IN = 4
@@ -185,21 +216,10 @@
 
 
 def interior_kernel(
-    temp, speeds, mix, count,
-    source_out, inverse_out, link_out, u_out, v_out,
-    tb, mb, east_lim, north_lim, sems,
+    tb, speeds, mb, count,
+    source_out, inverse_out, link_out,
+    east_lim, north_lim,
 ):
-    def load(which, c):
-        part = pl.ds(c * CHUNK, CHUNK)
-        origin, target = (
-            (mix, mb), (temp, tb), (speeds.at[0], u_out), (speeds.at[1], v_out)
-        )[which]
-        return pltpu.make_async_copy(origin.at[part], target.at[part], sems.at[which, c])
-
-    for c in range(CHUNKS):
-        for which in range(4):
-            load(which, c).start()
-
     lane, row = lane_id(), row_id()
     first_row, last_row = row == 0, row == 7
     first_lane, last_lane = lane == 0, lane == 127
@@ -227,8 +247,8 @@
             if b < BLOCKS - 1:
                 t_next = [tb[k, rows_of(b + 1), lanes_of(h)] for h in pair]
                 turned_next = [pltpu.roll(t_next[h], 7, 0) for h in pair]
-            u = [u_out[k, rows, lanes_of(h)] for h in pair]
-            v = [v_out[k, rows, lanes_of(h)] for h in pair]
+            u = [speeds[0, k, rows, lanes_of(h)] for h in pair]
+            v = [speeds[1, k, rows, lanes_of(h)] for h in pair]
             change = []
             for h in pair:
                 ahead = jnp.where(last_row, turned_next[h], turned[h])
@@ -265,39 +285,24 @@
                 new_links.append(below)
         return tuple(new_factors), tuple(new_links)
 
-    load(0, 0).wait()
-
-    def chunk_step(c, carry):
-        @pl.when(c < CHUNKS - 1)
-        def _():
-            load(0, c + 1).wait()
-
-        for which in range(1, 4):
-            load(which, c).wait()
-
-        def step(m, carry):
-            for n in range(UNROLL_IN):
-                carry = level_step(c * CHUNK + m * UNROLL_IN + n, *carry)
-            return carry
-
-        return lax.fori_loop(0, CHUNK // UNROLL_IN, step, carry)
+    def step(m, carry):
+        for n in range(UNROLL_IN):
+            carry = level_step(m * UNROLL_IN + n, *carry)
+        return carry
 
     blank = tuple(zero for _ in TILES)
-    lax.fori_loop(0, CHUNKS, chunk_step, (blank, blank))
+    lax.fori_loop(0, LEVELS // UNROLL_IN, step, (blank, blank))
 
 
 def interior(temp, speeds, mix, count):
     block = shape(LEVELS, ROWS, COLS)
-    scratch = pltpu.VMEM((LEVELS, ROWS, COLS), F32)
     return pl.pallas_call(
         interior_kernel,
-        out_shape=(block,) * 5,
-        in_specs=[ANY, ANY, ANY, VMEM],
-        out_specs=(VMEM,) * 5,
+        out_shape=(block,) * 3,
+        in_specs=[VMEM] * 4,
+        out_specs=(VMEM,) * 3,
         scratch_shapes=[
-            scratch, scratch,
             pltpu.VMEM((ROWS, COLS), F32), pltpu.VMEM((ROWS, COLS), F32),
-            pltpu.SemaphoreType.DMA((4, CHUNKS)),
         ],
         cost_estimate=pl.CostEstimate(
             flops=30 * LEVELS * ROWS * COLS, bytes_accessed=16 * LEVELS * ROWS * COLS,
@@ -446,7 +451,7 @@
 
 
 def momentum(
-    blocks, values, following, u_in, v_in, east_lim, north_lim, run, u_sum, v_sum, q_col,
+    blocks, values, following, speeds, east_lim, north_lim, run, u_sum, v_sum, q_col,
     keep_u, keep_v, keep_row,
 ):
     lane, row = lane_id(), row_id()
@@ -508,7 +513,7 @@
                 for n in many:
                     ahead = jnp.where(last_row, turned_next[h][n], turned[h][n])
                     speed = jnp.where(
-                        depths[n] < limit, u_in[(levels[n], *at)] - PRESS * (q[h][n] - ahead), 0.0
+                        depths[n] < limit, speeds[(0, levels[n], *at)] - PRESS * (q[h][n] - ahead), 0.0
                     )
                     keep_u(levels[n], b, h, speed)
                     total = total + speed
@@ -518,7 +523,7 @@
                 for n in many:
                     ahead = jnp.where(last_lane, left[1][n] if h == 0 else 0.0, left[h][n])
                     speed = jnp.where(
-                        depths[n] < limit, v_in[(levels[n], *at)] - PRESS * (q[h][n] - ahead), 0.0
+                        depths[n] < limit, speeds[(1, levels[n], *at)] - PRESS * (q[h][n] - ahead), 0.0
                     )
                     keep_v(levels[n], b, h, speed)
                     total = total + speed
@@ -558,12 +563,14 @@
 
 
 def outer_kernel(
-    source, inverse, link, u_in, v_in, count, rain, own_east, own_west, own_north, own_south,
-    west, east, south, north,
-    solved, to_east, to_west,
+    source, inverse, link, speeds, count, rain, own_east, own_west, own_north, own_south,
+    y_odd_in, y_even_in, x_odd_in, x_even_in,
+    solved, to_east, to_west, x_odd, x_even, west, east, south, north,
     row_low, row_high, col_low, col_high, east_lim, north_lim, south_lim, west_lim,
     run, u_sum, v_sum, q_col,
 ):
+    west[...], east[...] = sort_in("gx", x_even_in[...], x_odd_in[...])
+    south[...], north[...] = sort_in("gy", y_even_in[0:ROWS, :], y_odd_in[0:ROWS, :])
     face_limits(
         OUTER, count, west, east, south, north, east_lim, north_lim, south_lim, west_lim
     )
@@ -585,7 +592,7 @@
 
     momentum(
         OUTER, lambda k, b, h: solved[k, place(b), lanes_of(h)], lambda b: False,
-        u_in, v_in, east_lim, north_lim, run, u_sum, v_sum, q_col, drop, drop, keep_row,
+        speeds, east_lim, north_lim, run, u_sum, v_sum, q_col, drop, drop, keep_row,
     )
     row_sum = row_face_sum(west_lim, lambda h: to_west[24 + 40 * h : 64 + 40 * h, :])
     u_sum[rows_of(BLOCKS - 2), :] = jnp.zeros((8, COLS), F32)
@@ -604,6 +611,8 @@
             to_east[16:24, :] = pltpu.roll(side, 5, 0)
 
     forcing(OUTER, u_sum, v_sum, row_sum, south_lim, q_col, count, rain, keep)
+    to_east[24:104, :] = jnp.zeros((80, 128), F32)
+    x_even[...], x_odd[...] = sort_out("gx", to_west[...], to_east[...])
 
 
 def outer(*args):
@@ -612,9 +621,12 @@
     levels = pltpu.VMEM((2, LEVELS, 128), F32)
     return pl.pallas_call(
         outer_kernel,
-        out_shape=(shape(LEVELS, 16, COLS), shape(24, 128), shape(104, 128)),
-        in_specs=[VMEM] * 15,
-        out_specs=(VMEM,) * 3,
+        out_shape=(shape(LEVELS, 16, COLS),)
+        + (shape(104, 128),) * 4
+        + (shape(2, 88, 128),) * 2
+        + (shape(ROWS, 128),) * 2,
+        in_specs=[VMEM] * 14,
+        out_specs=(VMEM,) * 9,
         scratch_shapes=[
             levels, levels, strip, strip, plane, plane, strip, pltpu.VMEM((8, COLS), F32),
             plane, plane, plane, strip,
@@ -625,7 +637,7 @@
 
 
 def middle_kernel(
-    source, inverse, link, u_in, v_in, count, rain, own_north, own_south,
+    source, inverse, link, speeds, count, rain, own_north, own_south,
     west, east, south, north, outside, own_west,
     solved, u_new, v_low, v_high, force_out, q_col, sides,
     col_low, col_high, east_lim, north_lim, south_lim, west_lim, run, u_sum, v_sum,
@@ -660,7 +672,7 @@
             v_high[k, rows_of(b), :] = speed
 
     momentum(
-        every, values, lambda b: b < BLOCKS - 1, u_in, v_in, east_lim, north_lim,
+        every, values, lambda b: b < BLOCKS - 1, speeds, east_lim, north_lim,
         run, u_sum, v_sum, q_col, keep_u, keep_v, lambda k, h, value: None,
     )
     row_sum = [
@@ -685,7 +697,7 @@
             shape(LEVELS, ROWS - 16, COLS), shape(LEVELS, ROWS, COLS), half, half,
             shape(ROWS, COLS), shape(ROWS, 128), shape(ROWS, 128),
         ),
-        in_specs=[VMEM] * 15,
+        in_specs=[VMEM] * 14,
         out_specs=(VMEM,) * 7,
         scratch_shapes=[
             strip, strip, plane, plane, strip, pltpu.VMEM((8, COLS), F32), plane, plane, plane,
@@ -757,9 +769,10 @@
 
 
 def edges_kernel(
-    force, sides, q_col, count, west, east_in, own_east, own_west, from_west, from_east,
-    force_ext, count_ext, sides_ext, to_north, to_south,
+    force, sides, q_col, count, west, east_in, own_east, own_west, x_odd, x_even,
+    force_ext, count_ext, sides_ext, y_odd, y_even, from_east, from_west, to_north, to_south,
 ):
+    from_west[...], from_east[...] = sort_in("gx", x_even[...], x_odd[...])
     zeros8 = jnp.zeros((8, COLS), F32)
     count_ext[0:8, :] = zeros8
     for h in range(2):
@@ -810,16 +823,21 @@
         pltpu.roll(q_col[...], 64, 1),
         to_south[8 : 8 + ROWS, :],
     )
+    y_even[...], y_odd[...] = sort_out("gy", to_south[...], to_north[...])
 
 
 def edges(*args):
     return pl.pallas_call(
         edges_kernel,
         out_shape=(
-            shape(EXT, COLS), shape(EXT, COLS), shape(EXT, 128), shape(EXT, 128), shape(EXT, 128)
+            shape(EXT, COLS), shape(EXT, COLS), shape(EXT, 128), shape(EXT, 128), shape(EXT, 128),
+            shape(104, 128),
         ),
         in_specs=[VMEM] * 10,
-        out_specs=(VMEM,) * 5,
+        out_specs=(VMEM,) * 6,
+        scratch_shapes=[
+            pltpu.VMEM((104, 128), F32), pltpu.VMEM((EXT, 128), F32), pltpu.VMEM((EXT, 128), F32)
+        ],
         compiler_params=params(LIMIT_COLUMNS),
         name="edges",
     )(*args)
@@ -827,9 +845,10 @@
 
 def final_kernel(
     speeds, v_high, count,
-    force_ext, count_ext, sides_ext, south, north,
-    speeds_out, out, v_fix, sem,
+    force_ext, count_ext, sides_ext, y_odd, y_even,
+    speeds_out, out, v_fix, south, north, sem,
 ):
+    south[...], north[...] = sort_in("gy", y_even[...], y_odd[...])
     last_lane = lane_id(8) == 127
     for b in range(BLOCKS):
         rows = rows_of(b)
@@ -899,6 +918,7 @@
         out_specs=(ANY, VMEM),
         scratch_shapes=[
             pltpu.VMEM((LEVELS, ROWS, 128), F32),
+            pltpu.VMEM((EXT, 128), F32), pltpu.VMEM((EXT, 128), F32),
             pltpu.SemaphoreType.DMA,
         ],
         input_output_aliases={0: 0},
@@ -907,9 +927,13 @@
     )(*args)
 
 
-def shift(array, axis, step):
+def swap(array, axis, first):
     count = lax.axis_size(axis)
-    return lax.ppermute(array, axis, [(i, (i + step) % count) for i in range(count)])
+    pairs = []
+    for low in range(first, count + first, 2):
+        low, high = low % count, (low + 1) % count
+        pairs += [(low, high), (high, low)]
+    return lax.ppermute(array, axis, pairs)
 
 
 def local(
@@ -920,7 +944,7 @@
     submerged_layer_tally,
     rainfall_runoff_input,
 ):
-    count, to_east, to_west, to_north, to_south = pack(
+    near, count, to_east, to_west, to_north, to_south, y_odd, y_even, x_odd, x_even = pack(
         *(
             pltpu.with_memory_space_constraint(x, pltpu.HBM)
             for x in (
@@ -928,31 +952,35 @@
             )
         )
     )
-    south = shift(to_north, "gy", 1)
-    north = shift(to_south, "gy", -1)
-    west = shift(to_east, "gx", 1)
-    east = shift(to_west, "gx", -1)
-    inside = interior(thermal_departure, current_speeds, mixing_coefficient, count)
-    outside, own_east, own_west = outer(
+    y_odd = swap(y_odd, "gy", 1)
+    y_even = swap(y_even, "gy", 0)
+    x_odd = swap(x_odd, "gx", 1)
+    x_even = swap(x_even, "gx", 0)
+    speeds, mixing = (
+        pltpu.with_memory_space_constraint(x, pltpu.VMEM)
+        for x in (current_speeds, mixing_coefficient)
+    )
+    inside = (*interior(near, speeds, mixing, count), speeds)
+    outside, own_east, own_west, x_odd, x_even, west, east, south, north = outer(
         *inside, count, rainfall_runoff_input, to_east, to_west, to_north, to_south,
-        west, east, south, north,
-    )
-    from_west = shift(own_east, "gx", 1)
-    from_east = shift(own_west, "gx", -1)
+        y_odd, y_even, x_odd, x_even,
+    )
+    x_odd = swap(x_odd, "gx", 1)
+    x_even = swap(x_even, "gx", 0)
     solved, u_new, v_low, v_high, force, q_col, sides = middle(
         *inside, count, rainfall_runoff_input, to_north, to_south,
         west, east, south, north, outside, own_west,
     )
-    force_ext, count_ext, sides_ext, north_edge, south_edge = edges(
-        force, sides, q_col, count, west, east, own_east, own_west, from_west, from_east
-    )
-    from_south = shift(north_edge, "gy", 1)
-    from_north = shift(south_edge, "gy", -1)
-    temp_next, speeds = writer(
+    force_ext, count_ext, sides_ext, y_odd, y_even, from_east = edges(
+        force, sides, q_col, count, west, east, own_east, own_west, x_odd, x_even
+    )
+    y_odd = swap(y_odd, "gy", 1)
+    y_even = swap(y_even, "gy", 0)
+    temp_next, stored = writer(
         outside, solved, u_new, v_low, from_east, count, east
     )
     velocity_next, surface = final(
-        speeds, v_high, count, force_ext, count_ext, sides_ext, from_south, from_north,
+        stored, v_high, count, force_ext, count_ext, sides_ext, y_odd, y_even,
     )
     return (temp_next, velocity_next, surface)
 

time: 36.5 us -> 32.9 us (0.901)
  starting transfers between devices: 15.5 us -> 12.2 us
  Pallas kernels: 19.7 us -> 17.3 us
  waiting for transfers between devices: 0.42 us -> 2.43 us
    ppermute x8, starting transfers between devices: 15.5 us -> 12.2 us  [swap(): return lax.ppermute(array, axis, pairs)]
    ppermute x8, waiting for transfers between devices: 0.42 us -> 2.43 us  [swap(): return lax.ppermute(array, axis, pairs)]
    pallas_call x3, Pallas kernels: 10.3 us -> 8.71 us  [the longest x1 4.01 us: interior(): pl.pallas_call(interior_kernel, out_shape=(block,) * 3, in_specs=[VMEM] *...]
    pallas_call x1, Pallas kernels: 3.07 us -> 2.31 us  [final(): pl.pallas_call(final_kernel, out_shape=(shape(2, LEVELS, ROWS, COLS), sha...]
  transfers between devices with their start and end apart: 8 -> 8, of which waited for: 1 -> 2; matrix products, arithmetic and copies ran while one was open for 0% -> 0% of each run, Pallas kernels for 33% -> 31%
where the time goes in v4:
time: 32.9 us; the launch traced here: 32.7 us
  Pallas kernels  17.3 us (53%)
  starting transfers between devices  12.2 us (37%)
  waiting for transfers between devices  2.43 us (7%)
  between operations  0.74 us (2%)
    ppermute x8, starting transfers between devices, swap(): return lax.ppermute(array, axis, pairs)  12.2 us
    pallas_call x1, Pallas kernels, interior(): pl.pallas_call(interior_kernel, out_shape=(block,) * 3, in_specs=[VMEM] *...  4.01 us
    pallas_call x1, Pallas kernels, middle(): pl.pallas_call(middle_kernel, out_shape=(shape(LEVELS, ROWS - 16, COLS),...  3.43 us
    pallas_call x1, Pallas kernels, pack(): pl.pallas_call(pack_kernel, out_shape=(shape(LEVELS, ROWS, COLS), shape(R...  3 us
    pallas_call x1, Pallas kernels, writer(): pl.pallas_call(writer_kernel, out_shape=(shape(LEVELS, ROWS, COLS), shape...  2.79 us
    ppermute x8, waiting for transfers between devices, swap(): return lax.ppermute(array, axis, pairs)  2.43 us
    pallas_call x1, Pallas kernels, final(): pl.pallas_call(final_kernel, out_shape=(shape(2, LEVELS, ROWS, COLS), sha...  2.31 us
    pallas_call x1, Pallas kernels, outer(): pl.pallas_call(outer_kernel, out_shape=(shape(LEVELS, 16, COLS),) + (shap...  1.7 us
  transfers between devices with their start and end apart: 8, of which 2 were waited for; matrix products, arithmetic and copies ran while one was open for 0% of the time, Pallas kernels for 31%

profile of v4, /device:TPU:0, one launch (start us, length us, event | category | flops | bytes accessed | tf_op | source)
XLA Modules:
  0.0 32.7 jit_solution(18129494045338771244)
XLA Ops:
  0.6 0.0 copy-start
  0.6 0.0 copy-start.1
  0.7 3.0 %pack.1 = (f32[40,64,256]{2,1,0:T(8,128)S(1)}, f32[64,256]{1,0:T(8,128)S(1)}, f32[2,88,128]{2,1,0:T(8,128)S(1)}, f32[2,88,128]{2,1,0:T(8,128)S(1)}, f32[64,128]{...) custom-call(f32[40,64,256]{2,1,0:T(8,128)} %temp.1, ...), custom_call_target="tpu_custom_call" | custom-call | tf_op jit(solution)/shard_map/pack/pallas_call | solution.py:190
  3.7 6.7 %collective-permute-start = (f32[184,128]{1,0:T(8,128)S(1)}, f32[184,128]{1,0:T(8,128)S(1)}, u32[]{:S(2)}, u32[]{:S(2)}) collective-permute-start(f32[184,128]{1,0:T(8,128)S(1)} %get-tuple-element.51), channel_id=1, source_target_pairs={{1,2},{2,1},{3,4},{4,3},{5,6},{6,5},{7,8},{8,7},{9,10},{10,9},{11,... | collective-permute-start | bytes 282632 | tf_op jit(solution)/shard_map/ppermute | solution.py:936
  10.3 0.0 collective-permute-start.1
  10.3 1.9 %collective-permute-start.2 = (f32[2,88,128]{2,1,0:T(8,128)S(1)}, f32[2,88,128]{2,1,0:T(8,128)S(1)}, u32[]{:S(2)}, u32[]{:S(2)}) collective-permute-start(f32[2,88,128]{2,1,0:T(8,128)S(1)} %get-tuple-element.53), channel_id=1, source_target_pairs={{16,32},{32,16},{48,64},{64,48},{80,96},{96,80},{112,0},{0,112},{1... | collective-permute-start | bytes 270344 | tf_op jit(solution)/shard_map/ppermute | solution.py:936
  12.2 0.0 collective-permute-start.3
  12.2 0.0 copy-done
  12.2 0.0 copy-done.1
  12.2 0.0 copy-start.2
  12.3 4.0 %interior.1 = (f32[40,64,256]{2,1,0:T(8,128)S(1)}, f32[40,64,256]{2,1,0:T(8,128)S(1)}, f32[40,64,256]{2,1,0:T(8,128)S(1)}) custom-call(f32[40,64,256]{2,1,0:T(8,128)S(1)} %get-tuple-element.42.tb, f32[2,40,64,256]{3,2,1,0:T(8,128)S(1)} %copy-done, f32[40,64,256]{2,1,0:T(8,128)S(1)} %copy-done.1, f32[64,256]{1,0:T(8,128)S(1)} %get-tuple-element.43.count), custom_call_target="tpu_custom_call" | custom-call | flops 19660800 | bytes 10485760 | tf_op jit(solution)/shard_map/interior/pallas_call | solution.py:299
  16.3 0.0 collective-permute-done.2.x_odd_in
  16.3 0.0 collective-permute-done.3.x_even_in
  16.3 0.0 collective-permute-done.y_odd_in
  16.3 0.0 collective-permute-done.1.y_even_in
  16.3 0.0 copy-done.2
  16.3 1.7 %outer.1 = (f32[40,16,256]{2,1,0:T(8,128)S(1)}, f32[104,128]{1,0:T(8,128)S(1)}, f32[104,128]{1,0:T(8,128)S(1)}, f32[104,128]{1,0:T(8,128)S(1)}, f32[104,128]{1,0...) custom-call(f32[40,64,256]{2,1,0:T(8,128)S(1)} %get-tuple-element.44, ...), custom_call_target="tpu_custom_call" | custom-call | tf_op jit(solution)/shard_map/outer/pallas_call | solution.py:622
  18.0 1.2 %collective-permute-start.4 = (f32[104,128]{1,0:T(8,128)S(1)}, f32[104,128]{1,0:T(8,128)S(1)}, u32[]{:S(2)}, u32[]{:S(2)}) collective-permute-start(f32[104,128]{1,0:T(8,128)S(1)} %get-tuple-element.68), channel_id=1, source_target_pairs={{16,32},{32,16},{48,64},{64,48},{80,96},{96,80},{112,0},{0,112},{1... | collective-permute-start | bytes 159752 | tf_op jit(solution)/shard_map/ppermute | solution.py:936
  19.2 0.2 collective-permute-start.5
  19.4 3.4 %middle.1 = (f32[40,48,256]{2,1,0:T(8,128)S(1)}, f32[40,64,256]{2,1,0:T(8,128)S(1)}, f32[40,64,128]{2,1,0:T(8,128)S(1)}, f32[40,64,128]{2,1,0:T(8,128)S(1)}, f32...) custom-call(f32[40,64,256]{2,1,0:T(8,128)S(1)} %get-tuple-element.44.source, ...), custom_call_target="tpu_custom_call" | custom-call | flops 19660800 | bytes 10485760 | tf_op jit(solution)/shard_map/middle/pallas_call | solution.py:694
  22.8 0.1 collective-permute-done.4.x_odd
  22.9 0.0 collective-permute-done.5.x_even
  22.9 0.1 edges.1
  23.0 2.2 %collective-permute-start.6 = (f32[80,128]{1,0:T(8,128)S(1)}, f32[80,128]{1,0:T(8,128)S(1)}, u32[]{:S(2)}, u32[]{:S(2)}) collective-permute-start(f32[80,128]{1,0:T(8,128)S(1)} %get-tuple-element.77), channel_id=1, source_target_pairs={{1,2},{2,1},{3,4},{4,3},{5,6},{6,5},{7,8},{8,7},{9,10},{10,9},{11,... | collective-permute-start | bytes 122888 | tf_op jit(solution)/shard_map/ppermute | solution.py:936
  25.2 0.0 collective-permute-start.7
  25.2 2.8 %writer.1 = (f32[40,64,256]{2,1,0:T(8,128)}, f32[2,40,64,256]{3,2,1,0:T(8,128)}) custom-call(f32[40,16,256]{2,1,0:T(8,128)S(1)} %get-tuple-element.55.outside, f32[40,48,256]{2,1,0:T(8,128)S(1)} %get-tuple-element.61.solved, f32[40,64,256]{2,1,0:T(8,128)S(1)} %get-tuple-element.62.u_new, f32[40,64,128]{2,1,0:T(8,128)S(1)} %get-tuple-element.63.v_low, ...), custom_call_target="tpu_custom_call" | custom-call | flops 655360 | bytes 7864320 | tf_op jit(solution)/shard_map/writer/pallas_call | solution.py:750
  28.0 2.4 %collective-permute-done.6.y_odd = f32[80,128]{1,0:T(8,128)S(1)} collective-permute-done((f32[80,128]{1,0:T(8,128)S(1)}, f32[80,128]{1,0:T(8,128)S(1)}, u32[]{:S(2)}, u32[]{:S(2)}) %collective-permute-start.6) | collective-permute-done | bytes 40992 | tf_op jit(solution)/shard_map/ppermute | solution.py:936
  30.4 0.0 collective-permute-done.7.y_even
  30.4 2.3 %final.1 = (f32[2,40,64,256]{3,2,1,0:T(8,128)}, f32[64,256]{1,0:T(8,128)}) custom-call(f32[2,40,64,256]{3,2,1,0:T(8,128)} %get-tuple-element.72.speeds, f32[40,64,128]{2,1,0:T(8,128)S(1)} %get-tuple-element.73.v_high, f32[64,256]{1,0:T(8,128)S(1)} %get-tuple-element.43.count, ...), custom_call_target="tpu_custom_call", output_to_operand_aliasing={{0}: (0, {})} | custom-call | tf_op jit(solution)/shard_map/final/pallas_call | solution.py:914
Async XLA Ops:
  0.6 11.6 %copy-start = (f32[2,40,64,256]{3,2,1,0:T(8,128)S(1)}, f32[2,40,64,256]{3,2,1,0:T(8,128)}, u32[]{:S(2)}) copy-start(f32[2,40,64,256]{3,2,1,0:T(8,128)} %speeds.7) | copy-start | bytes 15728644
  0.6 11.6 %copy-start.1 = (f32[40,64,256]{2,1,0:T(8,128)S(1)}, f32[40,64,256]{2,1,0:T(8,128)}, u32[]{:S(2)}) copy-start(f32[40,64,256]{2,1,0:T(8,128)} %mb.1) | copy-start | bytes 7864324
  3.7 12.6 %collective-permute-start = (f32[184,128]{1,0:T(8,128)S(1)}, f32[184,128]{1,0:T(8,128)S(1)}, u32[]{:S(2)}, u32[]{:S(2)}) collective-permute-start(f32[184,128]{1,0:T(8,128)S(1)} %get-tuple-element.51), channel_id=1, source_target_pairs={{1,2},{2,1},{3,4},{4,3},{5,6},{6,5},{7,8},{8,7},{9,10},{10,9},{11,... | collective-permute-start | bytes 282632 | tf_op jit(solution)/shard_map/ppermute | solution.py:936
  10.3 6.0 %collective-permute-start.1 = (f32[184,128]{1,0:T(8,128)S(1)}, f32[184,128]{1,0:T(8,128)S(1)}, u32[]{:S(2)}, u32[]{:S(2)}) collective-permute-start(f32[184,128]{1,0:T(8,128)S(1)} %get-tuple-element.52), channel_id=1, source_target_pairs={{0,1},{1,0},{2,3},{3,2},{4,5},{5,4},{6,7},{7,6},{8,9},{9,8},{10,11... | collective-permute-start | bytes 282632 | tf_op jit(solution)/shard_map/ppermute | solution.py:936
  10.3 6.0 %collective-permute-start.2 = (f32[2,88,128]{2,1,0:T(8,128)S(1)}, f32[2,88,128]{2,1,0:T(8,128)S(1)}, u32[]{:S(2)}, u32[]{:S(2)}) collective-permute-start(f32[2,88,128]{2,1,0:T(8,128)S(1)} %get-tuple-element.53), channel_id=1, source_target_pairs={{16,32},{32,16},{48,64},{64,48},{80,96},{96,80},{112,0},{0,112},{1... | collective-permute-start | bytes 270344 | tf_op jit(solution)/shard_map/ppermute | solution.py:936
  12.2 4.1 %collective-permute-start.3 = (f32[2,88,128]{2,1,0:T(8,128)S(1)}, f32[2,88,128]{2,1,0:T(8,128)S(1)}, u32[]{:S(2)}, u32[]{:S(2)}) collective-permute-start(f32[2,88,128]{2,1,0:T(8,128)S(1)} %get-tuple-element.54), channel_id=1, source_target_pairs={{0,16},{16,0},{32,48},{48,32},{64,80},{80,64},{96,112},{112,96},{1... | collective-permute-start | bytes 270344 | tf_op jit(solution)/shard_map/ppermute | solution.py:936
  12.2 4.1 %copy-start.2 = (f32[64,256]{1,0:T(8,128)S(1)}, f32[64,256]{1,0:T(8,128)}, u32[]{:S(2)}) copy-start(f32[64,256]{1,0:T(8,128)} %rain.3) | copy-start | bytes 196612
  18.0 4.8 %collective-permute-start.4 = (f32[104,128]{1,0:T(8,128)S(1)}, f32[104,128]{1,0:T(8,128)S(1)}, u32[]{:S(2)}, u32[]{:S(2)}) collective-permute-start(f32[104,128]{1,0:T(8,128)S(1)} %get-tuple-element.68), channel_id=1, source_target_pairs={{16,32},{32,16},{48,64},{64,48},{80,96},{96,80},{112,0},{0,112},{1... | collective-permute-start | bytes 159752 | tf_op jit(solution)/shard_map/ppermute | solution.py:936
  19.2 3.7 %collective-permute-start.5 = (f32[104,128]{1,0:T(8,128)S(1)}, f32[104,128]{1,0:T(8,128)S(1)}, u32[]{:S(2)}, u32[]{:S(2)}) collective-permute-start(f32[104,128]{1,0:T(8,128)S(1)} %get-tuple-element.69), channel_id=1, source_target_pairs={{0,16},{16,0},{32,48},{48,32},{64,80},{80,64},{96,112},{112,96},{1... | collective-permute-start | bytes 159752 | tf_op jit(solution)/shard_map/ppermute | solution.py:936
  23.0 7.4 %collective-permute-start.6 = (f32[80,128]{1,0:T(8,128)S(1)}, f32[80,128]{1,0:T(8,128)S(1)}, u32[]{:S(2)}, u32[]{:S(2)}) collective-permute-start(f32[80,128]{1,0:T(8,128)S(1)} %get-tuple-element.77), channel_id=1, source_target_pairs={{1,2},{2,1},{3,4},{4,3},{5,6},{6,5},{7,8},{8,7},{9,10},{10,9},{11,... | collective-permute-start | bytes 122888 | tf_op jit(solution)/shard_map/ppermute | solution.py:936
  25.2 5.2 %collective-permute-start.7 = (f32[80,128]{1,0:T(8,128)S(1)}, f32[80,128]{1,0:T(8,128)S(1)}, u32[]{:S(2)}, u32[]{:S(2)}) collective-permute-start(f32[80,128]{1,0:T(8,128)S(1)} %get-tuple-element.78), channel_id=1, source_target_pairs={{0,1},{1,0},{2,3},{3,2},{4,5},{5,4},{6,7},{7,6},{8,9},{9,8},{10,11... | collective-permute-start | bytes 122888 | tf_op jit(solution)/shard_map/ppermute | solution.py:936

commit v5 on v4

--- a/solution.py
+++ b/solution.py
@@ -6,7 +6,8 @@
 from jax.sharding import PartitionSpec as P
 
 ITERS = 6
-Y_ROWS = 184
+FIX_CHUNK = 20
+COST = 10000
 LIMIT_PACK = 12
 LIMIT_INTERIOR = 8
 LIMIT_COLUMNS = 12
@@ -178,8 +179,6 @@
         to_south[rows_of(b), :] = low[b]
         to_north[rows_of(b), :] = high[b]
         y_even[rows_of(b), :], y_odd[rows_of(b), :] = sort_out("gy", low[b], high[b])
-    y_even[ROWS:, :] = jnp.zeros((Y_ROWS - ROWS, 128), F32)
-    y_odd[ROWS:, :] = jnp.zeros((Y_ROWS - ROWS, 128), F32)
     last.wait()
     for h in range(2):
         to_east[h, 40:80, :] = u_end[:, 7, lanes_of(h)]
@@ -192,7 +191,7 @@
         out_shape=(
             shape(LEVELS, ROWS, COLS), shape(ROWS, COLS),
             shape(2, 88, 128), shape(2, 88, 128), shape(ROWS, 128), shape(ROWS, 128),
-            shape(Y_ROWS, 128), shape(Y_ROWS, 128), shape(2, 88, 128), shape(2, 88, 128),
+            shape(ROWS, 128), shape(ROWS, 128), shape(2, 88, 128), shape(2, 88, 128),
         ),
         in_specs=[HBM] * 4,
         out_specs=(VMEM,) * 10,
@@ -213,6 +212,7 @@
 UNROLL_FWD = 20
 UNROLL_BACK = 20
 UNROLL_MOM = 5
+UNROLL_OUT = 40
 
 
 def interior_kernel(
@@ -234,13 +234,13 @@
     for b, h in TILES:
         north_lim[rows_of(b), lanes_of(h)] = jnp.minimum(counts[b, h], ahead[b, h])
 
-    def level_step(k, factors, links):
+    def level_step(k, factors, links, opens=None):
         level = k.astype(F32)
         below_at = jnp.minimum(k + 1, LEVELS - 1)
         t_next = [tb[k, rows_of(0), lanes_of(h)] for h in pair]
         turned_next = [pltpu.roll(t_next[h], 7, 0) for h in pair]
         flux_turned = [zero, zero]
-        new_factors, new_links = [], []
+        new_factors, new_links, new_opens = [], [], []
         for b in range(BLOCKS):
             rows = rows_of(b)
             t, turned = t_next, turned_next
@@ -271,11 +271,11 @@
                 at = (k, rows, lanes_of(h))
                 wet = count[rows, lanes_of(h)]
                 total = change[h] + (flux[h] - behind[h])
-                source_out[at] = t[h] - jnp.where(level < wet, advect_scale * total, 0.0)
+                open_here = level < wet if opens is None else opens[n]
+                open_below = level + 1.0 < wet
+                source_out[at] = t[h] - jnp.where(open_here, advect_scale * total, 0.0)
                 a = links[n]
-                below = jnp.where(
-                    level + 1.0 < wet, mb[below_at, rows, lanes_of(h)], 0.0
-                )
+                below = jnp.where(open_below, mb[below_at, rows, lanes_of(h)], 0.0)
                 pivot = (1.0 + below) + (a - a * factors[n])
                 inverse = pl.reciprocal(pivot, approx=True)
                 inverse = inverse * (2.0 - pivot * inverse)
@@ -283,12 +283,13 @@
                 link_out[at] = a
                 new_factors.append(below * inverse)
                 new_links.append(below)
-        return tuple(new_factors), tuple(new_links)
+                new_opens.append(open_below)
+        return tuple(new_factors), tuple(new_links), new_opens
 
     def step(m, carry):
         for n in range(UNROLL_IN):
             carry = level_step(m * UNROLL_IN + n, *carry)
-        return carry
+        return carry[:2]
 
     blank = tuple(zero for _ in TILES)
     lax.fori_loop(0, LEVELS // UNROLL_IN, step, (blank, blank))
@@ -305,7 +306,7 @@
             pltpu.VMEM((ROWS, COLS), F32), pltpu.VMEM((ROWS, COLS), F32),
         ],
         cost_estimate=pl.CostEstimate(
-            flops=30 * LEVELS * ROWS * COLS, bytes_accessed=16 * LEVELS * ROWS * COLS,
+            flops=COST * LEVELS * ROWS * COLS, bytes_accessed=COST * LEVELS * ROWS * COLS,
             transcendentals=0,
         ),
         compiler_params=params(LIMIT_INTERIOR),
@@ -405,7 +406,8 @@
                     total = total + jnp.where(first_row, spread(row_low, k, h), 0.0)
                 if b == BLOCKS - 1:
                     total = total + jnp.where(last_row, spread(row_high, k, h), 0.0)
-                value = (total + link[at] * values[2 * n + h]) * inverse[at]
+                turn = inverse[at]
+                value = total * turn + (link[at] * turn) * values[2 * n + h]
                 solved[k, place(b), lanes_of(h)] = value
                 out.append(value)
         return tuple(out)
@@ -419,18 +421,19 @@
 
     lax.fori_loop(0, LEVELS // UNROLL_FWD, forward_step, blank)
 
-    def back_step(m, linked):
+    def back_step(m, below):
         for n in range(UNROLL_BACK):
             k = LEVELS - 1 - m * UNROLL_BACK - n
+            below_at = jnp.minimum(k + 1, LEVELS - 1)
             out = []
-            for i, below in zip([(b, h) for b in blocks for h in pair], linked):
-                at = (k, rows_of(i[0]), lanes_of(i[1]))
+            for i, value in zip([(b, h) for b in blocks for h in pair], below):
+                at = (rows_of(i[0]), lanes_of(i[1]))
                 to = (k, place(i[0]), lanes_of(i[1]))
-                value = solved[to] + inverse[at] * below
+                value = solved[to] + (inverse[(k, *at)] * link[(below_at, *at)]) * value
                 solved[to] = value
-                out.append(link[at] * value)
-            linked = tuple(out)
-        return linked
+                out.append(value)
+            below = tuple(out)
+        return below
 
     lax.fori_loop(0, LEVELS // UNROLL_BACK, back_step, blank)
 
@@ -452,13 +455,13 @@
 
 def momentum(
     blocks, values, following, speeds, east_lim, north_lim, run, u_sum, v_sum, q_col,
-    keep_u, keep_v, keep_row,
+    keep_u, keep_v, keep_row, unroll,
 ):
     lane, row = lane_id(), row_id()
     last_row, last_lane = row == 7, lane == 127
     zero = jnp.zeros((8, 128), F32)
     pair = range(2)
-    many = range(UNROLL_MOM)
+    many = range(unroll)
     for b in blocks:
         run[rows_of(b), :] = jnp.zeros((8, COLS), F32)
         u_sum[rows_of(b), :] = jnp.zeros((8, COLS), F32)
@@ -466,7 +469,7 @@
         q_col[rows_of(b), :] = zero
 
     def step(m, _):
-        first = m * UNROLL_MOM
+        first = m * unroll
         levels = [first + n for n in many]
         depths = [k.astype(F32) for k in levels]
 
@@ -500,7 +503,7 @@
                 q_next = running(b + 1)
                 turned_next = [[pltpu.roll(x, 7, 0) for x in q_next[h]] for h in pair]
             else:
-                q_next, turned_next = None, [[zero] * UNROLL_MOM] * 2
+                q_next, turned_next = None, [[zero] * unroll] * 2
             left = [[pltpu.roll(x, 127, 1) for x in q[h]] for h in pair]
             column = q_col[rows, :]
             for n in many:
@@ -530,7 +533,7 @@
                 v_sum[at] = total
         return 0
 
-    lax.fori_loop(0, LEVELS // UNROLL_MOM, step, 0)
+    lax.fori_loop(0, LEVELS // unroll, step, 0)
 
 
 def forcing(blocks, u_sum, v_sum, row_sum, south_lim, q_col, count, rain, keep):
@@ -570,7 +573,7 @@
     run, u_sum, v_sum, q_col,
 ):
     west[...], east[...] = sort_in("gx", x_even_in[...], x_odd_in[...])
-    south[...], north[...] = sort_in("gy", y_even_in[0:ROWS, :], y_odd_in[0:ROWS, :])
+    south[...], north[...] = sort_in("gy", y_even_in[...], y_odd_in[...])
     face_limits(
         OUTER, count, west, east, south, north, east_lim, north_lim, south_lim, west_lim
     )
@@ -593,6 +596,7 @@
     momentum(
         OUTER, lambda k, b, h: solved[k, place(b), lanes_of(h)], lambda b: False,
         speeds, east_lim, north_lim, run, u_sum, v_sum, q_col, drop, drop, keep_row,
+        UNROLL_OUT,
     )
     row_sum = row_face_sum(west_lim, lambda h: to_west[24 + 40 * h : 64 + 40 * h, :])
     u_sum[rows_of(BLOCKS - 2), :] = jnp.zeros((8, COLS), F32)
@@ -674,6 +678,7 @@
     momentum(
         every, values, lambda b: b < BLOCKS - 1, speeds, east_lim, north_lim,
         run, u_sum, v_sum, q_col, keep_u, keep_v, lambda k, h, value: None,
+        UNROLL_MOM,
     )
     row_sum = [
         jnp.broadcast_to(own_west[8 * h + 5 : 8 * h + 6, :], (8, 128)) for h in range(2)
@@ -711,8 +716,35 @@
     )(*args)
 
 
+EXT = ROWS + 16
+
+
+def relax(force, count):
+    wide = force.shape[1]
+    root = jnp.sqrt(count * (1.0 / LEVELS))
+
+    def total(field):
+        sideways = pltpu.roll(field, 1, 1) + pltpu.roll(field, wide - 1, 1)
+        mixed = field + 0.5 * sideways
+        return sideways + (pltpu.roll(mixed, 1, 0) + pltpu.roll(mixed, EXT - 1, 0))
+
+    inverse = 1.0 / (damping + root * total(root))
+    force = force * inverse
+    share = root * inverse
+    update = force * (1.0 / cheb_gamma)
+    iterate = update
+    omega = 2.0 / cheb_gamma
+    for step in range(1, ITERS):
+        residual = (force - iterate) + share * total(root * iterate)
+        omega = 1.0 / (cheb_gamma - omega / (4.0 * cheb_alpha * cheb_alpha))
+        update = omega * residual + (cheb_gamma * omega - 1.0) * update
+        iterate = iterate + update
+    return iterate
+
+
 def writer_kernel(
-    outside, solved, u_new, v_low, from_east, count, east, temp_out, speeds_out, u_fix, sems
+    outside, solved, u_new, v_low, from_east, count, east, force_ext, count_ext,
+    temp_out, speeds_out, inner, u_fix, sems,
 ):
     copies = [
         (outside.at[:, pl.ds(0, 8), :], temp_out.at[:, pl.ds(0, 8), :]),
@@ -742,6 +774,7 @@
                 0.0,
             )
     copies[-1].start()
+    inner[...] = relax(force_ext[...], count_ext[...])[8 : 8 + ROWS]
     for copy in copies:
         copy.wait()
 
@@ -749,9 +782,11 @@
 def writer(*args):
     return pl.pallas_call(
         writer_kernel,
-        out_shape=(shape(LEVELS, ROWS, COLS), shape(2, LEVELS, ROWS, COLS)),
-        in_specs=[VMEM] * 7,
-        out_specs=(ANY, ANY),
+        out_shape=(
+            shape(LEVELS, ROWS, COLS), shape(2, LEVELS, ROWS, COLS), shape(ROWS, COLS)
+        ),
+        in_specs=[VMEM] * 9,
+        out_specs=(ANY, ANY, VMEM),
         scratch_shapes=[
             pltpu.VMEM((LEVELS, 8, COLS), F32),
             pltpu.SemaphoreType.DMA((6,)),
@@ -763,9 +798,6 @@
         compiler_params=params(LIMIT_COLUMNS),
         name="writer",
     )(*args)
-
-
-EXT = ROWS + 16
 
 
 def edges_kernel(
@@ -844,82 +876,89 @@
 
 
 def final_kernel(
-    speeds, v_high, count,
-    force_ext, count_ext, sides_ext, y_odd, y_even,
-    speeds_out, out, v_fix, south, north, sem,
+    speeds, v_high, count, inner, force_ext, count_ext, sides_ext, y_odd, y_even,
+    speeds_out, out, v_fix, south, north, sems,
 ):
     south[...], north[...] = sort_in("gy", y_even[...], y_odd[...])
     last_lane = lane_id(8) == 127
+    limits = []
     for b in range(BLOCKS):
-        rows = rows_of(b)
-        held = north[8 * b + 8 : 8 * b + 16, :]
-        limit = jnp.minimum(count[rows, 128:], pltpu.roll(held, 127 - 8, 1))
-        limit = jnp.where(last_lane, limit, 0.0)
-        for k in range(LEVELS):
-            v_fix[k, rows, :] = v_high[k, rows, :] + jnp.where(
-                float(k) < limit, PRESS * pltpu.roll(held, 63 - k, 1), 0.0
+        limit = jnp.minimum(
+            count[rows_of(b), 128:], pltpu.roll(north[rows_of(b + 1), :], 127 - 8, 1)
+        )
+        limits.append(jnp.where(last_lane, limit, 0.0))
+
+    def save(c):
+        part = pl.ds(c * FIX_CHUNK, FIX_CHUNK)
+        return pltpu.make_async_copy(
+            v_fix.at[part], speeds_out.at[1, part, :, pl.ds(128, 128)], sems.at[c]
+        )
+
+    for c in range(LEVELS // FIX_CHUNK):
+        for k in range(c * FIX_CHUNK, (c + 1) * FIX_CHUNK):
+            for b in range(BLOCKS):
+                rows = rows_of(b)
+                v_fix[k, rows, :] = v_high[k, rows, :] + jnp.where(
+                    float(k) < limits[b],
+                    PRESS * pltpu.roll(north[rows_of(b + 1), :], 63 - k, 1),
+                    0.0,
+                )
+        save(c).start()
+
+    @pl.when(lax.axis_index("gx") >= 0)
+    def _():
+        lane = lane_id(EXT)
+        count_side = jnp.where(
+            lane >= 122,
+            pltpu.roll(south[...], 6, 1),
+            jnp.where(lane < 6, pltpu.roll(north[...], 120, 1), 0.0),
+        )
+        force_side = jnp.where(
+            lane >= 123, south[...], jnp.where(lane < 5, north[...], 0.0)
+        )
+        side = sides_ext[...]
+        low, high = force_ext[:, :128], force_ext[:, 128:]
+        low = low + jnp.where(
+            (lane == 0) & (count_ext[:, :128] > 0.0), DIVERGE * south[...], 0.0
+        )
+        high = high - jnp.where(
+            (lane == 127) & (count_ext[:, 128:] > 0.0), DIVERGE * north[...], 0.0
+        )
+        force_side = force_side + jnp.where(
+            (lane == 0) & (count_side > 0.0), DIVERGE * side, 0.0
+        )
+        force_side = force_side - jnp.where(
+            (lane == 127) & (count_side > 0.0), DIVERGE * side, 0.0
+        )
+        left = (lane < 32) | (lane >= 96)
+
+        def strip(low, high, side):
+            return jnp.where(
+                left,
+                jnp.where(lane < 64, low, side),
+                pltpu.roll(jnp.where(lane >= 64, high, side), 64, 1),
             )
-    save_cols = pltpu.make_async_copy(
-        v_fix, speeds_out.at[1, :, :, pl.ds(128, 128)], sem
-    )
-    save_cols.start()
-    lane = lane_id(EXT)
-    count_side = jnp.where(
-        lane >= 122,
-        pltpu.roll(south[...], 6, 1),
-        jnp.where(lane < 6, pltpu.roll(north[...], 120, 1), 0.0),
-    )
-    force_side = jnp.where(
-        lane >= 123, south[...], jnp.where(lane < 5, north[...], 0.0)
-    )
-    side = sides_ext[...]
-    low, high = force_ext[:, :128], force_ext[:, 128:]
-    low = low + jnp.where(
-        (lane == 0) & (count_ext[:, :128] > 0.0), DIVERGE * south[...], 0.0
-    )
-    high = high - jnp.where(
-        (lane == 127) & (count_ext[:, 128:] > 0.0), DIVERGE * north[...], 0.0
-    )
-    force_side = force_side + jnp.where(
-        (lane == 0) & (count_side > 0.0), DIVERGE * side, 0.0
-    )
-    force_side = force_side - jnp.where(
-        (lane == 127) & (count_side > 0.0), DIVERGE * side, 0.0
-    )
-    force = jnp.concatenate([low, high, force_side], axis=1)
-    count = jnp.concatenate([count_ext[...], count_side], axis=1)
-    root = jnp.sqrt(count * (1.0 / LEVELS))
-    wide = COLS + 128
-
-    def total(field):
-        sideways = pltpu.roll(field, 1, 1) + pltpu.roll(field, wide - 1, 1)
-        mixed = field + 0.5 * sideways
-        return sideways + (pltpu.roll(mixed, 1, 0) + pltpu.roll(mixed, EXT - 1, 0))
-
-    diag = damping + root * total(root)
-    inverse = 1.0 / diag
-    update = inverse * force * (1.0 / cheb_gamma)
-    iterate = update
-    omega = 2.0 / cheb_gamma
-    for step in range(1, ITERS):
-        residual = force - (diag * iterate - root * total(root * iterate))
-        omega = 1.0 / (cheb_gamma - omega / (4.0 * cheb_alpha * cheb_alpha))
-        update = omega * inverse * residual + (cheb_gamma * omega - 1.0) * update
-        iterate = iterate + update
-    out[...] = iterate[8 : 8 + ROWS, 0:COLS]
-    save_cols.wait()
+
+        near = relax(
+            strip(low, high, force_side), strip(count_ext[:, :128], count_ext[:, 128:], count_side)
+        )[8 : 8 + ROWS]
+        lane = lane_id(ROWS)
+        out[:, :128] = jnp.where(lane < 6, near, inner[:, :128])
+        out[:, 128:] = jnp.where(lane >= 122, pltpu.roll(near, 64, 1), inner[:, 128:])
+    for c in range(LEVELS // FIX_CHUNK):
+        save(c).wait()
 
 
 def final(*args):
     return pl.pallas_call(
         final_kernel,
         out_shape=(shape(2, LEVELS, ROWS, COLS), shape(ROWS, COLS)),
-        in_specs=[ANY] + [VMEM] * 7,
+        in_specs=[ANY] + [VMEM] * 8,
         out_specs=(ANY, VMEM),
         scratch_shapes=[
             pltpu.VMEM((LEVELS, ROWS, 128), F32),
             pltpu.VMEM((EXT, 128), F32), pltpu.VMEM((EXT, 128), F32),
-            pltpu.SemaphoreType.DMA,
+            pltpu.SemaphoreType.DMA((LEVELS // FIX_CHUNK,)),
         ],
         input_output_aliases={0: 0},
         compiler_params=params(LIMIT_COLUMNS),
@@ -976,11 +1015,11 @@
     )
     y_odd = swap(y_odd, "gy", 1)
     y_even = swap(y_even, "gy", 0)
-    temp_next, stored = writer(
-        outside, solved, u_new, v_low, from_east, count, east
+    temp_next, stored, inner = writer(
+        outside, solved, u_new, v_low, from_east, count, east, force_ext, count_ext
     )
     velocity_next, surface = final(
-        stored, v_high, count, force_ext, count_ext, sides_ext, y_odd, y_even,
+        stored, v_high, count, inner, force_ext, count_ext, sides_ext, y_odd, y_even,
     )
     return (temp_next, velocity_next, surface)
 

time: 32.9 us -> 32.1 us (0.976)
  Pallas kernels: 17.3 us -> 16.6 us
    pallas_call x1, Pallas kernels: 1.7 us -> 1.29 us  [outer(): pl.pallas_call(outer_kernel, out_shape=(shape(LEVELS, 16, COLS),) + (shap...]
    pallas_call x1, Pallas kernels: 2.31 us -> 1.96 us  [final(): pl.pallas_call(final_kernel, out_shape=(shape(2, LEVELS, ROWS, COLS), sha...]
  transfers between devices with their start and end apart: 8 -> 8, of which waited for: 2 -> 2; matrix products, arithmetic and copies ran while one was open for 0% -> 0% of each run, Pallas kernels for 31% -> 32%
where the time goes in v5:
time: 32.1 us; the launch traced here: 32 us
  Pallas kernels  16.6 us (52%)
  starting transfers between devices  12 us (37%)
  waiting for transfers between devices  2.59 us (8%)
  between operations  0.74 us (2%)
    ppermute x8, starting transfers between devices, swap(): return lax.ppermute(array, axis, pairs)  12 us
    pallas_call x1, Pallas kernels, interior(): pl.pallas_call(interior_kernel, out_shape=(block,) * 3, in_specs=[VMEM] *...  4.06 us
    pallas_call x1, Pallas kernels, middle(): pl.pallas_call(middle_kernel, out_shape=(shape(LEVELS, ROWS - 16, COLS),...  3.37 us
    pallas_call x1, Pallas kernels, pack(): pl.pallas_call(pack_kernel, out_shape=(shape(LEVELS, ROWS, COLS), shape(R...  2.99 us
    pallas_call x1, Pallas kernels, writer(): pl.pallas_call(writer_kernel, out_shape=(shape(LEVELS, ROWS, COLS), shape...  2.83 us
    ppermute x8, waiting for transfers between devices, swap(): return lax.ppermute(array, axis, pairs)  2.59 us
    pallas_call x1, Pallas kernels, final(): pl.pallas_call(final_kernel, out_shape=(shape(2, LEVELS, ROWS, COLS), sha...  1.96 us
    pallas_call x1, Pallas kernels, outer(): pl.pallas_call(outer_kernel, out_shape=(shape(LEVELS, 16, COLS),) + (shap...  1.29 us
  transfers between devices with their start and end apart: 8, of which 2 were waited for; matrix products, arithmetic and copies ran while one was open for 0% of the time, Pallas kernels for 32%

profile of v5, /device:TPU:0, one launch (start us, length us, event | category | flops | bytes accessed | tf_op | source)
XLA Modules:
  0.0 32.0 jit_solution(15316930009822836500)
XLA Ops:
  0.6 0.0 copy-start
  0.6 0.0 copy-start.2
  0.7 3.0 %pack.1 = (f32[40,64,256]{2,1,0:T(8,128)S(1)}, f32[64,256]{1,0:T(8,128)S(1)}, f32[2,88,128]{2,1,0:T(8,128)S(1)}, f32[2,88,128]{2,1,0:T(8,128)S(1)}, f32[64,128]{...) custom-call(f32[40,64,256]{2,1,0:T(8,128)} %temp.1, ...), custom_call_target="tpu_custom_call" | custom-call | tf_op jit(solution)/shard_map/pack/pallas_call | solution.py:189
  3.7 6.7 %collective-permute-start = (f32[64,128]{1,0:T(8,128)S(1)}, f32[64,128]{1,0:T(8,128)S(1)}, u32[]{:S(2)}, u32[]{:S(2)}) collective-permute-start(f32[64,128]{1,0:T(8,128)S(1)} %get-tuple-element.52), channel_id=1, source_target_pairs={{1,2},{2,1},{3,4},{4,3},{5,6},{6,5},{7,8},{8,7},{9,10},{10,9},{11,... | collective-permute-start | bytes 98312 | tf_op jit(solution)/shard_map/ppermute | solution.py:975
  10.3 0.0 collective-permute-start.1
  10.3 1.9 %collective-permute-start.2 = (f32[2,88,128]{2,1,0:T(8,128)S(1)}, f32[2,88,128]{2,1,0:T(8,128)S(1)}, u32[]{:S(2)}, u32[]{:S(2)}) collective-permute-start(f32[2,88,128]{2,1,0:T(8,128)S(1)} %get-tuple-element.54), channel_id=1, source_target_pairs={{16,32},{32,16},{48,64},{64,48},{80,96},{96,80},{112,0},{0,112},{1... | collective-permute-start | bytes 270344 | tf_op jit(solution)/shard_map/ppermute | solution.py:975
  12.2 0.0 collective-permute-start.3
  12.2 0.0 copy-done
  12.2 0.0 copy-done.2
  12.2 0.0 copy-start.1
  12.2 4.1 %interior.1 = (f32[40,64,256]{2,1,0:T(8,128)S(1)}, f32[40,64,256]{2,1,0:T(8,128)S(1)}, f32[40,64,256]{2,1,0:T(8,128)S(1)}) custom-call(f32[40,64,256]{2,1,0:T(8,128)S(1)} %get-tuple-element.43.tb, f32[2,40,64,256]{3,2,1,0:T(8,128)S(1)} %copy-done, f32[40,64,256]{2,1,0:T(8,128)S(1)} %copy-done.2, f32[64,256]{1,0:T(8,128)S(1)} %get-tuple-element.44.count), custom_call_target="tpu_custom_call" | custom-call | flops 6553600000 | bytes 6553600000 | tf_op jit(solution)/shard_map/interior/pallas_call | solution.py:300
  16.3 0.0 collective-permute-done.y_odd_in
  16.3 0.0 collective-permute-done.1.y_even_in
  16.3 0.0 collective-permute-done.2.x_odd_in
  16.3 0.0 collective-permute-done.3.x_even_in
  16.4 0.0 copy-done.1
  16.4 1.3 %outer.1 = (f32[40,16,256]{2,1,0:T(8,128)S(1)}, f32[104,128]{1,0:T(8,128)S(1)}, f32[104,128]{1,0:T(8,128)S(1)}, f32[104,128]{1,0:T(8,128)S(1)}, f32[104,128]{1,0...) custom-call(f32[40,64,256]{2,1,0:T(8,128)S(1)} %get-tuple-element.45, ...), custom_call_target="tpu_custom_call" | custom-call | tf_op jit(solution)/shard_map/outer/pallas_call | solution.py:626
  17.7 1.1 %collective-permute-start.4 = (f32[104,128]{1,0:T(8,128)S(1)}, f32[104,128]{1,0:T(8,128)S(1)}, u32[]{:S(2)}, u32[]{:S(2)}) collective-permute-start(f32[104,128]{1,0:T(8,128)S(1)} %get-tuple-element.69), channel_id=1, source_target_pairs={{16,32},{32,16},{48,64},{64,48},{80,96},{96,80},{112,0},{0,112},{1... | collective-permute-start | bytes 159752 | tf_op jit(solution)/shard_map/ppermute | solution.py:975
  18.8 0.2 collective-permute-start.5
  19.0 3.4 %middle.1 = (f32[40,48,256]{2,1,0:T(8,128)S(1)}, f32[40,64,256]{2,1,0:T(8,128)S(1)}, f32[40,64,128]{2,1,0:T(8,128)S(1)}, f32[40,64,128]{2,1,0:T(8,128)S(1)}, f32...) custom-call(f32[40,64,256]{2,1,0:T(8,128)S(1)} %get-tuple-element.45.source, ...), custom_call_target="tpu_custom_call" | custom-call | flops 19660800 | bytes 10485760 | tf_op jit(solution)/shard_map/middle/pallas_call | solution.py:699
  22.4 0.1 collective-permute-done.4.x_odd
  22.5 0.0 collective-permute-done.5.x_even
  22.5 0.1 edges.1
  22.6 1.5 %collective-permute-start.6 = (f32[80,128]{1,0:T(8,128)S(1)}, f32[80,128]{1,0:T(8,128)S(1)}, u32[]{:S(2)}, u32[]{:S(2)}) collective-permute-start(f32[80,128]{1,0:T(8,128)S(1)} %get-tuple-element.79), channel_id=1, source_target_pairs={{1,2},{2,1},{3,4},{4,3},{5,6},{6,5},{7,8},{8,7},{9,10},{10,9},{11,... | collective-permute-start | bytes 122888 | tf_op jit(solution)/shard_map/ppermute | solution.py:975
  24.1 0.6 %collective-permute-start.7 = (f32[80,128]{1,0:T(8,128)S(1)}, f32[80,128]{1,0:T(8,128)S(1)}, u32[]{:S(2)}, u32[]{:S(2)}) collective-permute-start(f32[80,128]{1,0:T(8,128)S(1)} %get-tuple-element.80), channel_id=1, source_target_pairs={{0,1},{1,0},{2,3},{3,2},{4,5},{5,4},{6,7},{7,6},{8,9},{9,8},{10,11... | collective-permute-start | bytes 122888 | tf_op jit(solution)/shard_map/ppermute | solution.py:975
  24.7 2.8 %writer.1 = (f32[40,64,256]{2,1,0:T(8,128)}, f32[2,40,64,256]{3,2,1,0:T(8,128)}, f32[64,256]{1,0:T(8,128)S(1)}) custom-call(f32[40,16,256]{2,1,0:T(8,128)S(1)} %get-tuple-element.56.outside, f32[40,48,256]{2,1,0:T(8,128)S(1)} %get-tuple-element.62.solved, f32[40,64,256]{2,1,0:T(8,128)S(1)} %get-tuple-element.63.u_new, ...), custom_call_target="tpu_custom_call" | custom-call | flops 655360 | bytes 7864320 | tf_op jit(solution)/shard_map/writer/pallas_call | solution.py:783
  27.6 2.5 %collective-permute-done.6.y_odd = f32[80,128]{1,0:T(8,128)S(1)} collective-permute-done((f32[80,128]{1,0:T(8,128)S(1)}, f32[80,128]{1,0:T(8,128)S(1)}, u32[]{:S(2)}, u32[]{:S(2)}) %collective-permute-start.6) | collective-permute-done | bytes 40992 | tf_op jit(solution)/shard_map/ppermute | solution.py:975
  30.0 0.0 collective-permute-done.7.y_even
  30.0 2.0 %final.1 = (f32[2,40,64,256]{3,2,1,0:T(8,128)}, f32[64,256]{1,0:T(8,128)}) custom-call(f32[2,40,64,256]{3,2,1,0:T(8,128)} %get-tuple-element.75.speeds, f32[40,64,128]{2,1,0:T(8,128)S(1)} %get-tuple-element.76.v_high, f32[64,256]{1,0:T(8,128)S(1)} %get-tuple-element.44.count, ...), custom_call_target="tpu_custom_call", output_to_operand_aliasing={{0}: (0, {})} | custom-call | tf_op jit(solution)/shard_map/final/pallas_call | solution.py:953
Async XLA Ops:
  0.6 11.6 %copy-start = (f32[2,40,64,256]{3,2,1,0:T(8,128)S(1)}, f32[2,40,64,256]{3,2,1,0:T(8,128)}, u32[]{:S(2)}) copy-start(f32[2,40,64,256]{3,2,1,0:T(8,128)} %speeds.7) | copy-start | bytes 15728644
  0.6 11.6 %copy-start.2 = (f32[40,64,256]{2,1,0:T(8,128)S(1)}, f32[40,64,256]{2,1,0:T(8,128)}, u32[]{:S(2)}) copy-start(f32[40,64,256]{2,1,0:T(8,128)} %mb.1) | copy-start | bytes 7864324
  3.7 12.7 %collective-permute-start = (f32[64,128]{1,0:T(8,128)S(1)}, f32[64,128]{1,0:T(8,128)S(1)}, u32[]{:S(2)}, u32[]{:S(2)}) collective-permute-start(f32[64,128]{1,0:T(8,128)S(1)} %get-tuple-element.52), channel_id=1, source_target_pairs={{1,2},{2,1},{3,4},{4,3},{5,6},{6,5},{7,8},{8,7},{9,10},{10,9},{11,... | collective-permute-start | bytes 98312 | tf_op jit(solution)/shard_map/ppermute | solution.py:975
  10.3 6.0 %collective-permute-start.1 = (f32[64,128]{1,0:T(8,128)S(1)}, f32[64,128]{1,0:T(8,128)S(1)}, u32[]{:S(2)}, u32[]{:S(2)}) collective-permute-start(f32[64,128]{1,0:T(8,128)S(1)} %get-tuple-element.53), channel_id=1, source_target_pairs={{0,1},{1,0},{2,3},{3,2},{4,5},{5,4},{6,7},{7,6},{8,9},{9,8},{10,11... | collective-permute-start | bytes 98312 | tf_op jit(solution)/shard_map/ppermute | solution.py:975
  10.3 6.0 %collective-permute-start.2 = (f32[2,88,128]{2,1,0:T(8,128)S(1)}, f32[2,88,128]{2,1,0:T(8,128)S(1)}, u32[]{:S(2)}, u32[]{:S(2)}) collective-permute-start(f32[2,88,128]{2,1,0:T(8,128)S(1)} %get-tuple-element.54), channel_id=1, source_target_pairs={{16,32},{32,16},{48,64},{64,48},{80,96},{96,80},{112,0},{0,112},{1... | collective-permute-start | bytes 270344 | tf_op jit(solution)/shard_map/ppermute | solution.py:975
  12.2 4.1 %collective-permute-start.3 = (f32[2,88,128]{2,1,0:T(8,128)S(1)}, f32[2,88,128]{2,1,0:T(8,128)S(1)}, u32[]{:S(2)}, u32[]{:S(2)}) collective-permute-start(f32[2,88,128]{2,1,0:T(8,128)S(1)} %get-tuple-element.55), channel_id=1, source_target_pairs={{0,16},{16,0},{32,48},{48,32},{64,80},{80,64},{96,112},{112,96},{1... | collective-permute-start | bytes 270344 | tf_op jit(solution)/shard_map/ppermute | solution.py:975
  12.2 4.1 %copy-start.1 = (f32[64,256]{1,0:T(8,128)S(1)}, f32[64,256]{1,0:T(8,128)}, u32[]{:S(2)}) copy-start(f32[64,256]{1,0:T(8,128)} %rain.3) | copy-start | bytes 196612
  17.7 4.8 %collective-permute-start.4 = (f32[104,128]{1,0:T(8,128)S(1)}, f32[104,128]{1,0:T(8,128)S(1)}, u32[]{:S(2)}, u32[]{:S(2)}) collective-permute-start(f32[104,128]{1,0:T(8,128)S(1)} %get-tuple-element.69), channel_id=1, source_target_pairs={{16,32},{32,16},{48,64},{64,48},{80,96},{96,80},{112,0},{0,112},{1... | collective-permute-start | bytes 159752 | tf_op jit(solution)/shard_map/ppermute | solution.py:975
  18.8 3.7 %collective-permute-start.5 = (f32[104,128]{1,0:T(8,128)S(1)}, f32[104,128]{1,0:T(8,128)S(1)}, u32[]{:S(2)}, u32[]{:S(2)}) collective-permute-start(f32[104,128]{1,0:T(8,128)S(1)} %get-tuple-element.70), channel_id=1, source_target_pairs={{0,16},{16,0},{32,48},{48,32},{64,80},{80,64},{96,112},{112,96},{1... | collective-permute-start | bytes 159752 | tf_op jit(solution)/shard_map/ppermute | solution.py:975
  22.6 7.4 %collective-permute-start.6 = (f32[80,128]{1,0:T(8,128)S(1)}, f32[80,128]{1,0:T(8,128)S(1)}, u32[]{:S(2)}, u32[]{:S(2)}) collective-permute-start(f32[80,128]{1,0:T(8,128)S(1)} %get-tuple-element.79), channel_id=1, source_target_pairs={{1,2},{2,1},{3,4},{4,3},{5,6},{6,5},{7,8},{8,7},{9,10},{10,9},{11,... | collective-permute-start | bytes 122888 | tf_op jit(solution)/shard_map/ppermute | solution.py:975
  24.1 5.9 %collective-permute-start.7 = (f32[80,128]{1,0:T(8,128)S(1)}, f32[80,128]{1,0:T(8,128)S(1)}, u32[]{:S(2)}, u32[]{:S(2)}) collective-permute-start(f32[80,128]{1,0:T(8,128)S(1)} %get-tuple-element.80), channel_id=1, source_target_pairs={{0,1},{1,0},{2,3},{3,2},{4,5},{5,4},{6,7},{7,6},{8,9},{9,8},{10,11... | collective-permute-start | bytes 122888 | tf_op jit(solution)/shard_map/ppermute | solution.py:975

commit v6 on v5

--- a/solution.py
+++ b/solution.py
@@ -209,8 +209,8 @@
 
 
 UNROLL_IN = 4
-UNROLL_FWD = 20
-UNROLL_BACK = 20
+UNROLL_FWD = 40
+UNROLL_BACK = 40
 UNROLL_MOM = 5
 UNROLL_OUT = 40
 

time: 32.1 us -> 32.3 us (level)
    pallas_call x1, Pallas kernels: 3.37 us -> 3.7 us  [middle(): pl.pallas_call(middle_kernel, out_shape=(shape(LEVELS, ROWS - 16, COLS),...]
  transfers between devices with their start and end apart: 8 -> 8, of which waited for: 2 -> 1; matrix products, arithmetic and copies ran while one was open for 0% -> 0% of each run, Pallas kernels for 32% -> 33%
where the time goes in v6:
time: 32.3 us; the launch traced here: 32.1 us
  Pallas kernels  16.9 us (52%)
  starting transfers between devices  12.1 us (37%)
  waiting for transfers between devices  2.38 us (7%)
  between operations  0.76 us (2%)
    ppermute x8, starting transfers between devices, swap(): return lax.ppermute(array, axis, pairs)  12.1 us
    pallas_call x1, Pallas kernels, interior(): pl.pallas_call(interior_kernel, out_shape=(block,) * 3, in_specs=[VMEM] *...  4.06 us
    pallas_call x1, Pallas kernels, middle(): pl.pallas_call(middle_kernel, out_shape=(shape(LEVELS, ROWS - 16, COLS),...  3.7 us
    pallas_call x1, Pallas kernels, pack(): pl.pallas_call(pack_kernel, out_shape=(shape(LEVELS, ROWS, COLS), shape(R...  2.99 us
    pallas_call x1, Pallas kernels, writer(): pl.pallas_call(writer_kernel, out_shape=(shape(LEVELS, ROWS, COLS), shape...  2.83 us
    ppermute x8, waiting for transfers between devices, swap(): return lax.ppermute(array, axis, pairs)  2.38 us
    pallas_call x1, Pallas kernels, final(): pl.pallas_call(final_kernel, out_shape=(shape(2, LEVELS, ROWS, COLS), sha...  1.96 us
    pallas_call x1, Pallas kernels, outer(): pl.pallas_call(outer_kernel, out_shape=(shape(LEVELS, 16, COLS),) + (shap...  1.21 us
  transfers between devices with their start and end apart: 8, of which 1 were waited for; matrix products, arithmetic and copies ran while one was open for 0% of the time, Pallas kernels for 33%

profile of v6, /device:TPU:0, one launch (start us, length us, event | category | flops | bytes accessed | tf_op | source)
XLA Modules:
  0.0 32.1 jit_solution(17629539605306843435)
XLA Ops:
  0.6 0.0 copy-start
  0.6 0.0 copy-start.2
  0.7 3.0 %pack.1 = (f32[40,64,256]{2,1,0:T(8,128)S(1)}, f32[64,256]{1,0:T(8,128)S(1)}, f32[2,88,128]{2,1,0:T(8,128)S(1)}, f32[2,88,128]{2,1,0:T(8,128)S(1)}, f32[64,128]{...) custom-call(f32[40,64,256]{2,1,0:T(8,128)} %temp.1, ...), custom_call_target="tpu_custom_call" | custom-call | tf_op jit(solution)/shard_map/pack/pallas_call | solution.py:189
  3.7 6.7 %collective-permute-start = (f32[64,128]{1,0:T(8,128)S(1)}, f32[64,128]{1,0:T(8,128)S(1)}, u32[]{:S(2)}, u32[]{:S(2)}) collective-permute-start(f32[64,128]{1,0:T(8,128)S(1)} %get-tuple-element.52), channel_id=1, source_target_pairs={{1,2},{2,1},{3,4},{4,3},{5,6},{6,5},{7,8},{8,7},{9,10},{10,9},{11,... | collective-permute-start | bytes 98312 | tf_op jit(solution)/shard_map/ppermute | solution.py:975
  10.3 0.0 collective-permute-start.1
  10.3 1.9 %collective-permute-start.2 = (f32[2,88,128]{2,1,0:T(8,128)S(1)}, f32[2,88,128]{2,1,0:T(8,128)S(1)}, u32[]{:S(2)}, u32[]{:S(2)}) collective-permute-start(f32[2,88,128]{2,1,0:T(8,128)S(1)} %get-tuple-element.54), channel_id=1, source_target_pairs={{16,32},{32,16},{48,64},{64,48},{80,96},{96,80},{112,0},{0,112},{1... | collective-permute-start | bytes 270344 | tf_op jit(solution)/shard_map/ppermute | solution.py:975
  12.2 0.0 collective-permute-start.3
  12.2 0.0 copy-done
  12.2 0.0 copy-done.2
  12.2 0.0 copy-start.1
  12.2 4.1 %interior.1 = (f32[40,64,256]{2,1,0:T(8,128)S(1)}, f32[40,64,256]{2,1,0:T(8,128)S(1)}, f32[40,64,256]{2,1,0:T(8,128)S(1)}) custom-call(f32[40,64,256]{2,1,0:T(8,128)S(1)} %get-tuple-element.43.tb, f32[2,40,64,256]{3,2,1,0:T(8,128)S(1)} %copy-done, f32[40,64,256]{2,1,0:T(8,128)S(1)} %copy-done.2, f32[64,256]{1,0:T(8,128)S(1)} %get-tuple-element.44.count), custom_call_target="tpu_custom_call" | custom-call | flops 6553600000 | bytes 6553600000 | tf_op jit(solution)/shard_map/interior/pallas_call | solution.py:300
  16.3 0.0 collective-permute-done.y_odd_in
  16.3 0.0 collective-permute-done.1.y_even_in
  16.3 0.0 collective-permute-done.2.x_odd_in
  16.3 0.0 collective-permute-done.3.x_even_in
  16.4 0.0 copy-done.1
  16.4 1.2 %outer.1 = (f32[40,16,256]{2,1,0:T(8,128)S(1)}, f32[104,128]{1,0:T(8,128)S(1)}, f32[104,128]{1,0:T(8,128)S(1)}, f32[104,128]{1,0:T(8,128)S(1)}, f32[104,128]{1,0...) custom-call(f32[40,64,256]{2,1,0:T(8,128)S(1)} %get-tuple-element.45, ...), custom_call_target="tpu_custom_call" | custom-call | tf_op jit(solution)/shard_map/outer/pallas_call | solution.py:626
  17.6 1.1 %collective-permute-start.4 = (f32[104,128]{1,0:T(8,128)S(1)}, f32[104,128]{1,0:T(8,128)S(1)}, u32[]{:S(2)}, u32[]{:S(2)}) collective-permute-start(f32[104,128]{1,0:T(8,128)S(1)} %get-tuple-element.69), channel_id=1, source_target_pairs={{16,32},{32,16},{48,64},{64,48},{80,96},{96,80},{112,0},{0,112},{1... | collective-permute-start | bytes 159752 | tf_op jit(solution)/shard_map/ppermute | solution.py:975
  18.7 0.2 collective-permute-start.5
  18.9 3.7 %middle.1 = (f32[40,48,256]{2,1,0:T(8,128)S(1)}, f32[40,64,256]{2,1,0:T(8,128)S(1)}, f32[40,64,128]{2,1,0:T(8,128)S(1)}, f32[40,64,128]{2,1,0:T(8,128)S(1)}, f32...) custom-call(f32[40,64,256]{2,1,0:T(8,128)S(1)} %get-tuple-element.45.source, ...), custom_call_target="tpu_custom_call" | custom-call | flops 19660800 | bytes 10485760 | tf_op jit(solution)/shard_map/middle/pallas_call | solution.py:699
  22.6 0.0 collective-permute-done.4.x_odd
  22.7 0.0 collective-permute-done.5.x_even
  22.7 0.1 edges.1
  22.8 1.6 %collective-permute-start.6 = (f32[80,128]{1,0:T(8,128)S(1)}, f32[80,128]{1,0:T(8,128)S(1)}, u32[]{:S(2)}, u32[]{:S(2)}) collective-permute-start(f32[80,128]{1,0:T(8,128)S(1)} %get-tuple-element.79), channel_id=1, source_target_pairs={{1,2},{2,1},{3,4},{4,3},{5,6},{6,5},{7,8},{8,7},{9,10},{10,9},{11,... | collective-permute-start | bytes 122888 | tf_op jit(solution)/shard_map/ppermute | solution.py:975
  24.4 0.6 %collective-permute-start.7 = (f32[80,128]{1,0:T(8,128)S(1)}, f32[80,128]{1,0:T(8,128)S(1)}, u32[]{:S(2)}, u32[]{:S(2)}) collective-permute-start(f32[80,128]{1,0:T(8,128)S(1)} %get-tuple-element.80), channel_id=1, source_target_pairs={{0,1},{1,0},{2,3},{3,2},{4,5},{5,4},{6,7},{7,6},{8,9},{9,8},{10,11... | collective-permute-start | bytes 122888 | tf_op jit(solution)/shard_map/ppermute | solution.py:975
  25.0 2.8 %writer.1 = (f32[40,64,256]{2,1,0:T(8,128)}, f32[2,40,64,256]{3,2,1,0:T(8,128)}, f32[64,256]{1,0:T(8,128)S(1)}) custom-call(f32[40,16,256]{2,1,0:T(8,128)S(1)} %get-tuple-element.56.outside, f32[40,48,256]{2,1,0:T(8,128)S(1)} %get-tuple-element.62.solved, f32[40,64,256]{2,1,0:T(8,128)S(1)} %get-tuple-element.63.u_new, ...), custom_call_target="tpu_custom_call" | custom-call | flops 655360 | bytes 7864320 | tf_op jit(solution)/shard_map/writer/pallas_call | solution.py:783
  27.8 2.4 %collective-permute-done.6.y_odd = f32[80,128]{1,0:T(8,128)S(1)} collective-permute-done((f32[80,128]{1,0:T(8,128)S(1)}, f32[80,128]{1,0:T(8,128)S(1)}, u32[]{:S(2)}, u32[]{:S(2)}) %collective-permute-start.6) | collective-permute-done | bytes 40992 | tf_op jit(solution)/shard_map/ppermute | solution.py:975
  30.2 0.0 collective-permute-done.7.y_even
  30.2 2.0 %final.1 = (f32[2,40,64,256]{3,2,1,0:T(8,128)}, f32[64,256]{1,0:T(8,128)}) custom-call(f32[2,40,64,256]{3,2,1,0:T(8,128)} %get-tuple-element.75.speeds, f32[40,64,128]{2,1,0:T(8,128)S(1)} %get-tuple-element.76.v_high, f32[64,256]{1,0:T(8,128)S(1)} %get-tuple-element.44.count, ...), custom_call_target="tpu_custom_call", output_to_operand_aliasing={{0}: (0, {})} | custom-call | tf_op jit(solution)/shard_map/final/pallas_call | solution.py:953
Async XLA Ops:
  0.6 11.6 %copy-start = (f32[2,40,64,256]{3,2,1,0:T(8,128)S(1)}, f32[2,40,64,256]{3,2,1,0:T(8,128)}, u32[]{:S(2)}) copy-start(f32[2,40,64,256]{3,2,1,0:T(8,128)} %speeds.7) | copy-start | bytes 15728644
  0.6 11.6 %copy-start.2 = (f32[40,64,256]{2,1,0:T(8,128)S(1)}, f32[40,64,256]{2,1,0:T(8,128)}, u32[]{:S(2)}) copy-start(f32[40,64,256]{2,1,0:T(8,128)} %mb.1) | copy-start | bytes 7864324
  3.7 12.7 %collective-permute-start = (f32[64,128]{1,0:T(8,128)S(1)}, f32[64,128]{1,0:T(8,128)S(1)}, u32[]{:S(2)}, u32[]{:S(2)}) collective-permute-start(f32[64,128]{1,0:T(8,128)S(1)} %get-tuple-element.52), channel_id=1, source_target_pairs={{1,2},{2,1},{3,4},{4,3},{5,6},{6,5},{7,8},{8,7},{9,10},{10,9},{11,... | collective-permute-start | bytes 98312 | tf_op jit(solution)/shard_map/ppermute | solution.py:975
  10.3 6.0 %collective-permute-start.1 = (f32[64,128]{1,0:T(8,128)S(1)}, f32[64,128]{1,0:T(8,128)S(1)}, u32[]{:S(2)}, u32[]{:S(2)}) collective-permute-start(f32[64,128]{1,0:T(8,128)S(1)} %get-tuple-element.53), channel_id=1, source_target_pairs={{0,1},{1,0},{2,3},{3,2},{4,5},{5,4},{6,7},{7,6},{8,9},{9,8},{10,11... | collective-permute-start | bytes 98312 | tf_op jit(solution)/shard_map/ppermute | solution.py:975
  10.3 6.0 %collective-permute-start.2 = (f32[2,88,128]{2,1,0:T(8,128)S(1)}, f32[2,88,128]{2,1,0:T(8,128)S(1)}, u32[]{:S(2)}, u32[]{:S(2)}) collective-permute-start(f32[2,88,128]{2,1,0:T(8,128)S(1)} %get-tuple-element.54), channel_id=1, source_target_pairs={{16,32},{32,16},{48,64},{64,48},{80,96},{96,80},{112,0},{0,112},{1... | collective-permute-start | bytes 270344 | tf_op jit(solution)/shard_map/ppermute | solution.py:975
  12.2 4.1 %collective-permute-start.3 = (f32[2,88,128]{2,1,0:T(8,128)S(1)}, f32[2,88,128]{2,1,0:T(8,128)S(1)}, u32[]{:S(2)}, u32[]{:S(2)}) collective-permute-start(f32[2,88,128]{2,1,0:T(8,128)S(1)} %get-tuple-element.55), channel_id=1, source_target_pairs={{0,16},{16,0},{32,48},{48,32},{64,80},{80,64},{96,112},{112,96},{1... | collective-permute-start | bytes 270344 | tf_op jit(solution)/shard_map/ppermute | solution.py:975
  12.2 4.1 %copy-start.1 = (f32[64,256]{1,0:T(8,128)S(1)}, f32[64,256]{1,0:T(8,128)}, u32[]{:S(2)}) copy-start(f32[64,256]{1,0:T(8,128)} %rain.3) | copy-start | bytes 196612
  17.6 5.1 %collective-permute-start.4 = (f32[104,128]{1,0:T(8,128)S(1)}, f32[104,128]{1,0:T(8,128)S(1)}, u32[]{:S(2)}, u32[]{:S(2)}) collective-permute-start(f32[104,128]{1,0:T(8,128)S(1)} %get-tuple-element.69), channel_id=1, source_target_pairs={{16,32},{32,16},{48,64},{64,48},{80,96},{96,80},{112,0},{0,112},{1... | collective-permute-start | bytes 159752 | tf_op jit(solution)/shard_map/ppermute | solution.py:975
  18.7 4.0 %collective-permute-start.5 = (f32[104,128]{1,0:T(8,128)S(1)}, f32[104,128]{1,0:T(8,128)S(1)}, u32[]{:S(2)}, u32[]{:S(2)}) collective-permute-start(f32[104,128]{1,0:T(8,128)S(1)} %get-tuple-element.70), channel_id=1, source_target_pairs={{0,16},{16,0},{32,48},{48,32},{64,80},{80,64},{96,112},{112,96},{1... | collective-permute-start | bytes 159752 | tf_op jit(solution)/shard_map/ppermute | solution.py:975
  22.8 7.4 %collective-permute-start.6 = (f32[80,128]{1,0:T(8,128)S(1)}, f32[80,128]{1,0:T(8,128)S(1)}, u32[]{:S(2)}, u32[]{:S(2)}) collective-permute-start(f32[80,128]{1,0:T(8,128)S(1)} %get-tuple-element.79), channel_id=1, source_target_pairs={{1,2},{2,1},{3,4},{4,3},{5,6},{6,5},{7,8},{8,7},{9,10},{10,9},{11,... | collective-permute-start | bytes 122888 | tf_op jit(solution)/shard_map/ppermute | solution.py:975
  24.4 5.8 %collective-permute-start.7 = (f32[80,128]{1,0:T(8,128)S(1)}, f32[80,128]{1,0:T(8,128)S(1)}, u32[]{:S(2)}, u32[]{:S(2)}) collective-permute-start(f32[80,128]{1,0:T(8,128)S(1)} %get-tuple-element.80), channel_id=1, source_target_pairs={{0,1},{1,0},{2,3},{3,2},{4,5},{5,4},{6,7},{7,6},{8,9},{9,8},{10,11... | collective-permute-start | bytes 122888 | tf_op jit(solution)/shard_map/ppermute | solution.py:975

commit v7 on v5

--- a/solution.py
+++ b/solution.py
@@ -211,7 +211,7 @@
 UNROLL_IN = 4
 UNROLL_FWD = 20
 UNROLL_BACK = 20
-UNROLL_MOM = 5
+UNROLL_MOM = 8
 UNROLL_OUT = 40
 
 

time: 32.1 us -> 32.1 us (level)
  no operation moved by 1% of the time
where the time goes in v7:
time: 32.1 us; the launch traced here: 32 us
  Pallas kernels  16.5 us (51%)
  starting transfers between devices  12 us (37%)
  waiting for transfers between devices  2.73 us (9%)
  between operations  0.74 us (2%)
    ppermute x8, starting transfers between devices, swap(): return lax.ppermute(array, axis, pairs)  12 us
    pallas_call x1, Pallas kernels, interior(): pl.pallas_call(interior_kernel, out_shape=(block,) * 3, in_specs=[VMEM] *...  4.06 us
    pallas_call x1, Pallas kernels, middle(): pl.pallas_call(middle_kernel, out_shape=(shape(LEVELS, ROWS - 16, COLS),...  3.3 us
    pallas_call x1, Pallas kernels, pack(): pl.pallas_call(pack_kernel, out_shape=(shape(LEVELS, ROWS, COLS), shape(R...  2.99 us
    pallas_call x1, Pallas kernels, writer(): pl.pallas_call(writer_kernel, out_shape=(shape(LEVELS, ROWS, COLS), shape...  2.83 us
    ppermute x8, waiting for transfers between devices, swap(): return lax.ppermute(array, axis, pairs)  2.73 us
    pallas_call x1, Pallas kernels, final(): pl.pallas_call(final_kernel, out_shape=(shape(2, LEVELS, ROWS, COLS), sha...  1.96 us
    pallas_call x1, Pallas kernels, outer(): pl.pallas_call(outer_kernel, out_shape=(shape(LEVELS, 16, COLS),) + (shap...  1.29 us
  transfers between devices with their start and end apart: 8, of which 2 were waited for; matrix products, arithmetic and copies ran while one was open for 0% of the time, Pallas kernels for 32%

profile of v7, /device:TPU:0, one launch (start us, length us, event | category | flops | bytes accessed | tf_op | source)
XLA Modules:
  0.0 32.0 jit_solution(7479201838863241103)
XLA Ops:
  0.6 0.0 copy-start
  0.6 0.0 copy-start.2
  0.7 3.0 %pack.1 = (f32[40,64,256]{2,1,0:T(8,128)S(1)}, f32[64,256]{1,0:T(8,128)S(1)}, f32[2,88,128]{2,1,0:T(8,128)S(1)}, f32[2,88,128]{2,1,0:T(8,128)S(1)}, f32[64,128]{...) custom-call(f32[40,64,256]{2,1,0:T(8,128)} %temp.1, ...), custom_call_target="tpu_custom_call" | custom-call | tf_op jit(solution)/shard_map/pack/pallas_call | solution.py:189
  3.7 6.7 %collective-permute-start = (f32[64,128]{1,0:T(8,128)S(1)}, f32[64,128]{1,0:T(8,128)S(1)}, u32[]{:S(2)}, u32[]{:S(2)}) collective-permute-start(f32[64,128]{1,0:T(8,128)S(1)} %get-tuple-element.52), channel_id=1, source_target_pairs={{1,2},{2,1},{3,4},{4,3},{5,6},{6,5},{7,8},{8,7},{9,10},{10,9},{11,... | collective-permute-start | bytes 98312 | tf_op jit(solution)/shard_map/ppermute | solution.py:975
  10.3 0.0 collective-permute-start.1
  10.3 1.9 %collective-permute-start.2 = (f32[2,88,128]{2,1,0:T(8,128)S(1)}, f32[2,88,128]{2,1,0:T(8,128)S(1)}, u32[]{:S(2)}, u32[]{:S(2)}) collective-permute-start(f32[2,88,128]{2,1,0:T(8,128)S(1)} %get-tuple-element.54), channel_id=1, source_target_pairs={{16,32},{32,16},{48,64},{64,48},{80,96},{96,80},{112,0},{0,112},{1... | collective-permute-start | bytes 270344 | tf_op jit(solution)/shard_map/ppermute | solution.py:975
  12.2 0.0 collective-permute-start.3
  12.2 0.0 copy-done
  12.2 0.0 copy-done.2
  12.2 0.0 copy-start.1
  12.2 4.1 %interior.1 = (f32[40,64,256]{2,1,0:T(8,128)S(1)}, f32[40,64,256]{2,1,0:T(8,128)S(1)}, f32[40,64,256]{2,1,0:T(8,128)S(1)}) custom-call(f32[40,64,256]{2,1,0:T(8,128)S(1)} %get-tuple-element.43.tb, f32[2,40,64,256]{3,2,1,0:T(8,128)S(1)} %copy-done, f32[40,64,256]{2,1,0:T(8,128)S(1)} %copy-done.2, f32[64,256]{1,0:T(8,128)S(1)} %get-tuple-element.44.count), custom_call_target="tpu_custom_call" | custom-call | flops 6553600000 | bytes 6553600000 | tf_op jit(solution)/shard_map/interior/pallas_call | solution.py:300
  16.3 0.0 collective-permute-done.y_odd_in
  16.3 0.0 collective-permute-done.1.y_even_in
  16.3 0.0 collective-permute-done.2.x_odd_in
  16.3 0.0 collective-permute-done.3.x_even_in
  16.4 0.0 copy-done.1
  16.4 1.3 %outer.1 = (f32[40,16,256]{2,1,0:T(8,128)S(1)}, f32[104,128]{1,0:T(8,128)S(1)}, f32[104,128]{1,0:T(8,128)S(1)}, f32[104,128]{1,0:T(8,128)S(1)}, f32[104,128]{1,0...) custom-call(f32[40,64,256]{2,1,0:T(8,128)S(1)} %get-tuple-element.45, ...), custom_call_target="tpu_custom_call" | custom-call | tf_op jit(solution)/shard_map/outer/pallas_call | solution.py:626
  17.7 1.1 %collective-permute-start.4 = (f32[104,128]{1,0:T(8,128)S(1)}, f32[104,128]{1,0:T(8,128)S(1)}, u32[]{:S(2)}, u32[]{:S(2)}) collective-permute-start(f32[104,128]{1,0:T(8,128)S(1)} %get-tuple-element.69), channel_id=1, source_target_pairs={{16,32},{32,16},{48,64},{64,48},{80,96},{96,80},{112,0},{0,112},{1... | collective-permute-start | bytes 159752 | tf_op jit(solution)/shard_map/ppermute | solution.py:975
  18.8 0.2 collective-permute-start.5
  19.0 3.3 %middle.1 = (f32[40,48,256]{2,1,0:T(8,128)S(1)}, f32[40,64,256]{2,1,0:T(8,128)S(1)}, f32[40,64,128]{2,1,0:T(8,128)S(1)}, f32[40,64,128]{2,1,0:T(8,128)S(1)}, f32...) custom-call(f32[40,64,256]{2,1,0:T(8,128)S(1)} %get-tuple-element.45.source, ...), custom_call_target="tpu_custom_call" | custom-call | flops 19660800 | bytes 10485760 | tf_op jit(solution)/shard_map/middle/pallas_call | solution.py:699
  22.3 0.2 collective-permute-done.4.x_odd
  22.5 0.0 collective-permute-done.5.x_even
  22.5 0.1 edges.1
  22.6 1.4 %collective-permute-start.6 = (f32[80,128]{1,0:T(8,128)S(1)}, f32[80,128]{1,0:T(8,128)S(1)}, u32[]{:S(2)}, u32[]{:S(2)}) collective-permute-start(f32[80,128]{1,0:T(8,128)S(1)} %get-tuple-element.79), channel_id=1, source_target_pairs={{1,2},{2,1},{3,4},{4,3},{5,6},{6,5},{7,8},{8,7},{9,10},{10,9},{11,... | collective-permute-start | bytes 122888 | tf_op jit(solution)/shard_map/ppermute | solution.py:975
  24.1 0.6 %collective-permute-start.7 = (f32[80,128]{1,0:T(8,128)S(1)}, f32[80,128]{1,0:T(8,128)S(1)}, u32[]{:S(2)}, u32[]{:S(2)}) collective-permute-start(f32[80,128]{1,0:T(8,128)S(1)} %get-tuple-element.80), channel_id=1, source_target_pairs={{0,1},{1,0},{2,3},{3,2},{4,5},{5,4},{6,7},{7,6},{8,9},{9,8},{10,11... | collective-permute-start | bytes 122888 | tf_op jit(solution)/shard_map/ppermute | solution.py:975
  24.7 2.8 %writer.1 = (f32[40,64,256]{2,1,0:T(8,128)}, f32[2,40,64,256]{3,2,1,0:T(8,128)}, f32[64,256]{1,0:T(8,128)S(1)}) custom-call(f32[40,16,256]{2,1,0:T(8,128)S(1)} %get-tuple-element.56.outside, f32[40,48,256]{2,1,0:T(8,128)S(1)} %get-tuple-element.62.solved, f32[40,64,256]{2,1,0:T(8,128)S(1)} %get-tuple-element.63.u_new, ...), custom_call_target="tpu_custom_call" | custom-call | flops 655360 | bytes 7864320 | tf_op jit(solution)/shard_map/writer/pallas_call | solution.py:783
  27.5 2.5 %collective-permute-done.6.y_odd = f32[80,128]{1,0:T(8,128)S(1)} collective-permute-done((f32[80,128]{1,0:T(8,128)S(1)}, f32[80,128]{1,0:T(8,128)S(1)}, u32[]{:S(2)}, u32[]{:S(2)}) %collective-permute-start.6) | collective-permute-done | bytes 40992 | tf_op jit(solution)/shard_map/ppermute | solution.py:975
  30.0 0.0 collective-permute-done.7.y_even
  30.0 2.0 %final.1 = (f32[2,40,64,256]{3,2,1,0:T(8,128)}, f32[64,256]{1,0:T(8,128)}) custom-call(f32[2,40,64,256]{3,2,1,0:T(8,128)} %get-tuple-element.75.speeds, f32[40,64,128]{2,1,0:T(8,128)S(1)} %get-tuple-element.76.v_high, f32[64,256]{1,0:T(8,128)S(1)} %get-tuple-element.44.count, ...), custom_call_target="tpu_custom_call", output_to_operand_aliasing={{0}: (0, {})} | custom-call | tf_op jit(solution)/shard_map/final/pallas_call | solution.py:953
Async XLA Ops:
  0.6 11.6 %copy-start = (f32[2,40,64,256]{3,2,1,0:T(8,128)S(1)}, f32[2,40,64,256]{3,2,1,0:T(8,128)}, u32[]{:S(2)}) copy-start(f32[2,40,64,256]{3,2,1,0:T(8,128)} %speeds.7) | copy-start | bytes 15728644
  0.6 11.6 %copy-start.2 = (f32[40,64,256]{2,1,0:T(8,128)S(1)}, f32[40,64,256]{2,1,0:T(8,128)}, u32[]{:S(2)}) copy-start(f32[40,64,256]{2,1,0:T(8,128)} %mb.1) | copy-start | bytes 7864324
  3.7 12.7 %collective-permute-start = (f32[64,128]{1,0:T(8,128)S(1)}, f32[64,128]{1,0:T(8,128)S(1)}, u32[]{:S(2)}, u32[]{:S(2)}) collective-permute-start(f32[64,128]{1,0:T(8,128)S(1)} %get-tuple-element.52), channel_id=1, source_target_pairs={{1,2},{2,1},{3,4},{4,3},{5,6},{6,5},{7,8},{8,7},{9,10},{10,9},{11,... | collective-permute-start | bytes 98312 | tf_op jit(solution)/shard_map/ppermute | solution.py:975
  10.3 6.0 %collective-permute-start.1 = (f32[64,128]{1,0:T(8,128)S(1)}, f32[64,128]{1,0:T(8,128)S(1)}, u32[]{:S(2)}, u32[]{:S(2)}) collective-permute-start(f32[64,128]{1,0:T(8,128)S(1)} %get-tuple-element.53), channel_id=1, source_target_pairs={{0,1},{1,0},{2,3},{3,2},{4,5},{5,4},{6,7},{7,6},{8,9},{9,8},{10,11... | collective-permute-start | bytes 98312 | tf_op jit(solution)/shard_map/ppermute | solution.py:975
  10.3 6.0 %collective-permute-start.2 = (f32[2,88,128]{2,1,0:T(8,128)S(1)}, f32[2,88,128]{2,1,0:T(8,128)S(1)}, u32[]{:S(2)}, u32[]{:S(2)}) collective-permute-start(f32[2,88,128]{2,1,0:T(8,128)S(1)} %get-tuple-element.54), channel_id=1, source_target_pairs={{16,32},{32,16},{48,64},{64,48},{80,96},{96,80},{112,0},{0,112},{1... | collective-permute-start | bytes 270344 | tf_op jit(solution)/shard_map/ppermute | solution.py:975
  12.2 4.1 %collective-permute-start.3 = (f32[2,88,128]{2,1,0:T(8,128)S(1)}, f32[2,88,128]{2,1,0:T(8,128)S(1)}, u32[]{:S(2)}, u32[]{:S(2)}) collective-permute-start(f32[2,88,128]{2,1,0:T(8,128)S(1)} %get-tuple-element.55), channel_id=1, source_target_pairs={{0,16},{16,0},{32,48},{48,32},{64,80},{80,64},{96,112},{112,96},{1... | collective-permute-start | bytes 270344 | tf_op jit(solution)/shard_map/ppermute | solution.py:975
  12.2 4.1 %copy-start.1 = (f32[64,256]{1,0:T(8,128)S(1)}, f32[64,256]{1,0:T(8,128)}, u32[]{:S(2)}) copy-start(f32[64,256]{1,0:T(8,128)} %rain.3) | copy-start | bytes 196612
  17.7 4.8 %collective-permute-start.4 = (f32[104,128]{1,0:T(8,128)S(1)}, f32[104,128]{1,0:T(8,128)S(1)}, u32[]{:S(2)}, u32[]{:S(2)}) collective-permute-start(f32[104,128]{1,0:T(8,128)S(1)} %get-tuple-element.69), channel_id=1, source_target_pairs={{16,32},{32,16},{48,64},{64,48},{80,96},{96,80},{112,0},{0,112},{1... | collective-permute-start | bytes 159752 | tf_op jit(solution)/shard_map/ppermute | solution.py:975
  18.8 3.7 %collective-permute-start.5 = (f32[104,128]{1,0:T(8,128)S(1)}, f32[104,128]{1,0:T(8,128)S(1)}, u32[]{:S(2)}, u32[]{:S(2)}) collective-permute-start(f32[104,128]{1,0:T(8,128)S(1)} %get-tuple-element.70), channel_id=1, source_target_pairs={{0,16},{16,0},{32,48},{48,32},{64,80},{80,64},{96,112},{112,96},{1... | collective-permute-start | bytes 159752 | tf_op jit(solution)/shard_map/ppermute | solution.py:975
  22.6 7.4 %collective-permute-start.6 = (f32[80,128]{1,0:T(8,128)S(1)}, f32[80,128]{1,0:T(8,128)S(1)}, u32[]{:S(2)}, u32[]{:S(2)}) collective-permute-start(f32[80,128]{1,0:T(8,128)S(1)} %get-tuple-element.79), channel_id=1, source_target_pairs={{1,2},{2,1},{3,4},{4,3},{5,6},{6,5},{7,8},{8,7},{9,10},{10,9},{11,... | collective-permute-start | bytes 122888 | tf_op jit(solution)/shard_map/ppermute | solution.py:975
  24.1 6.0 %collective-permute-start.7 = (f32[80,128]{1,0:T(8,128)S(1)}, f32[80,128]{1,0:T(8,128)S(1)}, u32[]{:S(2)}, u32[]{:S(2)}) collective-permute-start(f32[80,128]{1,0:T(8,128)S(1)} %get-tuple-element.80), channel_id=1, source_target_pairs={{0,1},{1,0},{2,3},{3,2},{4,5},{5,4},{6,7},{7,6},{8,9},{9,8},{10,11... | collective-permute-start | bytes 122888 | tf_op jit(solution)/shard_map/ppermute | solution.py:975
